TPU v7x, 32 devices: a whole 2x2x4 slice. The times are simulated.
32 devices in a mesh: crops: 2 (over y), row: 4 (over z), col: 2 (over x), seq: 2 (over core).
Axes of the slice: x: 2, y: 2, z: 4, core: 2. Of those that a mesh axis runs over, the one named last changes fastest.
Arguments:
- homolog_embedding: bfloat16 [512, 64, 256], P(('crops', 'seq'), ('col', 'row')), parts along dimension 0, may hold values from -6 to 6
- homolog_cell_occupancy: int32 [512, 64], P(('crops', 'seq'), ('col', 'row')), parts along dimension 0, may hold values from 0 to 1, as said below
- peptide_occupancy: int32 [128], P(('crops', 'col', 'row')), parts along dimension 0, may hold values from 0 to 1
- standardize_multiplier: float32 [256], replicated, may hold values from 0.5 to 1.5
- standardize_addend: float32 [256], replicated, may hold values from -3 to 3
- lhs_linear_map: bfloat16 [256, 32], replicated, may hold values from -0.375 to 0.375
- lhs_linear_constant: float32 [32], replicated, may hold values from -3 to 3
- rhs_linear_map: bfloat16 [256, 32], replicated, may hold values from -0.375 to 0.375
- rhs_linear_constant: float32 [32], replicated, may hold values from -3 to 3
- closing_linear_map: bfloat16 [1024, 128], replicated, may hold values from -0.375 to 0.375
- closing_linear_constant: float32 [128], replicated, may hold values from -40 to 40
Outputs:
- pair_update: bfloat16 [128, 64, 128], P(('crops', 'row'), ('col', 'seq')), parts along dimension 0
There are 2 independent parts, one for each index of `crops`. A program takes and returns all parts, laid end to end along the dimension named above; an argument that names none is the same for every part. Nothing has to cross between parts.
Inputs may be any that keep to these rules, and one draw needn't show every extreme that they name: `homolog_cell_occupancy`: sequence 0 is present at every residue.
All inputs are finite; a program needn't handle non-finite values.
Results may differ from a plain program's by a relative error of at most 0.003.
Values may be sent and summed in bfloat16 or wider, within the bound.
No kernel may reach another device: no remote copies, remote signals or barrier semaphores. Data moves between devices by JAX's collectives and lax.ppermute only.
A program may use at most 128 MiB of HBM per device.

v0:
```python
import math

import jax
import jax.numpy as jnp
from jax import lax
from jax.sharding import PartitionSpec as P


def from_root(x, axis, root):
    mine = lax.axis_index(axis) == root
    return lax.psum(jnp.where(mine, x, jnp.zeros_like(x)), axis)


def project_side(normed, occupied_indicator, weight, bias):
    seq_count, res_count, width = normed.shape
    report_text = jnp.dot(
        normed.reshape(seq_count * res_count, width), weight, preferred_element_type=jnp.float32
    )
    report_text = (report_text + bias).reshape(seq_count, res_count, -1) * occupied_indicator[
        :, :, None
    ]
    return report_text.astype(jnp.bfloat16)


def pair_rows(left, right, closing_linear_map):
    row_count = left.shape[1]
    col_count = right.shape[1]
    block_rows = math.gcd(row_count, max(1, 512 // col_count))
    weight_f32 = closing_linear_map.astype(jnp.float32)

    def project_block(first_row):
        left_block = lax.dynamic_slice_in_dim(left, first_row, block_rows, 1)
        outer_prod = jnp.einsum(
            "sic,sjd->ijcd", left_block, right, preferred_element_type=jnp.float32
        )
        flattened = outer_prod.reshape(block_rows * col_count, -1)
        result = jnp.dot(flattened, weight_f32, precision=lax.Precision.HIGHEST)
        return result.reshape(block_rows, col_count, -1)

    starts = jnp.arange(row_count // block_rows) * block_rows
    return lax.map(project_block, starts).reshape(row_count, col_count, -1)


def shards(
    homolog_embedding,
    homolog_cell_occupancy,
    peptide_occupancy,
    standardize_multiplier,
    standardize_addend,
    lhs_linear_map,
    lhs_linear_constant,
    rhs_linear_map,
    rhs_linear_constant,
    closing_linear_map,
    closing_linear_constant,
):
    occupied_indicator = (homolog_cell_occupancy * peptide_occupancy[None, :]).astype(jnp.float32)
    report_text = homolog_embedding.astype(jnp.float32)
    average = jnp.mean(report_text, axis=-1, keepdims=True)
    spread = jnp.mean(jnp.square(report_text - average), axis=-1, keepdims=True)
    normed = (
        (report_text - average) * lax.rsqrt(spread + 1e-05) * standardize_multiplier
        + standardize_addend
    ).astype(jnp.bfloat16)
    left = project_side(normed, occupied_indicator, lhs_linear_map, lhs_linear_constant)
    right = project_side(normed, occupied_indicator, rhs_linear_map, rhs_linear_constant)
    mask_bf = occupied_indicator.astype(jnp.bfloat16)
    left_col, right_col, mask_col = (
        lax.all_gather(left, "row", axis=1, tiled=True),
        lax.all_gather(right, "row", axis=1, tiled=True),
        lax.all_gather(mask_bf, "row", axis=1, tiled=True),
    )
    row_devices = lax.axis_size("row")
    col_devices = lax.axis_size("col")
    col_len = left_col.shape[1]
    row_len = col_len * col_devices // row_devices
    row_index = lax.axis_index("row")
    root_col = row_index * col_devices // row_devices
    offset = row_index * row_len % col_len
    whole_left, whole_mask = (
        from_root(left_col, "col", root_col),
        from_root(mask_col, "col", root_col),
    )
    left_row = lax.dynamic_slice_in_dim(whole_left, offset, row_len, 1)
    mask_row = lax.dynamic_slice_in_dim(whole_mask, offset, row_len, 1)
    partial_value = pair_rows(left_row, right_col, closing_linear_map)
    mask_rows_all, mask_cols_all = (
        lax.all_gather(mask_row, "seq", axis=0, tiled=True),
        lax.all_gather(mask_col, "seq", axis=0, tiled=True),
    )
    counts_full = jnp.dot(mask_rows_all.T, mask_cols_all, preferred_element_type=jnp.float32)
    summed = lax.psum_scatter(
        partial_value.astype(jnp.bfloat16), "seq", scatter_dimension=1, tiled=True
    ).astype(jnp.float32)
    seq_devices = lax.axis_size("seq")
    part_cols = col_len // seq_devices
    counts = lax.dynamic_slice_in_dim(counts_full, lax.axis_index("seq") * part_cols, part_cols, 1)
    return ((summed + closing_linear_constant) / jnp.maximum(counts, 1.0)[:, :, None]).astype(
        jnp.bfloat16
    )


def solution(mesh):
    return jax.shard_map(
        shards,
        mesh=mesh,
        in_specs=(
            P(("crops", "seq"), ("col", "row"), None),
            P(("crops", "seq"), ("col", "row")),
            P(("crops", "col", "row")),
            P(),
            P(),
            P(),
            P(),
            P(),
            P(),
            P(),
            P(),
        ),
        out_specs=P(("crops", "row"), ("col", "seq"), None),
        check_vma=False,
    )
```

profile of v0, /device:TPU:1, one launch (start us, length us, event | category | flops | bytes accessed | tf_op | source)
XLA Modules:
  0.0 102.5 jit_solution(3513772024568678872)
XLA Ops:
  6.5 0.0 copy-start
  6.5 0.0 all-reduce.2.cloned.1.call-start
  6.5 0.0 copy-start.1
  6.5 0.0 copy-start.5
  6.5 0.0 copy-start.6
  6.6 0.0 copy-start.7
  6.6 0.0 copy-start.8
  6.6 1.3 %convert_reduce_fusion = f32[128,8]{1,0:T(8,128)S(1)} fusion(bf16[128,8,256]{2,1,0:T(8,128)(2,1)} %param.11), kind=kLoop, calls=%fused_computation.2 | loop fusion | flops 523264 | bytes 528384 | tf_op jit(solution)/shard_map/reduce_sum | solution.py:59
  7.9 1.4 %fusion.2 = f32[128,8]{1,0:T(8,128)S(1)} fusion(bf16[128,8,256]{2,1,0:T(8,128)(2,1)} %param.11, f32[128,8]{1,0:T(8,128)S(1)} %broadcast_multiply_fusion), kind=kLoop, calls=%fused_computation.8 | loop fusion | flops 1047552 | bytes 532480 | tf_op jit(solution)/shard_map/reduce_sum | solution.py:60
  9.4 1.5 %convolution_add_fusion.1 = f32[1024,32]{0,1:T(8,128)S(1)} fusion(bf16[256,32]{0,1:T(8,128)(2,1)} %param.18, bf16[128,8,256]{2,1,0:T(8,128)(2,1)} %param.11, f32[256]{0:T(256)} %param.15, f32[256]{0:T(256)} %param.14, f32[128,8]{1,0:T(8,128)S(1)} %add_rsqrt_fusion, f32[128,8]{1,0:T(8,128)S(1)} %broadcast_multiply_fusion, f32[32]{0:T(128)} %param.19), kind=kOutput, calls=%fused_computation.7 | convolution fusion | flops 18382848 | bytes 682112 | tf_op jit(solution)/shard_map/dot_general | solution.py:16
  10.9 0.0 copy-start.2
  10.9 0.0 copy-start.4
  10.9 0.2 copy.19
  11.1 0.0 copy-done.1
  11.1 0.0 copy-done.5
  11.2 0.0 copy-done.6
  11.2 0.0 copy-done.7
  11.2 0.0 copy-done.8
  11.2 0.5 convolution_add_fusion
  11.7 0.2 copy.22
  11.9 0.0 copy-done.2
  11.9 0.0 copy-done.4
  11.9 0.1 fusion.16
  12.0 0.1 copy.20
  12.1 0.2 fusion.7
  12.3 0.2 copy.23
  12.5 13.3 %all_gather.16 = bf16[128,32,32]{0,2,1:T(8,128)(2,1)S(1)} all-gather(bf16[128,8,32]{0,2,1:T(8,128)(2,1)S(1)} %copy.23), channel_id=1, replica_groups=mesh['crops'=2,'row'=4,'col'=2,'seq'=2] {'row'}, dimensions={1}, use_global_device_ids=true | all-gather | bytes 327680 | tf_op jit(solution)/shard_map/all_gather | solution.py:69
  25.8 0.7 broadcast_select_fusion
  26.5 0.0 all-reduce.2.cloned.1.call-update
  26.5 0.0 reduce-scatter.2.cloned.1.call-start
  26.5 9.3 %all_gather.17 = bf16[128,32]{0,1:T(8,128)(2,1)S(1)} all-gather(bf16[128,8]{0,1:T(8,128)(2,1)S(1)} %get-tuple-element.13), channel_id=1, replica_groups=mesh['crops'=2,'row'=4,'col'=2,'seq'=2] {'row'}, dimensions={1}, use_global_device_ids=true | all-gather | bytes 10240 | tf_op jit(solution)/shard_map/all_gather | solution.py:71
  35.8 0.2 copy.21
  36.0 4.3 %psum.15 = bf16[128,32]{0,1:T(8,128)(2,1)S(1)} all-reduce(bf16[128,32]{0,1:T(8,128)(2,1)S(1)} %broadcast_select_fusion.1), channel_id=1, replica_groups=mesh['crops'=2,'row'=4,'col'=2,'seq'=2] {'col'}, use_global_device_ids=true, to_apply=%region_4.5 | all-reduce | flops 4096 | bytes 16384 | tf_op jit(solution)/shard_map/psum | solution.py:11
  40.4 7.2 %all_gather.18 = bf16[256,16]{0,1:T(8,128)(2,1)S(1)} all-gather(bf16[128,16]{0,1:T(8,128)(2,1)S(1)} %constant_dynamic-slice_fusion), channel_id=1, replica_groups=mesh['crops'=2,'row'=4,'col'=2,'seq'=2] {'seq'}, dimensions={0}, use_global_device_ids=true | all-gather | bytes 12288 | tf_op jit(solution)/shard_map/all_gather | solution.py:88
  47.6 1.8 %all_gather.19 = bf16[256,32]{0,1:T(8,128)(2,1)S(1)} all-gather(bf16[128,32]{0,1:T(8,128)(2,1)S(1)} %all_gather.17), channel_id=1, replica_groups=mesh['crops'=2,'row'=4,'col'=2,'seq'=2] {'seq'}, dimensions={0}, use_global_device_ids=true | all-gather | bytes 24576 | tf_op jit(solution)/shard_map/all_gather | solution.py:89
  49.4 11.2 %all_gather.15 = bf16[128,32,32]{0,2,1:T(8,128)(2,1)S(1)} all-gather(bf16[128,8,32]{0,2,1:T(8,128)(2,1)S(1)} %copy.21), channel_id=1, replica_groups=mesh['crops'=2,'row'=4,'col'=2,'seq'=2] {'row'}, dimensions={1}, use_global_device_ids=true | all-gather | bytes 327680 | tf_op jit(solution)/shard_map/all_gather | solution.py:70
  60.6 5.4 %convolution_bitcast_fusion = f32[16,32,32,32]{2,3,0,1:T(8,128)} fusion(bf16[128,32,32]{0,2,1:T(8,128)(2,1)S(1)} %all_gather.15, bf16[128,32,32]{0,2,1:T(8,128)(2,1)} %all-reduce.2.cloned.1.call-done, s32[]{:T(128)S(6)} %select_n.40), kind=kOutput, calls=%fused_computation | convolution fusion | flops 134217728 | bytes 2490372 | tf_op jit(solution)/shard_map/while/body/eval_jaxpr/sic,sjd->ijcd/dot_general | solution.py:33
  66.0 8.9 %copy.24 = f32[16,32,32,32]{3,2,1,0:T(8,128)} copy(f32[16,32,32,32]{2,3,0,1:T(8,128)} %convolution_bitcast_fusion) | data formatting | bytes 4194304 | tf_op jit(solution)/shard_map/while/body/eval_jaxpr/sic,sjd->ijcd/transpose | solution.py:33
  75.0 6.6 %dot_general.22 = f32[16,32,1024]{2,1,0:T(8,128)S(1)} reshape(f32[16,32,32,32]{3,2,1,0:T(8,128)} %copy.24) | data formatting | bytes 4194304 | tf_op jit(solution)/shard_map/while/body/eval_jaxpr/dot_general | solution.py:37
  81.6 0.0 copy-done
  81.6 0.0 copy-start.3
  81.6 1.7 %convolution_convert_fusion = bf16[16,32,128]{2,1,0:T(8,128)(2,1)} fusion(f32[16,32,1024]{2,1,0:T(8,128)S(1)} %dot_general.22, bf16[1024,128]{1,0:T(8,128)(2,1)S(1)} %copy-done), kind=kOutput, calls=%fused_computation.5 | convolution fusion | flops 805371904 | bytes 2490368 | tf_op jit(solution)/shard_map/while/body/eval_jaxpr/dot_general | solution.py:37
  83.3 0.0 reduce-scatter.2.cloned.1.call-update
  83.4 0.1 fusion.17
  83.5 0.1 dynamic-slice_maximum_fusion
  83.5 10.6 %reduce-scatter.2.cloned.1.call-done = bf16[16,16,128]{2,1,0:T(8,128)(2,1)} async-done(((bf16[16,32,128]{2,1,0:T(8,128)(2,1)}), bf16[16,16,128]{2,1,0:T(8,128)(2,1)}) %reduce-scatter.2.cloned.1.call-update) | async-done | bytes 65552 | tf_op jit(solution)/shard_map/reduce_scatter | solution.py:92
  94.1 0.0 copy-done.3
  94.1 1.6 %divide_convert_fusion = bf16[16,16,128]{2,1,0:T(8,128)(2,1)} fusion(bf16[16,16,128]{2,1,0:T(8,128)(2,1)} %reduce-scatter.2.cloned.1.call-done, f32[16,16]{1,0:T(8,128)S(1)} %dynamic-slice_maximum_fusion, f32[128]{0:T(128)S(1)} %copy-done.3), kind=kLoop, calls=%fused_computation.21 | loop fusion | flops 131072 | bytes 132608 | tf_op jit(solution)/shard_map/convert_element_type | solution.py:98
  (5 shorter events, 0.0 us)
Async XLA Ops:
  6.5 75.1 %copy-start = (bf16[1024,128]{1,0:T(8,128)(2,1)S(1)}, bf16[1024,128]{1,0:T(8,128)(2,1)}, u32[]{:S(2)}) copy-start(bf16[1024,128]{1,0:T(8,128)(2,1)} %param.20) | copy-start | bytes 786436
  6.5 54.1 %all-reduce.2.cloned.1.call-start = ((), (), s32[]{:S(2)}) async-start(), calls=%async_computation.1 | async-start | bytes 524288 | tf_op jit(solution)/shard_map/psum | solution.py:11
  6.5 4.6 %copy-start.1 = (bf16[128,8,256]{2,1,0:T(8,128)(2,1)S(1)}, bf16[128,8,256]{2,1,0:T(8,128)(2,1)}, u32[]{:S(2)}) copy-start(bf16[128,8,256]{2,1,0:T(8,128)(2,1)} %param.11) | copy-start | bytes 1572868
  6.5 4.6 %copy-start.5 = (bf16[256,32]{0,1:T(8,128)(2,1)S(1)}, bf16[256,32]{0,1:T(8,128)(2,1)}, u32[]{:S(2)}) copy-start(bf16[256,32]{0,1:T(8,128)(2,1)} %param.16) | copy-start | bytes 49156
  6.5 4.6 %copy-start.6 = (f32[256]{0:T(256)S(1)}, f32[256]{0:T(256)}, u32[]{:S(2)}) copy-start(f32[256]{0:T(256)} %param.15) | copy-start | bytes 3076
  6.6 4.6 %copy-start.7 = (f32[256]{0:T(256)S(1)}, f32[256]{0:T(256)}, u32[]{:S(2)}) copy-start(f32[256]{0:T(256)} %param.14) | copy-start | bytes 3076
  6.6 4.6 %copy-start.8 = (f32[32]{0:T(128)S(1)}, f32[32]{0:T(128)}, u32[]{:S(2)}) copy-start(f32[32]{0:T(128)} %param.17) | copy-start | bytes 388
  10.9 1.0 copy-start.2
  10.9 0.9 copy-start.4
  26.5 67.6 %reduce-scatter.2.cloned.1.call-start = ((), (), s32[]{:S(2)}) async-start(), calls=%async_computation.2 | async-start | bytes 196608 | tf_op jit(solution)/shard_map/reduce_scatter | solution.py:92
  81.6 12.5 %copy-start.3 = (f32[128]{0:T(128)S(1)}, f32[128]{0:T(128)}, u32[]{:S(2)}) copy-start(f32[128]{0:T(128)} %param.21) | copy-start | bytes 1540
Sparse Core Ops, SparseCore 0:
  26.6 26.0 all-reduce.1
  83.5 10.5 reduce-scatter.1
where the time goes:
time: 103 us
  blocking collectives  47.2 us (46%)
  local copies, waits for them, and re-layouts  16.5 us (16%)
  between operations  13.6 us (13%)
  waiting for transfers between devices  10.6 us (10%)
  matrix products  9.23 us (9%)
  other arithmetic  5.39 us (5%)
    all_gather x1, blocking collectives, shards(): lax.all_gather(left, 'row', axis=1, tiled=True)  13.3 us
    all_gather x1, blocking collectives, shards(): lax.all_gather(right, 'row', axis=1, tiled=True)  11.2 us
    reduce_scatter x1, waiting for transfers between devices, shards(): lax.psum_scatter(partial_value.astype(jnp.bfloat16), 'seq', scatter_dimen...  10.6 us
    all_gather x1, blocking collectives, shards(): lax.all_gather(mask_bf, 'row', axis=1, tiled=True)  9.28 us
    transpose x1, local copies, waits for them, and re-layouts, project_block(): jnp.einsum('sic,sjd->ijcd', left_block, right, preferred_element_type=jnp...  8.95 us
    all_gather x1, blocking collectives, shards(): lax.all_gather(mask_row, 'seq', axis=0, tiled=True)  7.19 us
    dot_general x1, local copies, waits for them, and re-layouts, project_block(): result = jnp.dot(flattened, weight_f32, precision=lax.Precision.HIGHEST)  6.63 us
    dot_general x1, matrix products, project_block(): jnp.einsum('sic,sjd->ijcd', left_block, right, preferred_element_type=jnp...  5.39 us
  transfers between devices with their start and end apart: 2, of which 1 were waited for; matrix products, arithmetic and copies ran while one was open for 0% of the time, Pallas kernels for 0%

commit v1 on v0

--- a/solution.py
+++ b/solution.py
@@ -3,7 +3,13 @@
 import jax
 import jax.numpy as jnp
 from jax import lax
+from jax.experimental import pallas as pl
+from jax.experimental.pallas import tpu as pltpu
 from jax.sharding import PartitionSpec as P
+
+GROUP = ("row", "col", "seq")
+NT = (((1,), (1,)), ((), ()))
+MASK_ROWS = 16
 
 
 def from_root(x, axis, root):
@@ -41,7 +47,7 @@
     return lax.map(project_block, starts).reshape(row_count, col_count, -1)
 
 
-def shards(
+def general_shards(
     homolog_embedding,
     homolog_cell_occupancy,
     peptide_occupancy,
@@ -100,6 +106,185 @@
     )
 
 
+def project_kernel(
+    pept_ref, x_ref, occ_ref, gain_ref, shift_ref, wl_ref, bl_ref, wr_ref, br_ref,
+    left_ref, right_ref, y_ref, l_ref,
+):
+    residues, sequences = occ_ref.shape
+    hidden = wl_ref.shape[0]
+    x = x_ref[...].astype(jnp.float32)
+    average = jnp.mean(x, axis=-1, keepdims=True)
+    centred = x - average
+    spread = jnp.mean(jnp.square(centred), axis=-1, keepdims=True)
+    normed = (centred * lax.rsqrt(spread + 1e-05) * gain_ref[...] + shift_ref[...]).astype(
+        jnp.bfloat16
+    )
+    weight = jnp.concatenate([wl_ref[...], wr_ref[...]], axis=0)
+    bias = jnp.concatenate([bl_ref[...], br_ref[...]], axis=1)
+    y = lax.dot_general(normed, weight, NT, preferred_element_type=jnp.float32) + bias
+    y_ref[:, : 2 * hidden] = y
+    for i in range(residues):
+        live = (occ_ref[i : i + 1, :] * pept_ref[i]).astype(jnp.float32)
+        part = y_ref[pl.ds(i, sequences, stride=residues), :].T[: 2 * hidden] * live
+        l_ref[pl.ds(i, hidden, stride=residues), :] = part[:hidden]
+        right_ref[i * hidden : (i + 1) * hidden, :] = part[hidden:].astype(jnp.bfloat16)
+        l_ref[hidden * residues + i : hidden * residues + i + 1, :] = live
+    l_ref[hidden * residues + residues :, :] = jnp.zeros((MASK_ROWS - residues, sequences), jnp.float32)
+    left_ref[...] = l_ref[...].astype(jnp.bfloat16)
+    right_ref[hidden * residues :, :] = l_ref[hidden * residues :, :].astype(jnp.bfloat16)
+
+
+def pair_kernel(
+    l0, l1, l2, l3, r0, r1, r2, r3, w_ref, b_ref, out_ref, ls_ref, rs_ref, big_ref, p_ref
+):
+    hidden = 32
+    body = l0.shape[0] - MASK_ROWS
+    residues = body // hidden
+    width = w_ref.shape[1]
+    row, col, seq = (lax.axis_index(name) for name in GROUP)
+    for k, (left, right) in enumerate(((l0, r0), (l1, r1), (l2, r2), (l3, r3))):
+        ls_ref[seq ^ (k % 2), col ^ (k // 2)] = left[...]
+        rs_ref[(row % 2) ^ (k % 2), (row // 2) ^ (k // 2)] = right[...]
+
+    def rows(ref, first, last):
+        return jnp.concatenate(
+            [
+                jnp.concatenate([ref[h, p, first:last, :] for p in range(2)], axis=0)
+                for h in range(2)
+            ],
+            axis=1,
+        )
+
+    left = rows(ls_ref, 0, body)
+    right = rows(rs_ref, 0, body)
+    outer = lax.dot_general(left, right, NT, preferred_element_type=jnp.float32)
+    live_i = rows(ls_ref, body, body + MASK_ROWS)
+    live_j = rows(rs_ref, body, body + MASK_ROWS)
+    counts = lax.dot_general(live_i, live_j, NT, preferred_element_type=jnp.float32)
+    spread_shape = (2 * MASK_ROWS, 2 * body)
+    at_row = lax.broadcasted_iota(jnp.int32, spread_shape, 0)
+    at_lane = lax.broadcasted_iota(jnp.int32, spread_shape, 1)
+    hit = ((at_row // MASK_ROWS) * residues + at_row % MASK_ROWS == at_lane // hidden) & (
+        at_row % MASK_ROWS < residues
+    )
+    counts = jnp.dot(
+        counts.astype(jnp.bfloat16), hit.astype(jnp.bfloat16), preferred_element_type=jnp.float32
+    )
+    per_vector = 128 // hidden
+    lane = lax.broadcasted_iota(jnp.int32, (2 * residues, 128), 1) // hidden
+    masks = [(lane == a).astype(jnp.bfloat16) for a in range(per_vector)]
+
+    def put(slot, low, high):
+        both = jnp.concatenate([low, high], axis=0).astype(jnp.bfloat16)
+        for g in range(2 * residues // per_vector):
+            tile = both[:, g * 128 : (g + 1) * 128]
+            for a in range(per_vector):
+                first = (g * per_vector + a) * 2 * residues
+                big_ref[first : first + 2 * residues, slot * 128 : (slot + 1) * 128] = tile * masks[a]
+
+    for c in range(hidden):
+        put(c, outer[c * residues : (c + 1) * residues], outer[body + c * residues : body + (c + 1) * residues])
+    put(hidden, counts[:residues], counts[MASK_ROWS : MASK_ROWS + residues])
+    weight = jnp.concatenate(
+        [w_ref[c * hidden : (c + 1) * hidden, :] for c in range(hidden) for _ in range(per_vector)],
+        axis=0,
+    )
+    projected = jnp.dot(
+        big_ref[:, : hidden * 128], weight, preferred_element_type=jnp.float32
+    )
+    share = jnp.full((128, width), 1.0 / hidden, jnp.bfloat16)
+    divisor = jnp.dot(big_ref[:, hidden * 128 :], share, preferred_element_type=jnp.float32)
+    p_ref[...] = (projected + b_ref[...]) / jnp.maximum(divisor, 1.0)
+    for i in range(2 * residues):
+        out_ref[i] = p_ref[pl.ds(i, 2 * residues, stride=2 * residues), :].astype(jnp.bfloat16)
+
+
+def left_route(k):
+    route = []
+    for r in range(4):
+        for c in range(2):
+            for q in range(2):
+                to = (2 * c + r // 2, (r % 2) ^ (k // 2), q ^ (k % 2))
+                route.append((4 * r + 2 * c + q, 4 * to[0] + 2 * to[1] + to[2]))
+    return route
+
+
+def right_route(k):
+    route = []
+    for r in range(4):
+        for c in range(2):
+            for q in range(2):
+                to = (2 * ((r % 2) ^ (k // 2)) + (q ^ (k % 2)), c, r // 2)
+                route.append((4 * r + 2 * c + q, 4 * to[0] + 2 * to[1] + to[2]))
+    return route
+
+
+def direct_shards(
+    homolog_embedding,
+    homolog_cell_occupancy,
+    peptide_occupancy,
+    standardize_multiplier,
+    standardize_addend,
+    lhs_linear_map,
+    lhs_linear_constant,
+    rhs_linear_map,
+    rhs_linear_constant,
+    closing_linear_map,
+    closing_linear_constant,
+):
+    sequences, residues, signal = homolog_embedding.shape
+    hidden = lhs_linear_map.shape[1]
+    width = closing_linear_map.shape[1]
+    rows = residues * hidden + MASK_ROWS
+    payload = jax.ShapeDtypeStruct((rows, sequences), jnp.bfloat16)
+    vmem = pl.BlockSpec(memory_space=pltpu.VMEM)
+    left, right = pl.pallas_call(
+        project_kernel,
+        out_shape=(payload, payload),
+        in_specs=[pl.BlockSpec(memory_space=pltpu.SMEM)] + [vmem] * 8,
+        out_specs=(vmem, vmem),
+        scratch_shapes=[
+            pltpu.VMEM((sequences * residues, 128), jnp.float32),
+            pltpu.VMEM((rows, sequences), jnp.float32),
+        ],
+        compiler_params=pltpu.CompilerParams(vmem_limit_bytes=24 * 1024 * 1024),
+        name="normalize_and_project",
+    )(
+        peptide_occupancy,
+        homolog_embedding.reshape(sequences * residues, signal),
+        homolog_cell_occupancy.T,
+        standardize_multiplier.reshape(1, signal),
+        standardize_addend.reshape(1, signal),
+        lhs_linear_map.T,
+        lhs_linear_constant.reshape(1, hidden),
+        rhs_linear_map.T,
+        rhs_linear_constant.reshape(1, hidden),
+    )
+    lefts = [lax.ppermute(left, GROUP, left_route(k)) for k in range(4)]
+    rights = [lax.ppermute(right, GROUP, right_route(k)) for k in range(4)]
+    return pl.pallas_call(
+        pair_kernel,
+        out_shape=jax.ShapeDtypeStruct((2 * residues, 2 * residues, width), jnp.bfloat16),
+        in_specs=[vmem] * 10,
+        out_specs=vmem,
+        scratch_shapes=[
+            pltpu.VMEM((2, 2, rows, sequences), jnp.bfloat16),
+            pltpu.VMEM((2, 2, rows, sequences), jnp.bfloat16),
+            pltpu.VMEM((4 * residues * residues, (hidden + 1) * 128), jnp.bfloat16),
+            pltpu.VMEM((4 * residues * residues, width), jnp.float32),
+        ],
+        compiler_params=pltpu.CompilerParams(vmem_limit_bytes=32 * 1024 * 1024),
+        name="pair_update",
+    )(*lefts, *rights, closing_linear_map, closing_linear_constant.reshape(1, width))
+
+
+def shards(*arrays):
+    sizes = tuple(lax.axis_size(name) for name in GROUP)
+    if sizes == (4, 2, 2) and arrays[0].shape[:2] == (128, 8):
+        return direct_shards(*arrays)
+    return general_shards(*arrays)
+
+
 def solution(mesh):
     return jax.shard_map(
         shards,

time: 103 us -> 30.2 us (0.29)
  blocking collectives: 47.2 us -> 0 us
  starting transfers between devices: 0.04 us -> 21.9 us
  between operations: 13.6 us -> 0.11 us
  local copies, waits for them, and re-layouts: 16.5 us -> 3.2 us
  waiting for transfers between devices: 10.6 us -> 1.33 us
  matrix products: 9.23 us -> 0 us
  other arithmetic: 5.39 us -> 0 us
  Pallas kernels: 0 us -> 3.26 us
    all_gather x5 -> x0, blocking collectives: 42.8 us -> none  [the longest x1 13.3 us: shards(): lax.all_gather(left, 'row', axis=1, tiled=True)]
    ppermute x0 -> x8, starting transfers between devices: none -> 21.9 us  [the longest x4 16.2 us: direct_shards(): rights = [lax.ppermute(right, GROUP, right_route(k)) for k in range(4)]]
    reduce_scatter x1 -> x0, waiting for transfers between devices: 10.6 us -> none  [shards(): lax.psum_scatter(partial_value.astype(jnp.bfloat16), 'seq', scatter_dimen...]
    dot_general x5 -> x0, matrix products: 9.23 us -> none  [the longest x1 5.39 us: project_block(): jnp.einsum('sic,sjd->ijcd', left_block, right, preferred_element_type=jnp...]
    transpose x1 -> x0, local copies, waits for them, and re-layouts: 8.95 us -> none  [project_block(): jnp.einsum('sic,sjd->ijcd', left_block, right, preferred_element_type=jnp...]
    dot_general x1 -> x0, local copies, waits for them, and re-layouts: 6.63 us -> none  [project_block(): result = jnp.dot(flattened, weight_f32, precision=lax.Precision.HIGHEST)]
    psum x1 -> x0, blocking collectives: 4.35 us -> none  [from_root(): return lax.psum(jnp.where(mine, x, jnp.zeros_like(x)), axis)]
    pallas_call x0 -> x2, Pallas kernels: none -> 3.26 us  [the longest x1 1.96 us: direct_shards(): pl.pallas_call(pair_kernel, out_shape=jax.ShapeDtypeStruct((2 * residues,...]
  transfers between devices with their start and end apart: 2 -> 8, of which waited for: 1 -> 2; matrix products, arithmetic and copies ran while one was open for 0% -> 0% of each run, Pallas kernels for 0% -> 0%
where the time goes in v1:
time: 30.2 us; the launch traced here: 29.8 us
  starting transfers between devices  21.9 us (73%)
  Pallas kernels  3.26 us (11%)
  local copies, waits for them, and re-layouts  3.2 us (11%)
  waiting for transfers between devices  1.33 us (4%)
    ppermute x4, starting transfers between devices, direct_shards(): rights = [lax.ppermute(right, GROUP, right_route(k)) for k in range(4)]  16.2 us
    ppermute x4, starting transfers between devices, direct_shards(): lefts = [lax.ppermute(left, GROUP, left_route(k)) for k in range(4)]  5.73 us
    unnamed x22, local copies, waits for them, and re-layouts  3.2 us
    pallas_call x1, Pallas kernels, direct_shards(): pl.pallas_call(pair_kernel, out_shape=jax.ShapeDtypeStruct((2 * residues,...  1.96 us
    ppermute x4, waiting for transfers between devices, direct_shards(): rights = [lax.ppermute(right, GROUP, right_route(k)) for k in range(4)]  1.32 us
    pallas_call x1, Pallas kernels, direct_shards(): pl.pallas_call(project_kernel, out_shape=(payload, payload), in_specs=[pl...  1.31 us
  transfers between devices with their start and end apart: 8, of which 2 were waited for; matrix products, arithmetic and copies ran while one was open for 0% of the time, Pallas kernels for 0%

profile of v1, /device:TPU:1, one launch (start us, length us, event | category | flops | bytes accessed | tf_op | source)
XLA Modules:
  0.0 29.8 jit_solution(12634659686108515403)
XLA Ops:
  0.0 0.0 copy-start.4
  0.0 0.0 copy-start.6
  0.0 0.0 copy-start.8
  0.0 0.0 copy-start.9
  0.0 0.0 copy-start.5
  0.0 0.0 copy-start.7
  0.0 0.6 %copy-done.4 = s32[128,8]{0,1:T(8,128)S(1)} copy-done((s32[128,8]{0,1:T(8,128)S(1)}, s32[128,8]{0,1:T(8,128)}, u32[]{:S(2)}) %copy-start.4) | copy-done | bytes 4120
  0.7 0.0 copy-done.6
  0.7 0.0 copy-done.8
  0.7 0.0 copy-done.9
  0.7 0.0 copy-done.5
  0.7 0.0 copy-done.7
  0.7 0.0 copy-start
  0.7 1.0 %copy-done = bf16[128,8,256]{2,1,0:T(8,128)(2,1)S(1)} copy-done((bf16[128,8,256]{2,1,0:T(8,128)(2,1)S(1)}, bf16[128,8,256]{2,1,0:T(8,128)(2,1)}, u32[]{:S(2)}) %copy-start) | copy-done | bytes 524312
  1.8 0.0 copy-start.2
  1.8 0.7 %copy-done.2 = bf16[256,32]{0,1:T(8,128)(2,1)S(1)} copy-done((bf16[256,32]{0,1:T(8,128)(2,1)S(1)}, bf16[256,32]{0,1:T(8,128)(2,1)}, u32[]{:S(2)}) %copy-start.2) | copy-done | bytes 16408
  2.5 0.0 copy-start.3
  2.5 0.7 %copy-done.3 = bf16[256,32]{0,1:T(8,128)(2,1)S(1)} copy-done((bf16[256,32]{0,1:T(8,128)(2,1)S(1)}, bf16[256,32]{0,1:T(8,128)(2,1)}, u32[]{:S(2)}) %copy-start.3) | copy-done | bytes 16408
  3.2 0.0 copy-start.1
  3.2 1.3 %normalize_and_project.1 = (bf16[272,128]{1,0:T(8,128)(2,1)S(1)}, bf16[272,128]{1,0:T(8,128)(2,1)S(1)}) custom-call(s32[8]{0:T(128)S(1)} %copy-done.7, bf16[1024,256]{1,0:T(8,128)(2,1)S(1)} %bitcast.9, s32[8,128]{1,0:T(8,128)S(1)} %bitcast.12, f32[1,256]{1,0:T(1,128)S(1)} %bitcast.13, f32[1,256]{1,0:T(1,128)S(1)} %bitcast.14, bf16[32,256]{1,0:T(8,128)(2,1)S(1)} %bitcast.10, ...), custom_call_target="tpu_custom_call" | custom-call | tf_op jit(solution)/shard_map/normalize_and_project/pallas_call | solution.py:241
  4.5 2.7 %collective-permute-start.3 = (bf16[272,128]{1,0:T(8,128)(2,1)S(1)}, bf16[272,128]{1,0:T(8,128)(2,1)S(1)}, u32[]{:S(2)}, u32[]{:S(2)}) collective-permute-start(bf16[272,128]{1,0:T(8,128)(2,1)S(1)} %get-tuple-element.7), channel_id=1, source_target_pairs={{0,3},{1,2},{2,11},{3,10},{4,1},{5,0},{6,9},{7,8},{8,7},{9,6},{10,... | collective-permute-start | bytes 208904 | tf_op jit(solution)/shard_map/ppermute | solution.py:263
  7.2 2.3 %collective-permute-start.2 = (bf16[272,128]{1,0:T(8,128)(2,1)S(1)}, bf16[272,128]{1,0:T(8,128)(2,1)S(1)}, u32[]{:S(2)}, u32[]{:S(2)}) collective-permute-start(bf16[272,128]{1,0:T(8,128)(2,1)S(1)} %get-tuple-element.7), channel_id=1, source_target_pairs={{0,2},{1,3},{2,10},{3,11},{4,0},{5,1},{6,8},{7,9},{8,6},{9,7},{10,... | collective-permute-start | bytes 208904 | tf_op jit(solution)/shard_map/ppermute | solution.py:263
  9.5 0.1 collective-permute-start.1
  9.6 0.7 %collective-permute-start = (bf16[272,128]{1,0:T(8,128)(2,1)S(1)}, bf16[272,128]{1,0:T(8,128)(2,1)S(1)}, u32[]{:S(2)}, u32[]{:S(2)}) collective-permute-start(bf16[272,128]{1,0:T(8,128)(2,1)S(1)} %get-tuple-element.7), channel_id=1, source_target_pairs={{0,0},{1,1},{2,8},{3,9},{4,2},{5,3},{6,10},{7,11},{8,4},{9,5},{10,... | collective-permute-start | bytes 208904 | tf_op jit(solution)/shard_map/ppermute | solution.py:263
  10.3 0.0 copy-start.10
  10.3 7.3 %collective-permute-start.7 = (bf16[272,128]{1,0:T(8,128)(2,1)S(1)}, bf16[272,128]{1,0:T(8,128)(2,1)S(1)}, u32[]{:S(2)}, u32[]{:S(2)}) collective-permute-start(bf16[272,128]{1,0:T(8,128)(2,1)S(1)} %get-tuple-element.8), channel_id=1, source_target_pairs={{0,12},{1,8},{2,14},{3,10},{4,4},{5,0},{6,6},{7,2},{8,13},{9,9},{1... | collective-permute-start | bytes 208904 | tf_op jit(solution)/shard_map/ppermute | solution.py:264
  17.6 0.0 collective-permute-done.3.l3
  17.6 1.7 %collective-permute-start.6 = (bf16[272,128]{1,0:T(8,128)(2,1)S(1)}, bf16[272,128]{1,0:T(8,128)(2,1)S(1)}, u32[]{:S(2)}, u32[]{:S(2)}) collective-permute-start(bf16[272,128]{1,0:T(8,128)(2,1)S(1)} %get-tuple-element.8), channel_id=1, source_target_pairs={{0,8},{1,12},{2,10},{3,14},{4,0},{5,4},{6,2},{7,6},{8,9},{9,13},{1... | collective-permute-start | bytes 208904 | tf_op jit(solution)/shard_map/ppermute | solution.py:264
  19.3 0.0 collective-permute-done.2.l2
  19.3 0.7 %collective-permute-start.5 = (bf16[272,128]{1,0:T(8,128)(2,1)S(1)}, bf16[272,128]{1,0:T(8,128)(2,1)S(1)}, u32[]{:S(2)}, u32[]{:S(2)}) collective-permute-start(bf16[272,128]{1,0:T(8,128)(2,1)S(1)} %get-tuple-element.8), channel_id=1, source_target_pairs={{0,4},{1,0},{2,6},{3,2},{4,12},{5,8},{6,14},{7,10},{8,5},{9,1},{10... | collective-permute-start | bytes 208904 | tf_op jit(solution)/shard_map/ppermute | solution.py:264
  20.0 0.0 collective-permute-done.1.l1
  20.0 6.5 %collective-permute-start.4 = (bf16[272,128]{1,0:T(8,128)(2,1)S(1)}, bf16[272,128]{1,0:T(8,128)(2,1)S(1)}, u32[]{:S(2)}, u32[]{:S(2)}) collective-permute-start(bf16[272,128]{1,0:T(8,128)(2,1)S(1)} %get-tuple-element.8), channel_id=1, source_target_pairs={{0,0},{1,4},{2,2},{3,6},{4,8},{5,12},{6,10},{7,14},{8,1},{9,5},{10... | collective-permute-start | bytes 208904 | tf_op jit(solution)/shard_map/ppermute | solution.py:264
  26.5 0.0 collective-permute-done.l0
  26.5 0.0 collective-permute-done.7.r3
  26.5 0.0 collective-permute-done.6.r2
  26.5 0.2 collective-permute-done.5.r1
  26.7 1.1 %collective-permute-done.4.r0 = bf16[272,128]{1,0:T(8,128)(2,1)S(1)} collective-permute-done((bf16[272,128]{1,0:T(8,128)(2,1)S(1)}, bf16[272,128]{1,0:T(8,128)(2,1)S(1)}, u32[]{:S(2)}, u32[]{:S(2)}) %collective-permute-start.4) | collective-permute-done | bytes 69664 | tf_op jit(solution)/shard_map/ppermute | solution.py:264
  27.9 0.0 copy-done.1
  27.9 0.0 copy-done.10
  27.9 2.0 %pair_update.1 = bf16[16,16,128]{2,1,0:T(8,128)(2,1)} custom-call(bf16[272,128]{1,0:T(8,128)(2,1)S(1)} %collective-permute-done.l0, bf16[272,128]{1,0:T(8,128)(2,1)S(1)} %collective-permute-done.1.l1, bf16[272,128]{1,0:T(8,128)(2,1)S(1)} %collective-permute-done.2.l2, bf16[272,128]{1,0:T(8,128)(2,1)S(1)} %collective-permute-done.3.l3, ...), custom_call_target="tpu_custom_call" | custom-call | tf_op jit(solution)/shard_map/pair_update/pallas_call | solution.py:265
Async XLA Ops:
  0.0 0.7 %copy-start.4 = (s32[128,8]{0,1:T(8,128)S(1)}, s32[128,8]{0,1:T(8,128)}, u32[]{:S(2)}) copy-start(s32[128,8]{0,1:T(8,128)} %param.12) | copy-start | bytes 12292
  0.0 0.7 %copy-start.6 = (f32[256]{0:T(256)S(1)}, f32[256]{0:T(256)}, u32[]{:S(2)}) copy-start(f32[256]{0:T(256)} %param.15) | copy-start | bytes 3076
  0.0 0.7 %copy-start.8 = (f32[32]{0:T(128)S(1)}, f32[32]{0:T(128)}, u32[]{:S(2)}) copy-start(f32[32]{0:T(128)} %param.17) | copy-start | bytes 388
  0.0 0.7 %copy-start.9 = (f32[32]{0:T(128)S(1)}, f32[32]{0:T(128)}, u32[]{:S(2)}) copy-start(f32[32]{0:T(128)} %param.19) | copy-start | bytes 388
  0.0 0.7 %copy-start.5 = (f32[256]{0:T(256)S(1)}, f32[256]{0:T(256)}, u32[]{:S(2)}) copy-start(f32[256]{0:T(256)} %param.14) | copy-start | bytes 3076
  0.0 0.7 %copy-start.7 = (s32[8]{0:T(128)S(1)}, s32[8]{0:T(128)}, u32[]{:S(2)}) copy-start(s32[8]{0:T(128)} %pept_ref.1) | copy-start | bytes 100
  0.7 1.0 %copy-start = (bf16[128,8,256]{2,1,0:T(8,128)(2,1)S(1)}, bf16[128,8,256]{2,1,0:T(8,128)(2,1)}, u32[]{:S(2)}) copy-start(bf16[128,8,256]{2,1,0:T(8,128)(2,1)} %param.11) | copy-start | bytes 1572868
  1.8 0.7 %copy-start.2 = (bf16[256,32]{0,1:T(8,128)(2,1)S(1)}, bf16[256,32]{0,1:T(8,128)(2,1)}, u32[]{:S(2)}) copy-start(bf16[256,32]{0,1:T(8,128)(2,1)} %param.16) | copy-start | bytes 49156
  2.5 0.7 %copy-start.3 = (bf16[256,32]{0,1:T(8,128)(2,1)S(1)}, bf16[256,32]{0,1:T(8,128)(2,1)}, u32[]{:S(2)}) copy-start(bf16[256,32]{0,1:T(8,128)(2,1)} %param.18) | copy-start | bytes 49156
  3.2 24.6 %copy-start.1 = (bf16[1024,128]{1,0:T(8,128)(2,1)S(1)}, bf16[1024,128]{1,0:T(8,128)(2,1)}, u32[]{:S(2)}) copy-start(bf16[1024,128]{1,0:T(8,128)(2,1)} %w_ref.1) | copy-start | bytes 786436
  4.5 13.1 %collective-permute-start.3 = (bf16[272,128]{1,0:T(8,128)(2,1)S(1)}, bf16[272,128]{1,0:T(8,128)(2,1)S(1)}, u32[]{:S(2)}, u32[]{:S(2)}) collective-permute-start(bf16[272,128]{1,0:T(8,128)(2,1)S(1)} %get-tuple-element.7), channel_id=1, source_target_pairs={{0,3},{1,2},{2,11},{3,10},{4,1},{5,0},{6,9},{7,8},{8,7},{9,6},{10,... | collective-permute-start | bytes 208904 | tf_op jit(solution)/shard_map/ppermute | solution.py:263
  7.2 12.1 %collective-permute-start.2 = (bf16[272,128]{1,0:T(8,128)(2,1)S(1)}, bf16[272,128]{1,0:T(8,128)(2,1)S(1)}, u32[]{:S(2)}, u32[]{:S(2)}) collective-permute-start(bf16[272,128]{1,0:T(8,128)(2,1)S(1)} %get-tuple-element.7), channel_id=1, source_target_pairs={{0,2},{1,3},{2,10},{3,11},{4,0},{5,1},{6,8},{7,9},{8,6},{9,7},{10,... | collective-permute-start | bytes 208904 | tf_op jit(solution)/shard_map/ppermute | solution.py:263
  9.5 10.5 %collective-permute-start.1 = (bf16[272,128]{1,0:T(8,128)(2,1)S(1)}, bf16[272,128]{1,0:T(8,128)(2,1)S(1)}, u32[]{:S(2)}, u32[]{:S(2)}) collective-permute-start(bf16[272,128]{1,0:T(8,128)(2,1)S(1)} %get-tuple-element.7), channel_id=1, source_target_pairs={{0,1},{1,0},{2,9},{3,8},{4,3},{5,2},{6,11},{7,10},{8,5},{9,4},{10,... | collective-permute-start | bytes 208904 | tf_op jit(solution)/shard_map/ppermute | solution.py:263
  9.6 16.9 %collective-permute-start = (bf16[272,128]{1,0:T(8,128)(2,1)S(1)}, bf16[272,128]{1,0:T(8,128)(2,1)S(1)}, u32[]{:S(2)}, u32[]{:S(2)}) collective-permute-start(bf16[272,128]{1,0:T(8,128)(2,1)S(1)} %get-tuple-element.7), channel_id=1, source_target_pairs={{0,0},{1,1},{2,8},{3,9},{4,2},{5,3},{6,10},{7,11},{8,4},{9,5},{10,... | collective-permute-start | bytes 208904 | tf_op jit(solution)/shard_map/ppermute | solution.py:263
  10.3 17.6 %copy-start.10 = (f32[128]{0:T(128)S(1)}, f32[128]{0:T(128)}, u32[]{:S(2)}) copy-start(f32[128]{0:T(128)} %param.21) | copy-start | bytes 1540
  10.3 16.2 %collective-permute-start.7 = (bf16[272,128]{1,0:T(8,128)(2,1)S(1)}, bf16[272,128]{1,0:T(8,128)(2,1)S(1)}, u32[]{:S(2)}, u32[]{:S(2)}) collective-permute-start(bf16[272,128]{1,0:T(8,128)(2,1)S(1)} %get-tuple-element.8), channel_id=1, source_target_pairs={{0,12},{1,8},{2,14},{3,10},{4,4},{5,0},{6,6},{7,2},{8,13},{9,9},{1... | collective-permute-start | bytes 208904 | tf_op jit(solution)/shard_map/ppermute | solution.py:264
  17.6 8.9 %collective-permute-start.6 = (bf16[272,128]{1,0:T(8,128)(2,1)S(1)}, bf16[272,128]{1,0:T(8,128)(2,1)S(1)}, u32[]{:S(2)}, u32[]{:S(2)}) collective-permute-start(bf16[272,128]{1,0:T(8,128)(2,1)S(1)} %get-tuple-element.8), channel_id=1, source_target_pairs={{0,8},{1,12},{2,10},{3,14},{4,0},{5,4},{6,2},{7,6},{8,9},{9,13},{1... | collective-permute-start | bytes 208904 | tf_op jit(solution)/shard_map/ppermute | solution.py:264
  19.3 7.4 %collective-permute-start.5 = (bf16[272,128]{1,0:T(8,128)(2,1)S(1)}, bf16[272,128]{1,0:T(8,128)(2,1)S(1)}, u32[]{:S(2)}, u32[]{:S(2)}) collective-permute-start(bf16[272,128]{1,0:T(8,128)(2,1)S(1)} %get-tuple-element.8), channel_id=1, source_target_pairs={{0,4},{1,0},{2,6},{3,2},{4,12},{5,8},{6,14},{7,10},{8,5},{9,1},{10... | collective-permute-start | bytes 208904 | tf_op jit(solution)/shard_map/ppermute | solution.py:264
  20.0 7.8 %collective-permute-start.4 = (bf16[272,128]{1,0:T(8,128)(2,1)S(1)}, bf16[272,128]{1,0:T(8,128)(2,1)S(1)}, u32[]{:S(2)}, u32[]{:S(2)}) collective-permute-start(bf16[272,128]{1,0:T(8,128)(2,1)S(1)} %get-tuple-element.8), channel_id=1, source_target_pairs={{0,0},{1,4},{2,2},{3,6},{4,8},{5,12},{6,10},{7,14},{8,1},{9,5},{10... | collective-permute-start | bytes 208904 | tf_op jit(solution)/shard_map/ppermute | solution.py:264

commit v2 on v1

--- a/solution.py
+++ b/solution.py
@@ -107,22 +107,46 @@
 
 
 def project_kernel(
+    pept_hbm, x_hbm, occ_hbm, gain_hbm, shift_hbm, wl_hbm, bl_hbm, wr_hbm, br_hbm,
+    left_ref, right_ref,
     pept_ref, x_ref, occ_ref, gain_ref, shift_ref, wl_ref, bl_ref, wr_ref, br_ref,
-    left_ref, right_ref, y_ref, l_ref,
+    y_ref, l_ref, x_sems, sems,
 ):
     residues, sequences = occ_ref.shape
     hidden = wl_ref.shape[0]
-    x = x_ref[...].astype(jnp.float32)
-    average = jnp.mean(x, axis=-1, keepdims=True)
-    centred = x - average
-    spread = jnp.mean(jnp.square(centred), axis=-1, keepdims=True)
-    normed = (centred * lax.rsqrt(spread + 1e-05) * gain_ref[...] + shift_ref[...]).astype(
-        jnp.bfloat16
-    )
+    chunks = x_sems.shape[0]
+    size = x_ref.shape[0] // chunks
+    x_copies = [
+        pltpu.make_async_copy(
+            x_hbm.at[pl.ds(n * size, size)], x_ref.at[pl.ds(n * size, size)], x_sems.at[n]
+        )
+        for n in range(chunks)
+    ]
+    pairs = (
+        (wl_hbm, wl_ref), (wr_hbm, wr_ref), (gain_hbm, gain_ref), (shift_hbm, shift_ref),
+        (bl_hbm, bl_ref), (br_hbm, br_ref), (occ_hbm, occ_ref), (pept_hbm, pept_ref),
+    )
+    copies = [pltpu.make_async_copy(a, b, sems.at[n]) for n, (a, b) in enumerate(pairs)]
+    x_copies[0].start()
+    for copy in copies:
+        copy.start()
+    for copy in x_copies[1:]:
+        copy.start()
+    for copy in copies:
+        copy.wait()
     weight = jnp.concatenate([wl_ref[...], wr_ref[...]], axis=0)
     bias = jnp.concatenate([bl_ref[...], br_ref[...]], axis=1)
-    y = lax.dot_general(normed, weight, NT, preferred_element_type=jnp.float32) + bias
-    y_ref[:, : 2 * hidden] = y
+    for n, copy in enumerate(x_copies):
+        copy.wait()
+        x = x_ref[n * size : (n + 1) * size, :].astype(jnp.float32)
+        average = jnp.mean(x, axis=-1, keepdims=True)
+        centred = x - average
+        spread = jnp.mean(jnp.square(centred), axis=-1, keepdims=True)
+        normed = (centred * lax.rsqrt(spread + 1e-05) * gain_ref[...] + shift_ref[...]).astype(
+            jnp.bfloat16
+        )
+        y = lax.dot_general(normed, weight, NT, preferred_element_type=jnp.float32) + bias
+        y_ref[n * size : (n + 1) * size, : 2 * hidden] = y
     for i in range(residues):
         live = (occ_ref[i : i + 1, :] * pept_ref[i]).astype(jnp.float32)
         part = y_ref[pl.ds(i, sequences, stride=residues), :].T[: 2 * hidden] * live
@@ -134,34 +158,65 @@
     right_ref[hidden * residues :, :] = l_ref[hidden * residues :, :].astype(jnp.bfloat16)
 
 
+def expand(tile, store, hidden):
+    rows, lanes = tile.shape
+    per_vector = 128 // hidden
+    lane = lax.broadcasted_iota(jnp.int32, (rows, 128), 1) // hidden
+    for g in range(lanes // 128):
+        part = tile[:, g * 128 : (g + 1) * 128]
+        for a in range(per_vector):
+            first = (g * per_vector + a) * rows
+            store(first, part * (lane == a).astype(jnp.bfloat16))
+
+
 def pair_kernel(
-    l0, l1, l2, l3, r0, r1, r2, r3, w_ref, b_ref, out_ref, ls_ref, rs_ref, big_ref, p_ref
+    own, l0, l1, r0, r1, r2, r3, w_ref, out_ref, ls_ref, rs_ref, big_ref
 ):
+    body = l0.shape[0] - MASK_ROWS
     hidden = 32
-    body = l0.shape[0] - MASK_ROWS
     residues = body // hidden
-    width = w_ref.shape[1]
     row, col, seq = (lax.axis_index(name) for name in GROUP)
-    for k, (left, right) in enumerate(((l0, r0), (l1, r1), (l2, r2), (l3, r3))):
-        ls_ref[seq ^ (k % 2), col ^ (k // 2)] = left[...]
-        rs_ref[(row % 2) ^ (k % 2), (row // 2) ^ (k // 2)] = right[...]
-
-    def rows(ref, first, last):
-        return jnp.concatenate(
-            [
-                jnp.concatenate([ref[h, p, first:last, :] for p in range(2)], axis=0)
-                for h in range(2)
-            ],
-            axis=1,
-        )
-
-    left = rows(ls_ref, 0, body)
-    right = rows(rs_ref, 0, body)
-    outer = lax.dot_general(left, right, NT, preferred_element_type=jnp.float32)
-    live_i = rows(ls_ref, body, body + MASK_ROWS)
-    live_j = rows(rs_ref, body, body + MASK_ROWS)
+    for k, piece in enumerate((l0, l1)):
+        ls_ref[col ^ k] = piece[...]
+    for k, piece in enumerate((r0, r1, r2, r3)):
+        rs_ref[row ^ k] = piece[...]
+    half = 2 * (seq if own else 1 - seq)
+
+    def rows(ref, at, first, last):
+        return jnp.concatenate([ref[at + p, first:last, :] for p in range(2)], axis=0)
+
+    outer = lax.dot_general(
+        rows(ls_ref, 0, 0, body), rows(rs_ref, half, 0, body), NT, preferred_element_type=jnp.float32
+    )
+    live_i = rows(ls_ref, 0, body, body + MASK_ROWS)
+    live_j = rows(rs_ref, half, body, body + MASK_ROWS)
+    live_j = jnp.concatenate([live_j, jnp.zeros((128 - 2 * MASK_ROWS, live_j.shape[1]), live_j.dtype)], axis=0)
     counts = lax.dot_general(live_i, live_j, NT, preferred_element_type=jnp.float32)
-    spread_shape = (2 * MASK_ROWS, 2 * body)
+    for c in range(hidden):
+        tile = jnp.concatenate(
+            [outer[p * body + c * residues : p * body + (c + 1) * residues] for p in range(2)], axis=0
+        ).astype(jnp.bfloat16)
+
+        def store(first, value, c=c):
+            big_ref[first : first + 2 * residues, c * 128 : (c + 1) * 128] = value
+
+        expand(tile, store, hidden)
+    weight = jnp.concatenate(
+        [w_ref[c * hidden : (c + 1) * hidden, :] for c in range(hidden) for _ in range(128 // hidden)],
+        axis=0,
+    )
+    pairs = 4 * residues * residues
+    projected = jnp.dot(big_ref[...], weight, preferred_element_type=jnp.float32)
+    out_ref[:pairs, :] = projected.astype(out_ref.dtype)
+    out_ref[pairs:, :] = counts.astype(out_ref.dtype)
+
+
+def finish_kernel(mine_ref, other_ref, b_ref, out_ref, big_ref, p_ref):
+    residues = out_ref.shape[0] // 2
+    pairs = 4 * residues * residues
+    hidden = 32
+    counts = mine_ref[pairs:, :] + other_ref[pairs:, :].astype(jnp.float32)
+    spread_shape = (128, 2 * residues * hidden)
     at_row = lax.broadcasted_iota(jnp.int32, spread_shape, 0)
     at_lane = lax.broadcasted_iota(jnp.int32, spread_shape, 1)
     hit = ((at_row // MASK_ROWS) * residues + at_row % MASK_ROWS == at_lane // hidden) & (
@@ -170,53 +225,30 @@
     counts = jnp.dot(
         counts.astype(jnp.bfloat16), hit.astype(jnp.bfloat16), preferred_element_type=jnp.float32
     )
-    per_vector = 128 // hidden
-    lane = lax.broadcasted_iota(jnp.int32, (2 * residues, 128), 1) // hidden
-    masks = [(lane == a).astype(jnp.bfloat16) for a in range(per_vector)]
-
-    def put(slot, low, high):
-        both = jnp.concatenate([low, high], axis=0).astype(jnp.bfloat16)
-        for g in range(2 * residues // per_vector):
-            tile = both[:, g * 128 : (g + 1) * 128]
-            for a in range(per_vector):
-                first = (g * per_vector + a) * 2 * residues
-                big_ref[first : first + 2 * residues, slot * 128 : (slot + 1) * 128] = tile * masks[a]
-
-    for c in range(hidden):
-        put(c, outer[c * residues : (c + 1) * residues], outer[body + c * residues : body + (c + 1) * residues])
-    put(hidden, counts[:residues], counts[MASK_ROWS : MASK_ROWS + residues])
-    weight = jnp.concatenate(
-        [w_ref[c * hidden : (c + 1) * hidden, :] for c in range(hidden) for _ in range(per_vector)],
-        axis=0,
-    )
-    projected = jnp.dot(
-        big_ref[:, : hidden * 128], weight, preferred_element_type=jnp.float32
-    )
-    share = jnp.full((128, width), 1.0 / hidden, jnp.bfloat16)
-    divisor = jnp.dot(big_ref[:, hidden * 128 :], share, preferred_element_type=jnp.float32)
-    p_ref[...] = (projected + b_ref[...]) / jnp.maximum(divisor, 1.0)
+    tile = jnp.concatenate(
+        [counts[p * MASK_ROWS : p * MASK_ROWS + residues] for p in range(2)], axis=0
+    ).astype(jnp.bfloat16)
+
+    def store(first, value):
+        big_ref[first : first + 2 * residues, :] = value
+
+    expand(tile, store, hidden)
+    share = jnp.full((128, 128), 1.0 / hidden, jnp.bfloat16)
+    divisor = jnp.dot(big_ref[...], share, preferred_element_type=jnp.float32)
+    total = mine_ref[:pairs, :] + other_ref[:pairs, :].astype(jnp.float32)
+    p_ref[...] = (total + b_ref[...]) / jnp.maximum(divisor, 1.0)
     for i in range(2 * residues):
         out_ref[i] = p_ref[pl.ds(i, 2 * residues, stride=2 * residues), :].astype(jnp.bfloat16)
 
 
-def left_route(k):
-    route = []
-    for r in range(4):
-        for c in range(2):
-            for q in range(2):
-                to = (2 * c + r // 2, (r % 2) ^ (k // 2), q ^ (k % 2))
-                route.append((4 * r + 2 * c + q, 4 * to[0] + 2 * to[1] + to[2]))
-    return route
-
-
-def right_route(k):
-    route = []
-    for r in range(4):
-        for c in range(2):
-            for q in range(2):
-                to = (2 * ((r % 2) ^ (k // 2)) + (q ^ (k % 2)), c, r // 2)
-                route.append((4 * r + 2 * c + q, 4 * to[0] + 2 * to[1] + to[2]))
-    return route
+def route(target):
+    return [
+        (4 * r + 2 * c + q, 4 * to[0] + 2 * to[1] + to[2])
+        for r in range(4)
+        for c in range(2)
+        for q in range(2)
+        for to in (target(r, c, q),)
+    ]
 
 
 def direct_shards(
@@ -236,18 +268,31 @@
     hidden = lhs_linear_map.shape[1]
     width = closing_linear_map.shape[1]
     rows = residues * hidden + MASK_ROWS
+    pairs = 4 * residues * residues
     payload = jax.ShapeDtypeStruct((rows, sequences), jnp.bfloat16)
     vmem = pl.BlockSpec(memory_space=pltpu.VMEM)
+    in_hbm = pl.BlockSpec(memory_space=pltpu.HBM)
     left, right = pl.pallas_call(
         project_kernel,
         out_shape=(payload, payload),
-        in_specs=[pl.BlockSpec(memory_space=pltpu.SMEM)] + [vmem] * 8,
+        in_specs=[in_hbm] * 9,
         out_specs=(vmem, vmem),
         scratch_shapes=[
+            pltpu.SMEM((residues,), jnp.int32),
+            pltpu.VMEM((sequences * residues, signal), jnp.bfloat16),
+            pltpu.VMEM((residues, sequences), jnp.int32),
+            pltpu.VMEM((1, signal), jnp.float32),
+            pltpu.VMEM((1, signal), jnp.float32),
+            pltpu.VMEM((hidden, signal), jnp.bfloat16),
+            pltpu.VMEM((1, hidden), jnp.float32),
+            pltpu.VMEM((hidden, signal), jnp.bfloat16),
+            pltpu.VMEM((1, hidden), jnp.float32),
             pltpu.VMEM((sequences * residues, 128), jnp.float32),
             pltpu.VMEM((rows, sequences), jnp.float32),
+            pltpu.SemaphoreType.DMA((4,)),
+            pltpu.SemaphoreType.DMA((8,)),
         ],
-        compiler_params=pltpu.CompilerParams(vmem_limit_bytes=24 * 1024 * 1024),
+        compiler_params=pltpu.CompilerParams(vmem_limit_bytes=60 * 1024 * 1024),
         name="normalize_and_project",
     )(
         peptide_occupancy,
@@ -260,22 +305,47 @@
         rhs_linear_map.T,
         rhs_linear_constant.reshape(1, hidden),
     )
-    lefts = [lax.ppermute(left, GROUP, left_route(k)) for k in range(4)]
-    rights = [lax.ppermute(right, GROUP, right_route(k)) for k in range(4)]
+    rights = [right] + [
+        lax.ppermute(right, GROUP, route(lambda r, c, q, k=k: (r ^ k, c, q))) for k in (1, 2, 3)
+    ]
+    lefts = [
+        lax.ppermute(left, GROUP, route(lambda r, c, q, k=k: (2 * c + r // 2, (r % 2) ^ k, q)))
+        for k in range(2)
+    ]
+
+    def pair_sums(own, kind):
+        return pl.pallas_call(
+            lambda *refs: pair_kernel(own, *refs),
+            out_shape=jax.ShapeDtypeStruct((pairs + 2 * MASK_ROWS, width), kind),
+            in_specs=[vmem] * 7,
+            out_specs=vmem,
+            scratch_shapes=[
+                pltpu.VMEM((2, rows, sequences), jnp.bfloat16),
+                pltpu.VMEM((4, rows, sequences), jnp.bfloat16),
+                pltpu.VMEM((pairs, hidden * 128), jnp.bfloat16),
+            ],
+            compiler_params=pltpu.CompilerParams(vmem_limit_bytes=24 * 1024 * 1024),
+            cost_estimate=pl.CostEstimate(
+                flops=2 * pairs * hidden * 128 * width, bytes_accessed=1 << 20, transcendentals=0
+            ),
+            name="own_pair_sums" if own else "other_pair_sums",
+        )(*lefts, *rights, closing_linear_map)
+
+    theirs = pair_sums(False, jnp.bfloat16)
+    received = lax.ppermute(theirs, GROUP, route(lambda r, c, q: (r, c, 1 - q)))
+    mine = pair_sums(True, jnp.float32)
     return pl.pallas_call(
-        pair_kernel,
+        finish_kernel,
         out_shape=jax.ShapeDtypeStruct((2 * residues, 2 * residues, width), jnp.bfloat16),
-        in_specs=[vmem] * 10,
+        in_specs=[vmem] * 3,
         out_specs=vmem,
         scratch_shapes=[
-            pltpu.VMEM((2, 2, rows, sequences), jnp.bfloat16),
-            pltpu.VMEM((2, 2, rows, sequences), jnp.bfloat16),
-            pltpu.VMEM((4 * residues * residues, (hidden + 1) * 128), jnp.bfloat16),
-            pltpu.VMEM((4 * residues * residues, width), jnp.float32),
+            pltpu.VMEM((pairs, 128), jnp.bfloat16),
+            pltpu.VMEM((pairs, width), jnp.float32),
         ],
-        compiler_params=pltpu.CompilerParams(vmem_limit_bytes=32 * 1024 * 1024),
-        name="pair_update",
-    )(*lefts, *rights, closing_linear_map, closing_linear_constant.reshape(1, width))
+        compiler_params=pltpu.CompilerParams(vmem_limit_bytes=16 * 1024 * 1024),
+        name="divide",
+    )(mine, received, closing_linear_constant.reshape(1, width))
 
 
 def shards(*arrays):

time: 30.2 us -> 27.2 us (0.901)
  starting transfers between devices: 21.9 us -> 9.49 us
  waiting for transfers between devices: 1.33 us -> 8.63 us
  Pallas kernels: 3.26 us -> 7.27 us
  local copies, waits for them, and re-layouts: 3.2 us -> 1.53 us
    ppermute x8 -> x6, starting transfers between devices: 21.9 us -> 9.49 us  [the longest x3 5.16 us: direct_shards(): lax.ppermute(right, GROUP, route(lambda r, c, q, k=k: (r ^ k, c, q)))]
    ppermute x8 -> x6, waiting for transfers between devices: 1.33 us -> 8.63 us  [the longest x3 8.62 us: direct_shards(): lax.ppermute(right, GROUP, route(lambda r, c, q, k=k: (r ^ k, c, q)))]
    pallas_call x2 -> x4, Pallas kernels: 3.26 us -> 7.27 us  [the longest x1 3.5 us: direct_shards(): pl.pallas_call(project_kernel, out_shape=(payload, payload), in_specs=[in...]
    unnamed x22 -> x6, local copies, waits for them, and re-layouts: 3.2 us -> 1.53 us
  transfers between devices with their start and end apart: 8 -> 6, of which waited for: 2 -> 2; matrix products, arithmetic and copies ran while one was open for 0% -> 0% of each run, Pallas kernels for 0% -> 5%
where the time goes in v2:
time: 27.2 us; the launch traced here: 26.9 us
  starting transfers between devices  9.49 us (35%)
  waiting for transfers between devices  8.63 us (32%)
  Pallas kernels  7.27 us (27%)
  local copies, waits for them, and re-layouts  1.53 us (6%)
    ppermute x3, waiting for transfers between devices, direct_shards(): lax.ppermute(right, GROUP, route(lambda r, c, q, k=k: (r ^ k, c, q)))  8.62 us
    ppermute x3, starting transfers between devices, direct_shards(): lax.ppermute(right, GROUP, route(lambda r, c, q, k=k: (r ^ k, c, q)))  5.16 us
    ppermute x2, starting transfers between devices, direct_shards(): lax.ppermute(left, GROUP, route(lambda r, c, q, k=k: (2 * c + r // 2, r %...  3.62 us
    pallas_call x1, Pallas kernels, direct_shards(): pl.pallas_call(project_kernel, out_shape=(payload, payload), in_specs=[in...  3.5 us
    pallas_call x2, Pallas kernels, pair_sums(): pl.pallas_call(lambda *refs: pair_kernel(own, *refs), out_shape=jax.Shape...  2.8 us
    unnamed x6, local copies, waits for them, and re-layouts  1.53 us
    pallas_call x1, Pallas kernels, direct_shards(): pl.pallas_call(finish_kernel, out_shape=jax.ShapeDtypeStruct((2 * residue...  0.96 us
    ppermute x1, starting transfers between devices, direct_shards(): received = lax.ppermute(theirs, GROUP, route(lambda r, c, q: (r, c, 1 - q)))  0.71 us
  transfers between devices with their start and end apart: 6, of which 2 were waited for; matrix products, arithmetic and copies ran while one was open for 0% of the time, Pallas kernels for 5%

profile of v2, /device:TPU:1, one launch (start us, length us, event | category | flops | bytes accessed | tf_op | source)
XLA Modules:
  0.0 26.9 jit_solution(6924854857524880221)
XLA Ops:
  0.0 0.0 copy-start.1
  0.0 3.5 %normalize_and_project.1 = (bf16[272,128]{1,0:T(8,128)(2,1)}, bf16[272,128]{1,0:T(8,128)(2,1)}) custom-call(s32[8]{0:T(128)} %pept_hbm.1, bf16[1024,256]{1,0:T(8,128)(2,1)} %bitcast.10, s32[8,128]{1,0:T(8,128)} %bitcast.13, f32[1,256]{1,0:T(1,128)} %bitcast.14, f32[1,256]{1,0:T(1,128)} %bitcast.15, bf16[32,256]{1,0:T(8,128)(2,1)} %bitcast.11, ...), custom_call_target="tpu_custom_call" | custom-call | tf_op jit(solution)/shard_map/normalize_and_project/pallas_call | solution.py:275
  3.5 2.1 %collective-permute-start.1 = (bf16[272,128]{1,0:T(8,128)(2,1)}, bf16[272,128]{1,0:T(8,128)(2,1)S(1)}, u32[]{:S(2)}, u32[]{:S(2)}) collective-permute-start(bf16[272,128]{1,0:T(8,128)(2,1)} %get-tuple-element.7), channel_id=1, source_target_pairs={{0,2},{1,3},{2,10},{3,11},{4,0},{5,1},{6,8},{7,9},{8,6},{9,7},{10,... | collective-permute-start | bytes 208904 | tf_op jit(solution)/shard_map/ppermute | solution.py:312
  5.6 1.5 %collective-permute-start = (bf16[272,128]{1,0:T(8,128)(2,1)}, bf16[272,128]{1,0:T(8,128)(2,1)S(1)}, u32[]{:S(2)}, u32[]{:S(2)}) collective-permute-start(bf16[272,128]{1,0:T(8,128)(2,1)} %get-tuple-element.7), channel_id=1, source_target_pairs={{0,0},{1,1},{2,8},{3,9},{4,2},{5,3},{6,10},{7,11},{8,4},{9,5},{10,... | collective-permute-start | bytes 208904 | tf_op jit(solution)/shard_map/ppermute | solution.py:312
  7.1 4.8 %collective-permute-start.4 = (bf16[272,128]{1,0:T(8,128)(2,1)}, bf16[272,128]{1,0:T(8,128)(2,1)S(1)}, u32[]{:S(2)}, u32[]{:S(2)}) collective-permute-start(bf16[272,128]{1,0:T(8,128)(2,1)} %get-tuple-element.8.refs_2_), channel_id=1, source_target_pairs={{0,12},{1,13},{2,14},{3,15},{4,8},{5,9},{6,10},{7,11},{8,4},{9,5},... | collective-permute-start | bytes 208904 | tf_op jit(solution)/shard_map/ppermute | solution.py:309
  11.9 0.3 %collective-permute-start.3 = (bf16[272,128]{1,0:T(8,128)(2,1)}, bf16[272,128]{1,0:T(8,128)(2,1)S(1)}, u32[]{:S(2)}, u32[]{:S(2)}) collective-permute-start(bf16[272,128]{1,0:T(8,128)(2,1)} %get-tuple-element.8.refs_2_), channel_id=1, source_target_pairs={{0,8},{1,9},{2,10},{3,11},{4,12},{5,13},{6,14},{7,15},{8,0},{9,1},... | collective-permute-start | bytes 208904 | tf_op jit(solution)/shard_map/ppermute | solution.py:309
  12.2 0.1 collective-permute-start.2
  12.3 0.0 collective-permute-done.1.refs_1_
  12.3 0.0 collective-permute-done.refs_0_
  12.3 2.4 %collective-permute-done.4.refs_5_ = bf16[272,128]{1,0:T(8,128)(2,1)S(1)} collective-permute-done((bf16[272,128]{1,0:T(8,128)(2,1)}, bf16[272,128]{1,0:T(8,128)(2,1)S(1)}, u32[]{:S(2)}, u32[]{:S(2)}) %collective-permute-start.4) | collective-permute-done | bytes 69664 | tf_op jit(solution)/shard_map/ppermute | solution.py:309
  14.7 6.2 %collective-permute-done.3.refs_4_ = bf16[272,128]{1,0:T(8,128)(2,1)S(1)} collective-permute-done((bf16[272,128]{1,0:T(8,128)(2,1)}, bf16[272,128]{1,0:T(8,128)(2,1)S(1)}, u32[]{:S(2)}, u32[]{:S(2)}) %collective-permute-start.3) | collective-permute-done | bytes 69664 | tf_op jit(solution)/shard_map/ppermute | solution.py:309
  20.9 0.0 collective-permute-done.2.refs_3_
  20.9 0.0 copy-done.1
  20.9 0.0 copy-start.2
  20.9 0.9 %copy-done.2 = bf16[272,128]{1,0:T(8,128)(2,1)S(1)} copy-done((bf16[272,128]{1,0:T(8,128)(2,1)S(1)}, bf16[272,128]{1,0:T(8,128)(2,1)}, u32[]{:S(2)}) %copy-start.2) | copy-done | bytes 69656
  21.8 1.4 %other_pair_sums.1 = bf16[288,128]{1,0:T(8,128)(2,1)S(1)} custom-call(bf16[272,128]{1,0:T(8,128)(2,1)S(1)} %collective-permute-done.refs_0_, bf16[272,128]{1,0:T(8,128)(2,1)S(1)} %collective-permute-done.1.refs_1_, bf16[272,128]{1,0:T(8,128)(2,1)S(1)} %copy-done.2, bf16[272,128]{1,0:T(8,128)(2,1)S(1)} %collective-permute-done.2.refs_3_, ...), custom_call_target="tpu_custom_call" | custom-call | flops 268435456 | bytes 1048576 | tf_op jit(solution)/shard_map/other_pair_sums/pallas_call | solution.py:317
  23.2 0.7 %collective-permute-start.5 = (bf16[288,128]{1,0:T(8,128)(2,1)S(1)}, bf16[288,128]{1,0:T(8,128)(2,1)S(1)}, u32[]{:S(2)}, u32[]{:S(2)}) collective-permute-start(bf16[288,128]{1,0:T(8,128)(2,1)S(1)} %other_pair_sums.1), channel_id=1, source_target_pairs={{0,1},{1,0},{2,3},{3,2},{4,5},{5,4},{6,7},{7,6},{8,9},{9,8},{10,11... | collective-permute-start | bytes 221192 | tf_op jit(solution)/shard_map/ppermute | solution.py:335
  23.9 1.4 %own_pair_sums.1.mine_ref = f32[288,128]{1,0:T(8,128)S(1)} custom-call(bf16[272,128]{1,0:T(8,128)(2,1)S(1)} %collective-permute-done.refs_0_, bf16[272,128]{1,0:T(8,128)(2,1)S(1)} %collective-permute-done.1.refs_1_, bf16[272,128]{1,0:T(8,128)(2,1)S(1)} %copy-done.2, bf16[272,128]{1,0:T(8,128)(2,1)S(1)} %collective-permute-done.2.refs_3_, ...), custom_call_target="tpu_custom_call" | custom-call | flops 268435456 | bytes 1048576 | tf_op jit(solution)/shard_map/own_pair_sums/pallas_call | solution.py:317
  25.3 0.0 copy-start
  25.3 0.0 collective-permute-done.5.other_ref
  25.3 0.6 %copy-done = f32[128]{0:T(128)S(1)} copy-done((f32[128]{0:T(128)S(1)}, f32[128]{0:T(128)}, u32[]{:S(2)}) %copy-start) | copy-done | bytes 536
  26.0 1.0 %divide.1 = bf16[16,16,128]{2,1,0:T(8,128)(2,1)} custom-call(f32[288,128]{1,0:T(8,128)S(1)} %own_pair_sums.1.mine_ref, bf16[288,128]{1,0:T(8,128)(2,1)S(1)} %collective-permute-done.5.other_ref, f32[1,128]{1,0:T(1,128)S(1)} %bitcast.9), custom_call_target="tpu_custom_call" | custom-call | tf_op jit(solution)/shard_map/divide/pallas_call | solution.py:337
Async XLA Ops:
  0.0 20.9 %copy-start.1 = (bf16[1024,128]{1,0:T(8,128)(2,1)S(1)}, bf16[1024,128]{1,0:T(8,128)(2,1)}, u32[]{:S(2)}) copy-start(bf16[1024,128]{1,0:T(8,128)(2,1)} %refs_6_.3) | copy-start | bytes 786436
  3.5 8.8 %collective-permute-start.1 = (bf16[272,128]{1,0:T(8,128)(2,1)}, bf16[272,128]{1,0:T(8,128)(2,1)S(1)}, u32[]{:S(2)}, u32[]{:S(2)}) collective-permute-start(bf16[272,128]{1,0:T(8,128)(2,1)} %get-tuple-element.7), channel_id=1, source_target_pairs={{0,2},{1,3},{2,10},{3,11},{4,0},{5,1},{6,8},{7,9},{8,6},{9,7},{10,... | collective-permute-start | bytes 208904 | tf_op jit(solution)/shard_map/ppermute | solution.py:312
  5.6 6.7 %collective-permute-start = (bf16[272,128]{1,0:T(8,128)(2,1)}, bf16[272,128]{1,0:T(8,128)(2,1)S(1)}, u32[]{:S(2)}, u32[]{:S(2)}) collective-permute-start(bf16[272,128]{1,0:T(8,128)(2,1)} %get-tuple-element.7), channel_id=1, source_target_pairs={{0,0},{1,1},{2,8},{3,9},{4,2},{5,3},{6,10},{7,11},{8,4},{9,5},{10,... | collective-permute-start | bytes 208904 | tf_op jit(solution)/shard_map/ppermute | solution.py:312
  7.1 7.6 %collective-permute-start.4 = (bf16[272,128]{1,0:T(8,128)(2,1)}, bf16[272,128]{1,0:T(8,128)(2,1)S(1)}, u32[]{:S(2)}, u32[]{:S(2)}) collective-permute-start(bf16[272,128]{1,0:T(8,128)(2,1)} %get-tuple-element.8.refs_2_), channel_id=1, source_target_pairs={{0,12},{1,13},{2,14},{3,15},{4,8},{5,9},{6,10},{7,11},{8,4},{9,5},... | collective-permute-start | bytes 208904 | tf_op jit(solution)/shard_map/ppermute | solution.py:309
  11.9 9.0 %collective-permute-start.3 = (bf16[272,128]{1,0:T(8,128)(2,1)}, bf16[272,128]{1,0:T(8,128)(2,1)S(1)}, u32[]{:S(2)}, u32[]{:S(2)}) collective-permute-start(bf16[272,128]{1,0:T(8,128)(2,1)} %get-tuple-element.8.refs_2_), channel_id=1, source_target_pairs={{0,8},{1,9},{2,10},{3,11},{4,12},{5,13},{6,14},{7,15},{8,0},{9,1},... | collective-permute-start | bytes 208904 | tf_op jit(solution)/shard_map/ppermute | solution.py:309
  12.2 8.7 %collective-permute-start.2 = (bf16[272,128]{1,0:T(8,128)(2,1)}, bf16[272,128]{1,0:T(8,128)(2,1)S(1)}, u32[]{:S(2)}, u32[]{:S(2)}) collective-permute-start(bf16[272,128]{1,0:T(8,128)(2,1)} %get-tuple-element.8.refs_2_), channel_id=1, source_target_pairs={{0,4},{1,5},{2,6},{3,7},{4,0},{5,1},{6,2},{7,3},{8,12},{9,13},{10,... | collective-permute-start | bytes 208904 | tf_op jit(solution)/shard_map/ppermute | solution.py:309
  20.9 0.9 %copy-start.2 = (bf16[272,128]{1,0:T(8,128)(2,1)S(1)}, bf16[272,128]{1,0:T(8,128)(2,1)}, u32[]{:S(2)}) copy-start(bf16[272,128]{1,0:T(8,128)(2,1)} %get-tuple-element.8.refs_2_) | copy-start | bytes 208900
  23.2 2.1 %collective-permute-start.5 = (bf16[288,128]{1,0:T(8,128)(2,1)S(1)}, bf16[288,128]{1,0:T(8,128)(2,1)S(1)}, u32[]{:S(2)}, u32[]{:S(2)}) collective-permute-start(bf16[288,128]{1,0:T(8,128)(2,1)S(1)} %other_pair_sums.1), channel_id=1, source_target_pairs={{0,1},{1,0},{2,3},{3,2},{4,5},{5,4},{6,7},{7,6},{8,9},{9,8},{10,11... | collective-permute-start | bytes 221192 | tf_op jit(solution)/shard_map/ppermute | solution.py:335
  25.3 0.7 %copy-start = (f32[128]{0:T(128)S(1)}, f32[128]{0:T(128)}, u32[]{:S(2)}) copy-start(f32[128]{0:T(128)} %param.21) | copy-start | bytes 1540

commit v3 on v2

--- a/solution.py
+++ b/solution.py
@@ -170,8 +170,11 @@
 
 
 def pair_kernel(
-    own, l0, l1, r0, r1, r2, r3, w_ref, out_ref, ls_ref, rs_ref, big_ref
+    own, l0, l1, r0, r1, r2, r3, w_ref, b_hbm, out_ref, ls_ref, rs_ref, big_ref, b_ref, b_sem
 ):
+    if own:
+        bias_copy = pltpu.make_async_copy(b_hbm, b_ref, b_sem)
+        bias_copy.start()
     body = l0.shape[0] - MASK_ROWS
     hidden = 32
     residues = body // hidden
@@ -207,11 +210,14 @@
     )
     pairs = 4 * residues * residues
     projected = jnp.dot(big_ref[...], weight, preferred_element_type=jnp.float32)
+    if own:
+        bias_copy.wait()
+        projected = projected + b_ref[...]
     out_ref[:pairs, :] = projected.astype(out_ref.dtype)
     out_ref[pairs:, :] = counts.astype(out_ref.dtype)
 
 
-def finish_kernel(mine_ref, other_ref, b_ref, out_ref, big_ref, p_ref):
+def finish_kernel(mine_ref, other_ref, out_ref, big_ref, p_ref):
     residues = out_ref.shape[0] // 2
     pairs = 4 * residues * residues
     hidden = 32
@@ -236,7 +242,7 @@
     share = jnp.full((128, 128), 1.0 / hidden, jnp.bfloat16)
     divisor = jnp.dot(big_ref[...], share, preferred_element_type=jnp.float32)
     total = mine_ref[:pairs, :] + other_ref[:pairs, :].astype(jnp.float32)
-    p_ref[...] = (total + b_ref[...]) / jnp.maximum(divisor, 1.0)
+    p_ref[...] = total / jnp.maximum(divisor, 1.0)
     for i in range(2 * residues):
         out_ref[i] = p_ref[pl.ds(i, 2 * residues, stride=2 * residues), :].astype(jnp.bfloat16)
 
@@ -305,31 +311,33 @@
         rhs_linear_map.T,
         rhs_linear_constant.reshape(1, hidden),
     )
-    rights = [right] + [
-        lax.ppermute(right, GROUP, route(lambda r, c, q, k=k: (r ^ k, c, q))) for k in (1, 2, 3)
-    ]
-    lefts = [
-        lax.ppermute(left, GROUP, route(lambda r, c, q, k=k: (2 * c + r // 2, (r % 2) ^ k, q)))
-        for k in range(2)
-    ]
+    far = lax.ppermute(right, GROUP, route(lambda r, c, q: (r ^ 2, c, q)))
+    near = lax.ppermute(right, GROUP, route(lambda r, c, q: (r ^ 1, c, q)))
+    first = lax.ppermute(left, GROUP, route(lambda r, c, q: (2 * c + r // 2, r % 2, q)))
+    passed = lax.ppermute(far, GROUP, route(lambda r, c, q: (r ^ 1, c, q)))
+    second = lax.ppermute(first, GROUP, route(lambda r, c, q: (r, 1 - c, q)))
+    rights = [right, near, far, passed]
+    lefts = [first, second]
 
     def pair_sums(own, kind):
         return pl.pallas_call(
             lambda *refs: pair_kernel(own, *refs),
             out_shape=jax.ShapeDtypeStruct((pairs + 2 * MASK_ROWS, width), kind),
-            in_specs=[vmem] * 7,
+            in_specs=[vmem] * 7 + [in_hbm],
             out_specs=vmem,
             scratch_shapes=[
                 pltpu.VMEM((2, rows, sequences), jnp.bfloat16),
                 pltpu.VMEM((4, rows, sequences), jnp.bfloat16),
                 pltpu.VMEM((pairs, hidden * 128), jnp.bfloat16),
+                pltpu.VMEM((1, width), jnp.float32),
+                pltpu.SemaphoreType.DMA,
             ],
             compiler_params=pltpu.CompilerParams(vmem_limit_bytes=24 * 1024 * 1024),
             cost_estimate=pl.CostEstimate(
                 flops=2 * pairs * hidden * 128 * width, bytes_accessed=1 << 20, transcendentals=0
             ),
             name="own_pair_sums" if own else "other_pair_sums",
-        )(*lefts, *rights, closing_linear_map)
+        )(*lefts, *rights, closing_linear_map, closing_linear_constant.reshape(1, width))
 
     theirs = pair_sums(False, jnp.bfloat16)
     received = lax.ppermute(theirs, GROUP, route(lambda r, c, q: (r, c, 1 - q)))
@@ -337,7 +345,7 @@
     return pl.pallas_call(
         finish_kernel,
         out_shape=jax.ShapeDtypeStruct((2 * residues, 2 * residues, width), jnp.bfloat16),
-        in_specs=[vmem] * 3,
+        in_specs=[vmem] * 2,
         out_specs=vmem,
         scratch_shapes=[
             pltpu.VMEM((pairs, 128), jnp.bfloat16),
@@ -345,7 +353,7 @@
         ],
         compiler_params=pltpu.CompilerParams(vmem_limit_bytes=16 * 1024 * 1024),
         name="divide",
-    )(mine, received, closing_linear_constant.reshape(1, width))
+    )(mine, received)
 
 
 def shards(*arrays):

time: 27.2 us -> 26.3 us (0.967)
  waiting for transfers between devices: 8.63 us -> 2.35 us
  starting transfers between devices: 9.49 us -> 15.1 us
  local copies, waits for them, and re-layouts: 1.53 us -> 0.89 us
  Pallas kernels: 7.27 us -> 7.62 us
    ppermute x5, waiting for transfers between devices: 8.62 us -> 2.35 us  [the longest x1 1.97 us: direct_shards(): passed = lax.ppermute(far, GROUP, route(lambda r, c, q: (r ^ 1, c, q)))]
    ppermute x1, starting transfers between devices: 0.71 us -> 4.65 us  [direct_shards(): received = lax.ppermute(theirs, GROUP, route(lambda r, c, q: (r, c, 1 - q)))]
    ppermute x5, starting transfers between devices: 8.78 us -> 10.5 us  [the longest x1 3.76 us: direct_shards(): far = lax.ppermute(right, GROUP, route(lambda r, c, q: (r ^ 2, c, q)))]
    unnamed x6, local copies, waits for them, and re-layouts: 1.53 us -> 0.89 us
    pallas_call x2, Pallas kernels: 2.8 us -> 3.16 us  [pair_sums(): pl.pallas_call(lambda *refs: pair_kernel(own, *refs), out_shape=jax.Shape...]
  transfers between devices with their start and end apart: 6 -> 6, of which waited for: 2 -> 2; matrix products, arithmetic and copies ran while one was open for 0% -> 0% of each run, Pallas kernels for 5% -> 7%
where the time goes in v3:
time: 26.3 us; the launch traced here: 26.1 us
  starting transfers between devices  15.1 us (57%)
  Pallas kernels  7.62 us (29%)
  waiting for transfers between devices  2.35 us (9%)
  local copies, waits for them, and re-layouts  0.89 us (3%)
    ppermute x1, starting transfers between devices, direct_shards(): received = lax.ppermute(theirs, GROUP, route(lambda r, c, q: (r, c, 1 - q)))  4.65 us
    ppermute x1, starting transfers between devices, direct_shards(): far = lax.ppermute(right, GROUP, route(lambda r, c, q: (r ^ 2, c, q)))  3.76 us
    pallas_call x1, Pallas kernels, direct_shards(): pl.pallas_call(project_kernel, out_shape=(payload, payload), in_specs=[in...  3.5 us
    pallas_call x2, Pallas kernels, pair_sums(): pl.pallas_call(lambda *refs: pair_kernel(own, *refs), out_shape=jax.Shape...  3.16 us
    ppermute x1, starting transfers between devices, direct_shards(): passed = lax.ppermute(far, GROUP, route(lambda r, c, q: (r ^ 1, c, q)))  2.3 us
    ppermute x1, starting transfers between devices, direct_shards(): near = lax.ppermute(right, GROUP, route(lambda r, c, q: (r ^ 1, c, q)))  2.11 us
    ppermute x1, waiting for transfers between devices, direct_shards(): passed = lax.ppermute(far, GROUP, route(lambda r, c, q: (r ^ 1, c, q)))  1.97 us
    ppermute x1, starting transfers between devices, direct_shards(): lax.ppermute(left, GROUP, route(lambda r, c, q: (2 * c + r // 2, r % 2, q)))  1.54 us
  transfers between devices with their start and end apart: 6, of which 2 were waited for; matrix products, arithmetic and copies ran while one was open for 0% of the time, Pallas kernels for 7%

profile of v3, /device:TPU:1, one launch (start us, length us, event | category | flops | bytes accessed | tf_op | source)
XLA Modules:
  0.0 26.1 jit_solution(9463560403206121210)
XLA Ops:
  0.0 0.0 copy-start
  0.0 3.5 %normalize_and_project.1 = (bf16[272,128]{1,0:T(8,128)(2,1)}, bf16[272,128]{1,0:T(8,128)(2,1)}) custom-call(s32[8]{0:T(128)} %pept_hbm.1, bf16[1024,256]{1,0:T(8,128)(2,1)} %bitcast.11, s32[8,128]{1,0:T(8,128)} %bitcast.14, f32[1,256]{1,0:T(1,128)} %bitcast.15, f32[1,256]{1,0:T(1,128)} %bitcast.16, bf16[32,256]{1,0:T(8,128)(2,1)} %bitcast.12, ...), custom_call_target="tpu_custom_call" | custom-call | tf_op jit(solution)/shard_map/normalize_and_project/pallas_call | solution.py:281
  3.5 1.5 %collective-permute-start = (bf16[272,128]{1,0:T(8,128)(2,1)}, bf16[272,128]{1,0:T(8,128)(2,1)S(1)}, u32[]{:S(2)}, u32[]{:S(2)}) collective-permute-start(bf16[272,128]{1,0:T(8,128)(2,1)} %get-tuple-element.7), channel_id=1, source_target_pairs={{0,0},{1,1},{2,8},{3,9},{4,2},{5,3},{6,10},{7,11},{8,4},{9,5},{10,... | collective-permute-start | bytes 208904 | tf_op jit(solution)/shard_map/ppermute | solution.py:316
  5.0 0.0 copy-start.2
  5.0 3.8 %collective-permute-start.3 = (bf16[272,128]{1,0:T(8,128)(2,1)}, bf16[272,128]{1,0:T(8,128)(2,1)S(1)}, u32[]{:S(2)}, u32[]{:S(2)}) collective-permute-start(bf16[272,128]{1,0:T(8,128)(2,1)} %get-tuple-element.8.refs_2_), channel_id=1, source_target_pairs={{0,8},{1,9},{2,10},{3,11},{4,12},{5,13},{6,14},{7,15},{8,0},{9,1},... | collective-permute-start | bytes 208904 | tf_op jit(solution)/shard_map/ppermute | solution.py:314
  8.8 2.1 %collective-permute-start.2 = (bf16[272,128]{1,0:T(8,128)(2,1)}, bf16[272,128]{1,0:T(8,128)(2,1)S(1)}, u32[]{:S(2)}, u32[]{:S(2)}) collective-permute-start(bf16[272,128]{1,0:T(8,128)(2,1)} %get-tuple-element.8.refs_2_), channel_id=1, source_target_pairs={{0,4},{1,5},{2,6},{3,7},{4,0},{5,1},{6,2},{7,3},{8,12},{9,13},{10,... | collective-permute-start | bytes 208904 | tf_op jit(solution)/shard_map/ppermute | solution.py:315
  10.9 0.0 collective-permute-done.refs_0_
  10.9 0.8 %collective-permute-start.1 = (bf16[272,128]{1,0:T(8,128)(2,1)S(1)}, bf16[272,128]{1,0:T(8,128)(2,1)S(1)}, u32[]{:S(2)}, u32[]{:S(2)}) collective-permute-start(bf16[272,128]{1,0:T(8,128)(2,1)S(1)} %collective-permute-done.refs_0_), channel_id=1, source_target_pairs={{0,2},{1,3},{2,0},{3,1},{4,6},{5,7},{6,4},{7,5},{8,10},{9,11},{10,... | collective-permute-start | bytes 208904 | tf_op jit(solution)/shard_map/ppermute | solution.py:318
  11.7 0.0 collective-permute-done.3.refs_4_
  11.7 2.3 %collective-permute-start.4 = (bf16[272,128]{1,0:T(8,128)(2,1)S(1)}, bf16[272,128]{1,0:T(8,128)(2,1)S(1)}, u32[]{:S(2)}, u32[]{:S(2)}) collective-permute-start(bf16[272,128]{1,0:T(8,128)(2,1)S(1)} %collective-permute-done.3.refs_4_), channel_id=1, source_target_pairs={{0,4},{1,5},{2,6},{3,7},{4,0},{5,1},{6,2},{7,3},{8,12},{9,13},{10,... | collective-permute-start | bytes 208904 | tf_op jit(solution)/shard_map/ppermute | solution.py:317
  14.0 0.0 collective-permute-done.2.refs_3_
  14.0 0.4 %collective-permute-done.1.refs_1_ = bf16[272,128]{1,0:T(8,128)(2,1)S(1)} collective-permute-done((bf16[272,128]{1,0:T(8,128)(2,1)S(1)}, bf16[272,128]{1,0:T(8,128)(2,1)S(1)}, u32[]{:S(2)}, u32[]{:S(2)}) %collective-permute-start.1) | collective-permute-done | bytes 69664 | tf_op jit(solution)/shard_map/ppermute | solution.py:318
  14.4 2.0 %collective-permute-done.4.refs_5_ = bf16[272,128]{1,0:T(8,128)(2,1)S(1)} collective-permute-done((bf16[272,128]{1,0:T(8,128)(2,1)S(1)}, bf16[272,128]{1,0:T(8,128)(2,1)S(1)}, u32[]{:S(2)}, u32[]{:S(2)}) %collective-permute-start.4) | collective-permute-done | bytes 69664 | tf_op jit(solution)/shard_map/ppermute | solution.py:317
  16.4 0.0 copy-done
  16.4 0.0 copy-done.2
  16.4 0.0 copy-start.1
  16.4 0.9 %copy-done.1 = bf16[272,128]{1,0:T(8,128)(2,1)S(1)} copy-done((bf16[272,128]{1,0:T(8,128)(2,1)S(1)}, bf16[272,128]{1,0:T(8,128)(2,1)}, u32[]{:S(2)}) %copy-start.1) | copy-done | bytes 69656
  17.2 1.4 %other_pair_sums.1 = bf16[288,128]{1,0:T(8,128)(2,1)S(1)} custom-call(bf16[272,128]{1,0:T(8,128)(2,1)S(1)} %collective-permute-done.refs_0_, bf16[272,128]{1,0:T(8,128)(2,1)S(1)} %collective-permute-done.1.refs_1_, bf16[272,128]{1,0:T(8,128)(2,1)S(1)} %copy-done.1, bf16[272,128]{1,0:T(8,128)(2,1)S(1)} %collective-permute-done.2.refs_3_, ...), custom_call_target="tpu_custom_call" | custom-call | flops 268435456 | bytes 1048576 | tf_op jit(solution)/shard_map/other_pair_sums/pallas_call | solution.py:323
  18.7 4.7 %collective-permute-start.5 = (bf16[288,128]{1,0:T(8,128)(2,1)S(1)}, bf16[288,128]{1,0:T(8,128)(2,1)S(1)}, u32[]{:S(2)}, u32[]{:S(2)}) collective-permute-start(bf16[288,128]{1,0:T(8,128)(2,1)S(1)} %other_pair_sums.1), channel_id=1, source_target_pairs={{0,1},{1,0},{2,3},{3,2},{4,5},{5,4},{6,7},{7,6},{8,9},{9,8},{10,11... | collective-permute-start | bytes 221192 | tf_op jit(solution)/shard_map/ppermute | solution.py:343
  23.3 1.7 %own_pair_sums.1.mine_ref = f32[288,128]{1,0:T(8,128)S(1)} custom-call(bf16[272,128]{1,0:T(8,128)(2,1)S(1)} %collective-permute-done.refs_0_, bf16[272,128]{1,0:T(8,128)(2,1)S(1)} %collective-permute-done.1.refs_1_, bf16[272,128]{1,0:T(8,128)(2,1)S(1)} %copy-done.1, bf16[272,128]{1,0:T(8,128)(2,1)S(1)} %collective-permute-done.2.refs_3_, ...), custom_call_target="tpu_custom_call" | custom-call | flops 268435456 | bytes 1048576 | tf_op jit(solution)/shard_map/own_pair_sums/pallas_call | solution.py:323
  25.1 0.0 collective-permute-done.5.other_ref
  25.1 1.0 %divide.1 = bf16[16,16,128]{2,1,0:T(8,128)(2,1)} custom-call(f32[288,128]{1,0:T(8,128)S(1)} %own_pair_sums.1.mine_ref, bf16[288,128]{1,0:T(8,128)(2,1)S(1)} %collective-permute-done.5.other_ref), custom_call_target="tpu_custom_call" | custom-call | tf_op jit(solution)/shard_map/divide/pallas_call | solution.py:345
Async XLA Ops:
  0.0 16.4 %copy-start = (bf16[1024,128]{1,0:T(8,128)(2,1)S(1)}, bf16[1024,128]{1,0:T(8,128)(2,1)}, u32[]{:S(2)}) copy-start(bf16[1024,128]{1,0:T(8,128)(2,1)} %refs_6_.3) | copy-start | bytes 786436
  3.5 7.4 %collective-permute-start = (bf16[272,128]{1,0:T(8,128)(2,1)}, bf16[272,128]{1,0:T(8,128)(2,1)S(1)}, u32[]{:S(2)}, u32[]{:S(2)}) collective-permute-start(bf16[272,128]{1,0:T(8,128)(2,1)} %get-tuple-element.7), channel_id=1, source_target_pairs={{0,0},{1,1},{2,8},{3,9},{4,2},{5,3},{6,10},{7,11},{8,4},{9,5},{10,... | collective-permute-start | bytes 208904 | tf_op jit(solution)/shard_map/ppermute | solution.py:316
  5.0 11.3 %copy-start.2 = (f32[128]{0:T(128)S(1)}, f32[128]{0:T(128)}, u32[]{:S(2)}) copy-start(f32[128]{0:T(128)} %param.21) | copy-start | bytes 1540
  5.0 6.7 %collective-permute-start.3 = (bf16[272,128]{1,0:T(8,128)(2,1)}, bf16[272,128]{1,0:T(8,128)(2,1)S(1)}, u32[]{:S(2)}, u32[]{:S(2)}) collective-permute-start(bf16[272,128]{1,0:T(8,128)(2,1)} %get-tuple-element.8.refs_2_), channel_id=1, source_target_pairs={{0,8},{1,9},{2,10},{3,11},{4,12},{5,13},{6,14},{7,15},{8,0},{9,1},... | collective-permute-start | bytes 208904 | tf_op jit(solution)/shard_map/ppermute | solution.py:314
  8.8 5.2 %collective-permute-start.2 = (bf16[272,128]{1,0:T(8,128)(2,1)}, bf16[272,128]{1,0:T(8,128)(2,1)S(1)}, u32[]{:S(2)}, u32[]{:S(2)}) collective-permute-start(bf16[272,128]{1,0:T(8,128)(2,1)} %get-tuple-element.8.refs_2_), channel_id=1, source_target_pairs={{0,4},{1,5},{2,6},{3,7},{4,0},{5,1},{6,2},{7,3},{8,12},{9,13},{10,... | collective-permute-start | bytes 208904 | tf_op jit(solution)/shard_map/ppermute | solution.py:315
  10.9 3.5 %collective-permute-start.1 = (bf16[272,128]{1,0:T(8,128)(2,1)S(1)}, bf16[272,128]{1,0:T(8,128)(2,1)S(1)}, u32[]{:S(2)}, u32[]{:S(2)}) collective-permute-start(bf16[272,128]{1,0:T(8,128)(2,1)S(1)} %collective-permute-done.refs_0_), channel_id=1, source_target_pairs={{0,2},{1,3},{2,0},{3,1},{4,6},{5,7},{6,4},{7,5},{8,10},{9,11},{10,... | collective-permute-start | bytes 208904 | tf_op jit(solution)/shard_map/ppermute | solution.py:318
  11.7 4.6 %collective-permute-start.4 = (bf16[272,128]{1,0:T(8,128)(2,1)S(1)}, bf16[272,128]{1,0:T(8,128)(2,1)S(1)}, u32[]{:S(2)}, u32[]{:S(2)}) collective-permute-start(bf16[272,128]{1,0:T(8,128)(2,1)S(1)} %collective-permute-done.3.refs_4_), channel_id=1, source_target_pairs={{0,4},{1,5},{2,6},{3,7},{4,0},{5,1},{6,2},{7,3},{8,12},{9,13},{10,... | collective-permute-start | bytes 208904 | tf_op jit(solution)/shard_map/ppermute | solution.py:317
  16.4 0.9 %copy-start.1 = (bf16[272,128]{1,0:T(8,128)(2,1)S(1)}, bf16[272,128]{1,0:T(8,128)(2,1)}, u32[]{:S(2)}) copy-start(bf16[272,128]{1,0:T(8,128)(2,1)} %get-tuple-element.8.refs_2_) | copy-start | bytes 208900
  18.7 6.4 %collective-permute-start.5 = (bf16[288,128]{1,0:T(8,128)(2,1)S(1)}, bf16[288,128]{1,0:T(8,128)(2,1)S(1)}, u32[]{:S(2)}, u32[]{:S(2)}) collective-permute-start(bf16[288,128]{1,0:T(8,128)(2,1)S(1)} %other_pair_sums.1), channel_id=1, source_target_pairs={{0,1},{1,0},{2,3},{3,2},{4,5},{5,4},{6,7},{7,6},{8,9},{9,8},{10,11... | collective-permute-start | bytes 221192 | tf_op jit(solution)/shard_map/ppermute | solution.py:343

commit v4 on v3

--- a/solution.py
+++ b/solution.py
@@ -169,12 +169,19 @@
             store(first, part * (lane == a).astype(jnp.bfloat16))
 
 
+def keep_kernel(right_ref, w_ref, b_ref, right_out, w_out, b_out):
+    hidden = 32
+    right_out[...] = right_ref[...]
+    b_out[...] = b_ref[...]
+    for c in range(hidden):
+        block = w_ref[c * hidden : (c + 1) * hidden, :]
+        for a in range(128 // hidden):
+            w_out[c * 128 + a * hidden : c * 128 + (a + 1) * hidden, :] = block
+
+
 def pair_kernel(
-    own, l0, l1, r0, r1, r2, r3, w_ref, b_hbm, out_ref, ls_ref, rs_ref, big_ref, b_ref, b_sem
+    own, l0, l1, r0, r1, r2, r3, w_ref, b_ref, out_ref, ls_ref, rs_ref, big_ref
 ):
-    if own:
-        bias_copy = pltpu.make_async_copy(b_hbm, b_ref, b_sem)
-        bias_copy.start()
     body = l0.shape[0] - MASK_ROWS
     hidden = 32
     residues = body // hidden
@@ -204,14 +211,9 @@
             big_ref[first : first + 2 * residues, c * 128 : (c + 1) * 128] = value
 
         expand(tile, store, hidden)
-    weight = jnp.concatenate(
-        [w_ref[c * hidden : (c + 1) * hidden, :] for c in range(hidden) for _ in range(128 // hidden)],
-        axis=0,
-    )
     pairs = 4 * residues * residues
-    projected = jnp.dot(big_ref[...], weight, preferred_element_type=jnp.float32)
+    projected = jnp.dot(big_ref[...], w_ref[...], preferred_element_type=jnp.float32)
     if own:
-        bias_copy.wait()
         projected = projected + b_ref[...]
     out_ref[:pairs, :] = projected.astype(out_ref.dtype)
     out_ref[pairs:, :] = counts.astype(out_ref.dtype)
@@ -316,28 +318,39 @@
     first = lax.ppermute(left, GROUP, route(lambda r, c, q: (2 * c + r // 2, r % 2, q)))
     passed = lax.ppermute(far, GROUP, route(lambda r, c, q: (r ^ 1, c, q)))
     second = lax.ppermute(first, GROUP, route(lambda r, c, q: (r, 1 - c, q)))
-    rights = [right, near, far, passed]
+    kept, weight, bias = pl.pallas_call(
+        keep_kernel,
+        out_shape=(
+            payload,
+            jax.ShapeDtypeStruct((hidden * 128, width), jnp.bfloat16),
+            jax.ShapeDtypeStruct((1, width), jnp.float32),
+        ),
+        in_specs=[vmem] * 3,
+        out_specs=(vmem,) * 3,
+        compiler_params=pltpu.CompilerParams(vmem_limit_bytes=16 * 1024 * 1024),
+        cost_estimate=pl.CostEstimate(flops=0, bytes_accessed=1 << 22, transcendentals=0),
+        name="keep",
+    )(right, closing_linear_map, closing_linear_constant.reshape(1, width))
+    rights = [kept, near, far, passed]
     lefts = [first, second]
 
     def pair_sums(own, kind):
         return pl.pallas_call(
             lambda *refs: pair_kernel(own, *refs),
             out_shape=jax.ShapeDtypeStruct((pairs + 2 * MASK_ROWS, width), kind),
-            in_specs=[vmem] * 7 + [in_hbm],
+            in_specs=[vmem] * 8,
             out_specs=vmem,
             scratch_shapes=[
                 pltpu.VMEM((2, rows, sequences), jnp.bfloat16),
                 pltpu.VMEM((4, rows, sequences), jnp.bfloat16),
                 pltpu.VMEM((pairs, hidden * 128), jnp.bfloat16),
-                pltpu.VMEM((1, width), jnp.float32),
-                pltpu.SemaphoreType.DMA,
             ],
             compiler_params=pltpu.CompilerParams(vmem_limit_bytes=24 * 1024 * 1024),
             cost_estimate=pl.CostEstimate(
                 flops=2 * pairs * hidden * 128 * width, bytes_accessed=1 << 20, transcendentals=0
             ),
             name="own_pair_sums" if own else "other_pair_sums",
-        )(*lefts, *rights, closing_linear_map, closing_linear_constant.reshape(1, width))
+        )(*lefts, *rights, weight, bias)
 
     theirs = pair_sums(False, jnp.bfloat16)
     received = lax.ppermute(theirs, GROUP, route(lambda r, c, q: (r, c, 1 - q)))

time: 26.3 us -> 25 us (0.951)
  waiting for transfers between devices: 2.35 us -> 1.3 us
    ppermute x1, waiting for transfers between devices: 1.97 us -> 1.29 us  [direct_shards(): passed = lax.ppermute(far, GROUP, route(lambda r, c, q: (r ^ 1, c, q)))]
    ppermute x1, waiting for transfers between devices: 0.36 us -> 0.01 us  [direct_shards(): second = lax.ppermute(first, GROUP, route(lambda r, c, q: (r, 1 - c, q)))]
    pallas_call x2, Pallas kernels: 3.16 us -> 2.81 us  [pair_sums(): pl.pallas_call(lambda *refs: pair_kernel(own, *refs), out_shape=jax.Shape...]
  transfers between devices with their start and end apart: 6 -> 6, of which waited for: 2 -> 1; matrix products, arithmetic and copies ran while one was open for 0% -> 0% of each run, Pallas kernels for 7% -> 6%
where the time goes in v4:
time: 25 us; the launch traced here: 24.8 us
  starting transfers between devices  15.1 us (60%)
  Pallas kernels  7.42 us (30%)
  waiting for transfers between devices  1.3 us (5%)
  local copies, waits for them, and re-layouts  0.89 us (4%)
    ppermute x1, starting transfers between devices, direct_shards(): received = lax.ppermute(theirs, GROUP, route(lambda r, c, q: (r, c, 1 - q)))  4.64 us
    ppermute x1, starting transfers between devices, direct_shards(): far = lax.ppermute(right, GROUP, route(lambda r, c, q: (r ^ 2, c, q)))  3.76 us
    pallas_call x1, Pallas kernels, direct_shards(): pl.pallas_call(project_kernel, out_shape=(payload, payload), in_specs=[in...  3.5 us
    pallas_call x2, Pallas kernels, pair_sums(): pl.pallas_call(lambda *refs: pair_kernel(own, *refs), out_shape=jax.Shape...  2.81 us
    ppermute x1, starting transfers between devices, direct_shards(): passed = lax.ppermute(far, GROUP, route(lambda r, c, q: (r ^ 1, c, q)))  2.3 us
    ppermute x1, starting transfers between devices, direct_shards(): near = lax.ppermute(right, GROUP, route(lambda r, c, q: (r ^ 1, c, q)))  2.11 us
    ppermute x1, starting transfers between devices, direct_shards(): lax.ppermute(left, GROUP, route(lambda r, c, q: (2 * c + r // 2, r % 2, q)))  1.54 us
    ppermute x1, waiting for transfers between devices, direct_shards(): passed = lax.ppermute(far, GROUP, route(lambda r, c, q: (r ^ 1, c, q)))  1.29 us
  transfers between devices with their start and end apart: 6, of which 1 were waited for; matrix products, arithmetic and copies ran while one was open for 0% of the time, Pallas kernels for 6%

profile of v4, /device:TPU:1, one launch (start us, length us, event | category | flops | bytes accessed | tf_op | source)
XLA Modules:
  0.0 24.8 jit_solution(4351666485985413715)
XLA Ops:
  0.0 0.0 copy-start
  0.0 3.5 %normalize_and_project.1 = (bf16[272,128]{1,0:T(8,128)(2,1)}, bf16[272,128]{1,0:T(8,128)(2,1)}) custom-call(s32[8]{0:T(128)} %pept_hbm.1, bf16[1024,256]{1,0:T(8,128)(2,1)} %bitcast.10, s32[8,128]{1,0:T(8,128)} %bitcast.13, f32[1,256]{1,0:T(1,128)} %bitcast.14, f32[1,256]{1,0:T(1,128)} %bitcast.15, bf16[32,256]{1,0:T(8,128)(2,1)} %bitcast.11, ...), custom_call_target="tpu_custom_call" | custom-call | tf_op jit(solution)/shard_map/normalize_and_project/pallas_call | solution.py:283
  3.5 1.5 %collective-permute-start = (bf16[272,128]{1,0:T(8,128)(2,1)}, bf16[272,128]{1,0:T(8,128)(2,1)S(1)}, u32[]{:S(2)}, u32[]{:S(2)}) collective-permute-start(bf16[272,128]{1,0:T(8,128)(2,1)} %get-tuple-element.10), channel_id=1, source_target_pairs={{0,0},{1,1},{2,8},{3,9},{4,2},{5,3},{6,10},{7,11},{8,4},{9,5},{10,... | collective-permute-start | bytes 208904 | tf_op jit(solution)/shard_map/ppermute | solution.py:318
  5.1 0.0 copy-start.2
  5.1 3.8 %collective-permute-start.3 = (bf16[272,128]{1,0:T(8,128)(2,1)}, bf16[272,128]{1,0:T(8,128)(2,1)S(1)}, u32[]{:S(2)}, u32[]{:S(2)}) collective-permute-start(bf16[272,128]{1,0:T(8,128)(2,1)} %get-tuple-element.11.right_ref), channel_id=1, source_target_pairs={{0,8},{1,9},{2,10},{3,11},{4,12},{5,13},{6,14},{7,15},{8,0},{9,1},... | collective-permute-start | bytes 208904 | tf_op jit(solution)/shard_map/ppermute | solution.py:316
  8.8 2.1 %collective-permute-start.2 = (bf16[272,128]{1,0:T(8,128)(2,1)}, bf16[272,128]{1,0:T(8,128)(2,1)S(1)}, u32[]{:S(2)}, u32[]{:S(2)}) collective-permute-start(bf16[272,128]{1,0:T(8,128)(2,1)} %get-tuple-element.11.right_ref), channel_id=1, source_target_pairs={{0,4},{1,5},{2,6},{3,7},{4,0},{5,1},{6,2},{7,3},{8,12},{9,13},{10,... | collective-permute-start | bytes 208904 | tf_op jit(solution)/shard_map/ppermute | solution.py:317
  10.9 0.0 collective-permute-done.refs_0_
  10.9 0.8 %collective-permute-start.1 = (bf16[272,128]{1,0:T(8,128)(2,1)S(1)}, bf16[272,128]{1,0:T(8,128)(2,1)S(1)}, u32[]{:S(2)}, u32[]{:S(2)}) collective-permute-start(bf16[272,128]{1,0:T(8,128)(2,1)S(1)} %collective-permute-done.refs_0_), channel_id=1, source_target_pairs={{0,2},{1,3},{2,0},{3,1},{4,6},{5,7},{6,4},{7,5},{8,10},{9,11},{10,... | collective-permute-start | bytes 208904 | tf_op jit(solution)/shard_map/ppermute | solution.py:320
  11.7 0.0 collective-permute-done.3.refs_4_
  11.7 2.3 %collective-permute-start.4 = (bf16[272,128]{1,0:T(8,128)(2,1)S(1)}, bf16[272,128]{1,0:T(8,128)(2,1)S(1)}, u32[]{:S(2)}, u32[]{:S(2)}) collective-permute-start(bf16[272,128]{1,0:T(8,128)(2,1)S(1)} %collective-permute-done.3.refs_4_), channel_id=1, source_target_pairs={{0,4},{1,5},{2,6},{3,7},{4,0},{5,1},{6,2},{7,3},{8,12},{9,13},{10,... | collective-permute-start | bytes 208904 | tf_op jit(solution)/shard_map/ppermute | solution.py:319
  14.0 0.0 copy-done
  14.0 0.0 copy-done.2
  14.0 0.0 copy-start.1
  14.0 0.9 %copy-done.1 = bf16[272,128]{1,0:T(8,128)(2,1)S(1)} copy-done((bf16[272,128]{1,0:T(8,128)(2,1)S(1)}, bf16[272,128]{1,0:T(8,128)(2,1)}, u32[]{:S(2)}) %copy-start.1) | copy-done | bytes 69656
  14.9 0.1 keep.1
  15.0 0.0 collective-permute-done.2.refs_3_
  15.1 0.0 collective-permute-done.1.refs_1_
  15.1 1.3 %collective-permute-done.4.refs_5_ = bf16[272,128]{1,0:T(8,128)(2,1)S(1)} collective-permute-done((bf16[272,128]{1,0:T(8,128)(2,1)S(1)}, bf16[272,128]{1,0:T(8,128)(2,1)S(1)}, u32[]{:S(2)}, u32[]{:S(2)}) %collective-permute-start.4) | collective-permute-done | bytes 69664 | tf_op jit(solution)/shard_map/ppermute | solution.py:319
  16.4 1.4 %other_pair_sums.1 = bf16[288,128]{1,0:T(8,128)(2,1)S(1)} custom-call(bf16[272,128]{1,0:T(8,128)(2,1)S(1)} %collective-permute-done.refs_0_, bf16[272,128]{1,0:T(8,128)(2,1)S(1)} %collective-permute-done.1.refs_1_, bf16[272,128]{1,0:T(8,128)(2,1)S(1)} %get-tuple-element.12.refs_2_, bf16[272,128]{1,0:T(8,128)(2,1)S(1)} %collective-permute-done.2.refs_3_, ...), custom_call_target="tpu_custom_call" | custom-call | flops 268435456 | bytes 1048576 | tf_op jit(solution)/shard_map/other_pair_sums/pallas_call | solution.py:338
  17.8 4.6 %collective-permute-start.5 = (bf16[288,128]{1,0:T(8,128)(2,1)S(1)}, bf16[288,128]{1,0:T(8,128)(2,1)S(1)}, u32[]{:S(2)}, u32[]{:S(2)}) collective-permute-start(bf16[288,128]{1,0:T(8,128)(2,1)S(1)} %other_pair_sums.1), channel_id=1, source_target_pairs={{0,1},{1,0},{2,3},{3,2},{4,5},{5,4},{6,7},{7,6},{8,9},{9,8},{10,11... | collective-permute-start | bytes 221192 | tf_op jit(solution)/shard_map/ppermute | solution.py:356
  22.4 1.4 %own_pair_sums.1.mine_ref = f32[288,128]{1,0:T(8,128)S(1)} custom-call(bf16[272,128]{1,0:T(8,128)(2,1)S(1)} %collective-permute-done.refs_0_, bf16[272,128]{1,0:T(8,128)(2,1)S(1)} %collective-permute-done.1.refs_1_, bf16[272,128]{1,0:T(8,128)(2,1)S(1)} %get-tuple-element.12.refs_2_, bf16[272,128]{1,0:T(8,128)(2,1)S(1)} %collective-permute-done.2.refs_3_, ...), custom_call_target="tpu_custom_call" | custom-call | flops 268435456 | bytes 1048576 | tf_op jit(solution)/shard_map/own_pair_sums/pallas_call | solution.py:338
  23.8 0.0 collective-permute-done.5.other_ref
  23.8 1.0 %divide.1 = bf16[16,16,128]{2,1,0:T(8,128)(2,1)} custom-call(f32[288,128]{1,0:T(8,128)S(1)} %own_pair_sums.1.mine_ref, bf16[288,128]{1,0:T(8,128)(2,1)S(1)} %collective-permute-done.5.other_ref), custom_call_target="tpu_custom_call" | custom-call | tf_op jit(solution)/shard_map/divide/pallas_call | solution.py:358
Async XLA Ops:
  0.0 14.0 %copy-start = (bf16[1024,128]{1,0:T(8,128)(2,1)S(1)}, bf16[1024,128]{1,0:T(8,128)(2,1)}, u32[]{:S(2)}) copy-start(bf16[1024,128]{1,0:T(8,128)(2,1)} %w_ref.1) | copy-start | bytes 786436
  3.5 7.4 %collective-permute-start = (bf16[272,128]{1,0:T(8,128)(2,1)}, bf16[272,128]{1,0:T(8,128)(2,1)S(1)}, u32[]{:S(2)}, u32[]{:S(2)}) collective-permute-start(bf16[272,128]{1,0:T(8,128)(2,1)} %get-tuple-element.10), channel_id=1, source_target_pairs={{0,0},{1,1},{2,8},{3,9},{4,2},{5,3},{6,10},{7,11},{8,4},{9,5},{10,... | collective-permute-start | bytes 208904 | tf_op jit(solution)/shard_map/ppermute | solution.py:318
  5.1 9.0 %copy-start.2 = (f32[128]{0:T(128)S(1)}, f32[128]{0:T(128)}, u32[]{:S(2)}) copy-start(f32[128]{0:T(128)} %param.21) | copy-start | bytes 1540
  5.1 6.7 %collective-permute-start.3 = (bf16[272,128]{1,0:T(8,128)(2,1)}, bf16[272,128]{1,0:T(8,128)(2,1)S(1)}, u32[]{:S(2)}, u32[]{:S(2)}) collective-permute-start(bf16[272,128]{1,0:T(8,128)(2,1)} %get-tuple-element.11.right_ref), channel_id=1, source_target_pairs={{0,8},{1,9},{2,10},{3,11},{4,12},{5,13},{6,14},{7,15},{8,0},{9,1},... | collective-permute-start | bytes 208904 | tf_op jit(solution)/shard_map/ppermute | solution.py:316
  8.8 6.2 %collective-permute-start.2 = (bf16[272,128]{1,0:T(8,128)(2,1)}, bf16[272,128]{1,0:T(8,128)(2,1)S(1)}, u32[]{:S(2)}, u32[]{:S(2)}) collective-permute-start(bf16[272,128]{1,0:T(8,128)(2,1)} %get-tuple-element.11.right_ref), channel_id=1, source_target_pairs={{0,4},{1,5},{2,6},{3,7},{4,0},{5,1},{6,2},{7,3},{8,12},{9,13},{10,... | collective-permute-start | bytes 208904 | tf_op jit(solution)/shard_map/ppermute | solution.py:317
  10.9 4.1 %collective-permute-start.1 = (bf16[272,128]{1,0:T(8,128)(2,1)S(1)}, bf16[272,128]{1,0:T(8,128)(2,1)S(1)}, u32[]{:S(2)}, u32[]{:S(2)}) collective-permute-start(bf16[272,128]{1,0:T(8,128)(2,1)S(1)} %collective-permute-done.refs_0_), channel_id=1, source_target_pairs={{0,2},{1,3},{2,0},{3,1},{4,6},{5,7},{6,4},{7,5},{8,10},{9,11},{10,... | collective-permute-start | bytes 208904 | tf_op jit(solution)/shard_map/ppermute | solution.py:320
  11.7 4.6 %collective-permute-start.4 = (bf16[272,128]{1,0:T(8,128)(2,1)S(1)}, bf16[272,128]{1,0:T(8,128)(2,1)S(1)}, u32[]{:S(2)}, u32[]{:S(2)}) collective-permute-start(bf16[272,128]{1,0:T(8,128)(2,1)S(1)} %collective-permute-done.3.refs_4_), channel_id=1, source_target_pairs={{0,4},{1,5},{2,6},{3,7},{4,0},{5,1},{6,2},{7,3},{8,12},{9,13},{10,... | collective-permute-start | bytes 208904 | tf_op jit(solution)/shard_map/ppermute | solution.py:319
  14.0 0.9 %copy-start.1 = (bf16[272,128]{1,0:T(8,128)(2,1)S(1)}, bf16[272,128]{1,0:T(8,128)(2,1)}, u32[]{:S(2)}) copy-start(bf16[272,128]{1,0:T(8,128)(2,1)} %get-tuple-element.11.right_ref) | copy-start | bytes 208900
  17.8 6.1 %collective-permute-start.5 = (bf16[288,128]{1,0:T(8,128)(2,1)S(1)}, bf16[288,128]{1,0:T(8,128)(2,1)S(1)}, u32[]{:S(2)}, u32[]{:S(2)}) collective-permute-start(bf16[288,128]{1,0:T(8,128)(2,1)S(1)} %other_pair_sums.1), channel_id=1, source_target_pairs={{0,1},{1,0},{2,3},{3,2},{4,5},{5,4},{6,7},{7,6},{8,9},{9,8},{10,11... | collective-permute-start | bytes 221192 | tf_op jit(solution)/shard_map/ppermute | solution.py:356

commit v5 on v4

--- a/solution.py
+++ b/solution.py
@@ -151,11 +151,15 @@
         live = (occ_ref[i : i + 1, :] * pept_ref[i]).astype(jnp.float32)
         part = y_ref[pl.ds(i, sequences, stride=residues), :].T[: 2 * hidden] * live
         l_ref[pl.ds(i, hidden, stride=residues), :] = part[:hidden]
-        right_ref[i * hidden : (i + 1) * hidden, :] = part[hidden:].astype(jnp.bfloat16)
+        mine = part[hidden:].astype(jnp.bfloat16)
+        for n in range(right_ref.shape[0]):
+            right_ref[n, i * hidden : (i + 1) * hidden, :] = mine
         l_ref[hidden * residues + i : hidden * residues + i + 1, :] = live
     l_ref[hidden * residues + residues :, :] = jnp.zeros((MASK_ROWS - residues, sequences), jnp.float32)
     left_ref[...] = l_ref[...].astype(jnp.bfloat16)
-    right_ref[hidden * residues :, :] = l_ref[hidden * residues :, :].astype(jnp.bfloat16)
+    masks = l_ref[hidden * residues :, :].astype(jnp.bfloat16)
+    for n in range(right_ref.shape[0]):
+        right_ref[n, hidden * residues :, :] = masks
 
 
 def expand(tile, store, hidden):
@@ -169,9 +173,8 @@
             store(first, part * (lane == a).astype(jnp.bfloat16))
 
 
-def keep_kernel(right_ref, w_ref, b_ref, right_out, w_out, b_out):
+def keep_kernel(w_ref, b_ref, w_out, b_out):
     hidden = 32
-    right_out[...] = right_ref[...]
     b_out[...] = b_ref[...]
     for c in range(hidden):
         block = w_ref[c * hidden : (c + 1) * hidden, :]
@@ -180,16 +183,14 @@
 
 
 def pair_kernel(
-    own, l0, l1, r0, r1, r2, r3, w_ref, b_ref, out_ref, ls_ref, rs_ref, big_ref
+    own, l0, l1, rs_ref, w_ref, b_ref, out_ref, ls_ref, big_ref
 ):
     body = l0.shape[0] - MASK_ROWS
     hidden = 32
     residues = body // hidden
-    row, col, seq = (lax.axis_index(name) for name in GROUP)
+    col, seq = lax.axis_index("col"), lax.axis_index("seq")
     for k, piece in enumerate((l0, l1)):
         ls_ref[col ^ k] = piece[...]
-    for k, piece in enumerate((r0, r1, r2, r3)):
-        rs_ref[row ^ k] = piece[...]
     half = 2 * (seq if own else 1 - seq)
 
     def rows(ref, at, first, last):
@@ -278,11 +279,12 @@
     rows = residues * hidden + MASK_ROWS
     pairs = 4 * residues * residues
     payload = jax.ShapeDtypeStruct((rows, sequences), jnp.bfloat16)
+    payloads = jax.ShapeDtypeStruct((lax.axis_size("row"), rows, sequences), jnp.bfloat16)
     vmem = pl.BlockSpec(memory_space=pltpu.VMEM)
     in_hbm = pl.BlockSpec(memory_space=pltpu.HBM)
     left, right = pl.pallas_call(
         project_kernel,
-        out_shape=(payload, payload),
+        out_shape=(payload, payloads),
         in_specs=[in_hbm] * 9,
         out_specs=(vmem, vmem),
         scratch_shapes=[
@@ -313,36 +315,31 @@
         rhs_linear_map.T,
         rhs_linear_constant.reshape(1, hidden),
     )
-    far = lax.ppermute(right, GROUP, route(lambda r, c, q: (r ^ 2, c, q)))
-    near = lax.ppermute(right, GROUP, route(lambda r, c, q: (r ^ 1, c, q)))
+    rights = lax.all_to_all(right, "row", 0, 0)
     first = lax.ppermute(left, GROUP, route(lambda r, c, q: (2 * c + r // 2, r % 2, q)))
-    passed = lax.ppermute(far, GROUP, route(lambda r, c, q: (r ^ 1, c, q)))
     second = lax.ppermute(first, GROUP, route(lambda r, c, q: (r, 1 - c, q)))
-    kept, weight, bias = pl.pallas_call(
+    weight, bias = pl.pallas_call(
         keep_kernel,
         out_shape=(
-            payload,
             jax.ShapeDtypeStruct((hidden * 128, width), jnp.bfloat16),
             jax.ShapeDtypeStruct((1, width), jnp.float32),
         ),
-        in_specs=[vmem] * 3,
-        out_specs=(vmem,) * 3,
+        in_specs=[vmem] * 2,
+        out_specs=(vmem,) * 2,
         compiler_params=pltpu.CompilerParams(vmem_limit_bytes=16 * 1024 * 1024),
         cost_estimate=pl.CostEstimate(flops=0, bytes_accessed=1 << 22, transcendentals=0),
         name="keep",
-    )(right, closing_linear_map, closing_linear_constant.reshape(1, width))
-    rights = [kept, near, far, passed]
+    )(closing_linear_map, closing_linear_constant.reshape(1, width))
     lefts = [first, second]
 
     def pair_sums(own, kind):
         return pl.pallas_call(
             lambda *refs: pair_kernel(own, *refs),
             out_shape=jax.ShapeDtypeStruct((pairs + 2 * MASK_ROWS, width), kind),
-            in_specs=[vmem] * 8,
+            in_specs=[vmem] * 5,
             out_specs=vmem,
             scratch_shapes=[
                 pltpu.VMEM((2, rows, sequences), jnp.bfloat16),
-                pltpu.VMEM((4, rows, sequences), jnp.bfloat16),
                 pltpu.VMEM((pairs, hidden * 128), jnp.bfloat16),
             ],
             compiler_params=pltpu.CompilerParams(vmem_limit_bytes=24 * 1024 * 1024),
@@ -350,7 +347,7 @@
                 flops=2 * pairs * hidden * 128 * width, bytes_accessed=1 << 20, transcendentals=0
             ),
             name="own_pair_sums" if own else "other_pair_sums",
-        )(*lefts, *rights, weight, bias)
+        )(*lefts, rights, weight, bias)
 
     theirs = pair_sums(False, jnp.bfloat16)
     received = lax.ppermute(theirs, GROUP, route(lambda r, c, q: (r, c, 1 - q)))

time: 25 us -> 28.9 us (1.16)
  the two profiles are of different devices: /device:TPU:1 before, /device:TPU:9 now
where the time goes in v5:
time: 28.9 us; the launch traced here: 28.6 us
  starting transfers between devices  10.8 us (37%)
  waiting for transfers between devices  10.3 us (36%)
  Pallas kernels  7.41 us (26%)
    ppermute x1, waiting for transfers between devices, direct_shards(): lax.ppermute(left, GROUP, route(lambda r, c, q: (2 * c + r // 2, r % 2, q)))  7.31 us
    all_to_all x1, starting transfers between devices, direct_shards(): rights = lax.all_to_all(right, 'row', 0, 0)  4.9 us
    pallas_call x1, Pallas kernels, direct_shards(): pl.pallas_call(project_kernel, out_shape=(payload, payloads), in_specs=[i...  3.55 us
    ppermute x1, waiting for transfers between devices, direct_shards(): second = lax.ppermute(first, GROUP, route(lambda r, c, q: (r, 1 - c, q)))  3 us
    ppermute x1, starting transfers between devices, direct_shards(): lax.ppermute(left, GROUP, route(lambda r, c, q: (2 * c + r // 2, r % 2, q)))  2.96 us
    ppermute x1, starting transfers between devices, direct_shards(): received = lax.ppermute(theirs, GROUP, route(lambda r, c, q: (r, c, 1 - q)))  2.95 us
    pallas_call x2, Pallas kernels, pair_sums(): pl.pallas_call(lambda *refs: pair_kernel(own, *refs), out_shape=jax.Shape...  2.76 us
    pallas_call x1, Pallas kernels, direct_shards(): pl.pallas_call(finish_kernel, out_shape=jax.ShapeDtypeStruct((2 * residue...  0.97 us
  transfers between devices with their start and end apart: 4, of which 2 were waited for; matrix products, arithmetic and copies ran while one was open for 0% of the time, Pallas kernels for 5%

profile of v5, /device:TPU:9, one launch (start us, length us, event | category | flops | bytes accessed | tf_op | source)
XLA Modules:
  0.0 28.6 jit_solution(6916751247348563241)
XLA Ops:
  0.0 3.6 %normalize_and_project.1 = (bf16[272,128]{1,0:T(8,128)(2,1)}, bf16[4,272,128]{2,1,0:T(8,128)(2,1)}) custom-call(s32[8]{0:T(128)} %pept_hbm.1, bf16[1024,256]{1,0:T(8,128)(2,1)} %bitcast.10, s32[8,128]{1,0:T(8,128)} %bitcast.13, f32[1,256]{1,0:T(1,128)} %bitcast.14, f32[1,256]{1,0:T(1,128)} %bitcast.15, bf16[32,256]{1,0:T(8,128)(2,1)} %bitcast.11, ...), custom_call_target="tpu_custom_call" | custom-call | tf_op jit(solution)/shard_map/normalize_and_project/pallas_call | solution.py:285
  3.6 0.0 copy-start.2
  3.6 0.0 copy-start
  3.6 4.9 %all-to-all-start = ((bf16[4,272,128]{2,1,0:T(8,128)(2,1)}), bf16[4,272,128]{2,1,0:T(8,128)(2,1)S(1)}, u32[]{:S(2)}, u32[]{:S(2)}) async-start(bf16[4,272,128]{2,1,0:T(8,128)(2,1)} %get-tuple-element.10), calls=%async_computation | async-start | bytes 557056 | tf_op jit(solution)/shard_map/all_to_all | solution.py:318
  8.5 0.0 copy-done.2
  8.5 0.0 copy-start.1
  8.5 3.0 %collective-permute-start = (bf16[272,128]{1,0:T(8,128)(2,1)S(1)}, bf16[272,128]{1,0:T(8,128)(2,1)S(1)}, u32[]{:S(2)}, u32[]{:S(2)}) collective-permute-start(bf16[272,128]{1,0:T(8,128)(2,1)S(1)} %copy-done.2), channel_id=1, source_target_pairs={{0,0},{1,1},{2,8},{3,9},{4,2},{5,3},{6,10},{7,11},{8,4},{9,5},{10,... | collective-permute-start | bytes 208904 | tf_op jit(solution)/shard_map/ppermute | solution.py:319
  11.5 7.3 %collective-permute-done.refs_0_ = bf16[272,128]{1,0:T(8,128)(2,1)S(1)} collective-permute-done((bf16[272,128]{1,0:T(8,128)(2,1)S(1)}, bf16[272,128]{1,0:T(8,128)(2,1)S(1)}, u32[]{:S(2)}, u32[]{:S(2)}) %collective-permute-start) | collective-permute-done | bytes 69664 | tf_op jit(solution)/shard_map/ppermute | solution.py:319
  18.8 0.0 collective-permute-start.1
  18.8 0.0 copy-done
  18.8 0.0 copy-done.1
  18.8 0.1 keep.1
  18.9 3.0 %collective-permute-done.1.refs_1_ = bf16[272,128]{1,0:T(8,128)(2,1)S(1)} collective-permute-done((bf16[272,128]{1,0:T(8,128)(2,1)S(1)}, bf16[272,128]{1,0:T(8,128)(2,1)S(1)}, u32[]{:S(2)}, u32[]{:S(2)}) %collective-permute-start.1) | collective-permute-done | bytes 69664 | tf_op jit(solution)/shard_map/ppermute | solution.py:320
  21.9 0.0 all-to-all-done.refs_2_
  21.9 1.4 %other_pair_sums.1 = bf16[288,128]{1,0:T(8,128)(2,1)S(1)} custom-call(bf16[272,128]{1,0:T(8,128)(2,1)S(1)} %collective-permute-done.refs_0_, bf16[272,128]{1,0:T(8,128)(2,1)S(1)} %collective-permute-done.1.refs_1_, bf16[4,272,128]{2,1,0:T(8,128)(2,1)S(1)} %all-to-all-done.refs_2_, bf16[4096,128]{1,0:T(8,128)(2,1)S(1)} %get-tuple-element.11.refs_3_, ...), custom_call_target="tpu_custom_call" | custom-call | flops 268435456 | bytes 1048576 | tf_op jit(solution)/shard_map/other_pair_sums/pallas_call | solution.py:336
  23.3 2.9 %collective-permute-start.2 = (bf16[288,128]{1,0:T(8,128)(2,1)S(1)}, bf16[288,128]{1,0:T(8,128)(2,1)S(1)}, u32[]{:S(2)}, u32[]{:S(2)}) collective-permute-start(bf16[288,128]{1,0:T(8,128)(2,1)S(1)} %other_pair_sums.1), channel_id=1, source_target_pairs={{0,1},{1,0},{2,3},{3,2},{4,5},{5,4},{6,7},{7,6},{8,9},{9,8},{10,11... | collective-permute-start | bytes 221192 | tf_op jit(solution)/shard_map/ppermute | solution.py:353
  26.3 1.4 %own_pair_sums.1.mine_ref = f32[288,128]{1,0:T(8,128)S(1)} custom-call(bf16[272,128]{1,0:T(8,128)(2,1)S(1)} %collective-permute-done.refs_0_, bf16[272,128]{1,0:T(8,128)(2,1)S(1)} %collective-permute-done.1.refs_1_, bf16[4,272,128]{2,1,0:T(8,128)(2,1)S(1)} %all-to-all-done.refs_2_, bf16[4096,128]{1,0:T(8,128)(2,1)S(1)} %get-tuple-element.11.refs_3_, ...), custom_call_target="tpu_custom_call" | custom-call | flops 268435456 | bytes 1048576 | tf_op jit(solution)/shard_map/own_pair_sums/pallas_call | solution.py:336
  27.6 0.0 collective-permute-done.2.other_ref
  27.7 1.0 %divide.1 = bf16[16,16,128]{2,1,0:T(8,128)(2,1)} custom-call(f32[288,128]{1,0:T(8,128)S(1)} %own_pair_sums.1.mine_ref, bf16[288,128]{1,0:T(8,128)(2,1)S(1)} %collective-permute-done.2.other_ref), custom_call_target="tpu_custom_call" | custom-call | tf_op jit(solution)/shard_map/divide/pallas_call | solution.py:355
Async XLA Ops:
  3.6 4.9 %copy-start.2 = (bf16[272,128]{1,0:T(8,128)(2,1)S(1)}, bf16[272,128]{1,0:T(8,128)(2,1)}, u32[]{:S(2)}) copy-start(bf16[272,128]{1,0:T(8,128)(2,1)} %get-tuple-element.9) | copy-start | bytes 208900
  3.6 15.2 %copy-start = (bf16[1024,128]{1,0:T(8,128)(2,1)S(1)}, bf16[1024,128]{1,0:T(8,128)(2,1)}, u32[]{:S(2)}) copy-start(bf16[1024,128]{1,0:T(8,128)(2,1)} %w_ref.1) | copy-start | bytes 786436
  3.6 18.3 %all-to-all-start = ((bf16[4,272,128]{2,1,0:T(8,128)(2,1)}), bf16[4,272,128]{2,1,0:T(8,128)(2,1)S(1)}, u32[]{:S(2)}, u32[]{:S(2)}) async-start(bf16[4,272,128]{2,1,0:T(8,128)(2,1)} %get-tuple-element.10), calls=%async_computation | async-start | bytes 557056 | tf_op jit(solution)/shard_map/all_to_all | solution.py:318
  8.5 10.3 %copy-start.1 = (f32[128]{0:T(128)S(1)}, f32[128]{0:T(128)}, u32[]{:S(2)}) copy-start(f32[128]{0:T(128)} %param.21) | copy-start | bytes 1540
  8.5 10.3 %collective-permute-start = (bf16[272,128]{1,0:T(8,128)(2,1)S(1)}, bf16[272,128]{1,0:T(8,128)(2,1)S(1)}, u32[]{:S(2)}, u32[]{:S(2)}) collective-permute-start(bf16[272,128]{1,0:T(8,128)(2,1)S(1)} %copy-done.2), channel_id=1, source_target_pairs={{0,0},{1,1},{2,8},{3,9},{4,2},{5,3},{6,10},{7,11},{8,4},{9,5},{10,... | collective-permute-start | bytes 208904 | tf_op jit(solution)/shard_map/ppermute | solution.py:319
  18.8 3.2 %collective-permute-start.1 = (bf16[272,128]{1,0:T(8,128)(2,1)S(1)}, bf16[272,128]{1,0:T(8,128)(2,1)S(1)}, u32[]{:S(2)}, u32[]{:S(2)}) collective-permute-start(bf16[272,128]{1,0:T(8,128)(2,1)S(1)} %collective-permute-done.refs_0_), channel_id=1, source_target_pairs={{0,2},{1,3},{2,0},{3,1},{4,6},{5,7},{6,4},{7,5},{8,10},{9,11},{10,... | collective-permute-start | bytes 208904 | tf_op jit(solution)/shard_map/ppermute | solution.py:320
  23.3 4.3 %collective-permute-start.2 = (bf16[288,128]{1,0:T(8,128)(2,1)S(1)}, bf16[288,128]{1,0:T(8,128)(2,1)S(1)}, u32[]{:S(2)}, u32[]{:S(2)}) collective-permute-start(bf16[288,128]{1,0:T(8,128)(2,1)S(1)} %other_pair_sums.1), channel_id=1, source_target_pairs={{0,1},{1,0},{2,3},{3,2},{4,5},{5,4},{6,7},{7,6},{8,9},{9,8},{10,11... | collective-permute-start | bytes 221192 | tf_op jit(solution)/shard_map/ppermute | solution.py:353

commit v6 on v4

--- a/solution.py
+++ b/solution.py
@@ -10,6 +10,7 @@
 GROUP = ("row", "col", "seq")
 NT = (((1,), (1,)), ((), ()))
 MASK_ROWS = 16
+WIDE = 2
 
 
 def from_root(x, axis, root):
@@ -108,7 +109,7 @@
 
 def project_kernel(
     pept_hbm, x_hbm, occ_hbm, gain_hbm, shift_hbm, wl_hbm, bl_hbm, wr_hbm, br_hbm,
-    left_ref, right_ref,
+    right_ref, left_ref,
     pept_ref, x_ref, occ_ref, gain_ref, shift_ref, wl_ref, bl_ref, wr_ref, br_ref,
     y_ref, l_ref, x_sems, sems,
 ):
@@ -158,29 +159,35 @@
     right_ref[hidden * residues :, :] = l_ref[hidden * residues :, :].astype(jnp.bfloat16)
 
 
-def expand(tile, store, hidden):
+def expand(tile, store, hidden, wide):
     rows, lanes = tile.shape
     per_vector = 128 // hidden
-    lane = lax.broadcasted_iota(jnp.int32, (rows, 128), 1) // hidden
+    lane = lax.broadcasted_iota(jnp.int32, (rows, 128), 1) // (hidden * wide)
     for g in range(lanes // 128):
         part = tile[:, g * 128 : (g + 1) * 128]
-        for a in range(per_vector):
-            first = (g * per_vector + a) * rows
+        for a in range(per_vector // wide):
+            first = (g * (per_vector // wide) + a) * rows
             store(first, part * (lane == a).astype(jnp.bfloat16))
 
 
-def keep_kernel(right_ref, w_ref, b_ref, right_out, w_out, b_out):
+def keep_kernel(right_ref, left_ref, w_ref, b_ref, right_out, left_out, w_out, b_out):
     hidden = 32
     right_out[...] = right_ref[...]
+    left_out[...] = left_ref[...]
     b_out[...] = b_ref[...]
+    width = b_ref.shape[1]
+    zero = jnp.zeros((hidden, width), jnp.bfloat16)
     for c in range(hidden):
         block = w_ref[c * hidden : (c + 1) * hidden, :]
         for a in range(128 // hidden):
-            w_out[c * 128 + a * hidden : c * 128 + (a + 1) * hidden, :] = block
+            for n in range(WIDE):
+                w_out[c * 128 + a * hidden : c * 128 + (a + 1) * hidden, n * width : (n + 1) * width] = (
+                    block if a % WIDE == n else zero
+                )
 
 
 def pair_kernel(
-    own, l0, l1, r0, r1, r2, r3, w_ref, b_ref, out_ref, ls_ref, rs_ref, big_ref
+    own, r2, r3, l0, l1, r1, r0, w_ref, b_ref, out_ref, ls_ref, rs_ref, big_ref
 ):
     body = l0.shape[0] - MASK_ROWS
     hidden = 32
@@ -210,12 +217,18 @@
         def store(first, value, c=c):
             big_ref[first : first + 2 * residues, c * 128 : (c + 1) * 128] = value
 
-        expand(tile, store, hidden)
+        expand(tile, store, hidden, WIDE)
     pairs = 4 * residues * residues
     projected = jnp.dot(big_ref[...], w_ref[...], preferred_element_type=jnp.float32)
-    if own:
-        projected = projected + b_ref[...]
-    out_ref[:pairs, :] = projected.astype(out_ref.dtype)
+    width = b_ref.shape[1]
+    size = 2 * residues
+    for g in range(pairs // (size * WIDE)):
+        for n in range(WIDE):
+            part = projected[g * size : (g + 1) * size, n * width : (n + 1) * width]
+            if own:
+                part = part + b_ref[...]
+            first = (g * WIDE + n) * size
+            out_ref[first : first + size, :] = part.astype(out_ref.dtype)
     out_ref[pairs:, :] = counts.astype(out_ref.dtype)
 
 
@@ -240,7 +253,7 @@
     def store(first, value):
         big_ref[first : first + 2 * residues, :] = value
 
-    expand(tile, store, hidden)
+    expand(tile, store, hidden, 1)
     share = jnp.full((128, 128), 1.0 / hidden, jnp.bfloat16)
     divisor = jnp.dot(big_ref[...], share, preferred_element_type=jnp.float32)
     total = mine_ref[:pairs, :] + other_ref[:pairs, :].astype(jnp.float32)
@@ -280,7 +293,7 @@
     payload = jax.ShapeDtypeStruct((rows, sequences), jnp.bfloat16)
     vmem = pl.BlockSpec(memory_space=pltpu.VMEM)
     in_hbm = pl.BlockSpec(memory_space=pltpu.HBM)
-    left, right = pl.pallas_call(
+    right, left = pl.pallas_call(
         project_kernel,
         out_shape=(payload, payload),
         in_specs=[in_hbm] * 9,
@@ -313,26 +326,26 @@
         rhs_linear_map.T,
         rhs_linear_constant.reshape(1, hidden),
     )
-    far = lax.ppermute(right, GROUP, route(lambda r, c, q: (r ^ 2, c, q)))
-    near = lax.ppermute(right, GROUP, route(lambda r, c, q: (r ^ 1, c, q)))
-    first = lax.ppermute(left, GROUP, route(lambda r, c, q: (2 * c + r // 2, r % 2, q)))
-    passed = lax.ppermute(far, GROUP, route(lambda r, c, q: (r ^ 1, c, q)))
-    second = lax.ppermute(first, GROUP, route(lambda r, c, q: (r, 1 - c, q)))
-    kept, weight, bias = pl.pallas_call(
+    kept, left, weight, bias = pl.pallas_call(
         keep_kernel,
         out_shape=(
             payload,
-            jax.ShapeDtypeStruct((hidden * 128, width), jnp.bfloat16),
+            payload,
+            jax.ShapeDtypeStruct((hidden * 128, WIDE * width), jnp.bfloat16),
             jax.ShapeDtypeStruct((1, width), jnp.float32),
         ),
-        in_specs=[vmem] * 3,
-        out_specs=(vmem,) * 3,
+        in_specs=[vmem] * 4,
+        out_specs=(vmem,) * 4,
         compiler_params=pltpu.CompilerParams(vmem_limit_bytes=16 * 1024 * 1024),
         cost_estimate=pl.CostEstimate(flops=0, bytes_accessed=1 << 22, transcendentals=0),
         name="keep",
-    )(right, closing_linear_map, closing_linear_constant.reshape(1, width))
-    rights = [kept, near, far, passed]
-    lefts = [first, second]
+    )(right, left, closing_linear_map, closing_linear_constant.reshape(1, width))
+
+    first = lax.ppermute(left, GROUP, route(lambda r, c, q: (2 * c + r // 2, r % 2, q)))
+    second = lax.ppermute(first, GROUP, route(lambda r, c, q: (r, 1 - c, q)))
+    far = lax.ppermute(right, GROUP, route(lambda r, c, q: (r ^ 2, c, q)))
+    near = lax.ppermute(right, GROUP, route(lambda r, c, q: (r ^ 1, c, q)))
+    passed = lax.ppermute(far, GROUP, route(lambda r, c, q: (r ^ 1, c, q)))
 
     def pair_sums(own, kind):
         return pl.pallas_call(
@@ -343,14 +356,14 @@
             scratch_shapes=[
                 pltpu.VMEM((2, rows, sequences), jnp.bfloat16),
                 pltpu.VMEM((4, rows, sequences), jnp.bfloat16),
-                pltpu.VMEM((pairs, hidden * 128), jnp.bfloat16),
+                pltpu.VMEM((pairs // WIDE, hidden * 128), jnp.bfloat16),
             ],
             compiler_params=pltpu.CompilerParams(vmem_limit_bytes=24 * 1024 * 1024),
             cost_estimate=pl.CostEstimate(
                 flops=2 * pairs * hidden * 128 * width, bytes_accessed=1 << 20, transcendentals=0
             ),
             name="own_pair_sums" if own else "other_pair_sums",
-        )(*lefts, *rights, weight, bias)
+        )(far, passed, first, second, near, kept, weight, bias)
 
     theirs = pair_sums(False, jnp.bfloat16)
     received = lax.ppermute(theirs, GROUP, route(lambda r, c, q: (r, c, 1 - q)))

time: 25 us -> 26.8 us (1.072)
  the two profiles are of different devices: /device:TPU:1 before, /device:TPU:11 now
where the time goes in v6:
time: 26.8 us; the launch traced here: 26.6 us
  starting transfers between devices  9.8 us (37%)
  Pallas kernels  6.68 us (25%)
  waiting for transfers between devices  6.65 us (25%)
  local copies, waits for them, and re-layouts  3.37 us (13%)
    ppermute x1, starting transfers between devices, direct_shards(): received = lax.ppermute(theirs, GROUP, route(lambda r, c, q: (r, c, 1 - q)))  3.97 us
    ppermute x1, waiting for transfers between devices, direct_shards(): lax.ppermute(left, GROUP, route(lambda r, c, q: (2 * c + r // 2, r % 2, q)))  3.49 us
    pallas_call x1, Pallas kernels, direct_shards(): pl.pallas_call(project_kernel, out_shape=(payload, payload), in_specs=[in...  3.47 us
    unnamed x8, local copies, waits for them, and re-layouts  3.37 us
    ppermute x1, waiting for transfers between devices, direct_shards(): second = lax.ppermute(first, GROUP, route(lambda r, c, q: (r, 1 - c, q)))  2.91 us
    ppermute x1, starting transfers between devices, direct_shards(): far = lax.ppermute(right, GROUP, route(lambda r, c, q: (r ^ 2, c, q)))  2.37 us
    pallas_call x2, Pallas kernels, pair_sums(): pl.pallas_call(lambda *refs: pair_kernel(own, *refs), out_shape=jax.Shape...  1.96 us
    ppermute x1, starting transfers between devices, direct_shards(): lax.ppermute(left, GROUP, route(lambda r, c, q: (2 * c + r // 2, r % 2, q)))  1.92 us
  transfers between devices with their start and end apart: 6, of which 3 were waited for; matrix products, arithmetic and copies ran while one was open for 0% of the time, Pallas kernels for 5%

profile of v6, /device:TPU:11, one launch (start us, length us, event | category | flops | bytes accessed | tf_op | source)
XLA Modules:
  0.0 26.6 jit_solution(3443844829716018576)
XLA Ops:
  0.0 3.5 %normalize_and_project.1 = (bf16[272,128]{1,0:T(8,128)(2,1)}, bf16[272,128]{1,0:T(8,128)(2,1)}) custom-call(s32[8]{0:T(128)} %pept_hbm.1, bf16[1024,256]{1,0:T(8,128)(2,1)} %bitcast.10, s32[8,128]{1,0:T(8,128)} %bitcast.13, f32[1,256]{1,0:T(1,128)} %bitcast.14, f32[1,256]{1,0:T(1,128)} %bitcast.15, bf16[32,256]{1,0:T(8,128)(2,1)} %bitcast.11, ...), custom_call_target="tpu_custom_call" | custom-call | tf_op jit(solution)/shard_map/normalize_and_project/pallas_call | solution.py:296
  3.5 2.4 %collective-permute-start = (bf16[272,128]{1,0:T(8,128)(2,1)}, bf16[272,128]{1,0:T(8,128)(2,1)S(1)}, u32[]{:S(2)}, u32[]{:S(2)}) collective-permute-start(bf16[272,128]{1,0:T(8,128)(2,1)} %get-tuple-element.11.right_ref), channel_id=1, source_target_pairs={{0,8},{1,9},{2,10},{3,11},{4,12},{5,13},{6,14},{7,15},{8,0},{9,1},... | collective-permute-start | bytes 208904 | tf_op jit(solution)/shard_map/ppermute | solution.py:346
  5.9 0.0 copy-start
  5.9 0.9 %copy-done = bf16[1024,128]{1,0:T(8,128)(2,1)S(1)} copy-done((bf16[1024,128]{1,0:T(8,128)(2,1)S(1)}, bf16[1024,128]{1,0:T(8,128)(2,1)}, u32[]{:S(2)}) %copy-start) | copy-done | bytes 262168
  6.8 0.0 copy-start.1
  6.8 0.9 %copy-done.1 = bf16[272,128]{1,0:T(8,128)(2,1)S(1)} copy-done((bf16[272,128]{1,0:T(8,128)(2,1)S(1)}, bf16[272,128]{1,0:T(8,128)(2,1)}, u32[]{:S(2)}) %copy-start.1) | copy-done | bytes 69656
  7.7 0.0 copy-start.2
  7.7 0.9 %copy-done.2 = bf16[272,128]{1,0:T(8,128)(2,1)S(1)} copy-done((bf16[272,128]{1,0:T(8,128)(2,1)S(1)}, bf16[272,128]{1,0:T(8,128)(2,1)}, u32[]{:S(2)}) %copy-start.2) | copy-done | bytes 69656
  8.6 0.0 copy-start.3
  8.6 0.7 %copy-done.3 = f32[128]{0:T(128)S(1)} copy-done((f32[128]{0:T(128)S(1)}, f32[128]{0:T(128)}, u32[]{:S(2)}) %copy-start.3) | copy-done | bytes 536
  9.2 0.3 %keep.1 = (bf16[272,128]{1,0:T(8,128)(2,1)S(1)}, bf16[272,128]{1,0:T(8,128)(2,1)S(1)}, bf16[4096,256]{1,0:T(8,128)(2,1)S(1)}, f32[1,128]{1,0:T(1,128)S(1)}) custom-call(bf16[272,128]{1,0:T(8,128)(2,1)S(1)} %copy-done.1, bf16[272,128]{1,0:T(8,128)(2,1)S(1)} %copy-done.2, bf16[1024,128]{1,0:T(8,128)(2,1)S(1)} %copy-done, f32[1,128]{1,0:T(1,128)S(1)} %bitcast.9), custom_call_target="tpu_custom_call" | custom-call | bytes 4194304 | tf_op jit(solution)/shard_map/keep/pallas_call | solution.py:329
  9.5 1.9 %collective-permute-start.2 = (bf16[272,128]{1,0:T(8,128)(2,1)S(1)}, bf16[272,128]{1,0:T(8,128)(2,1)S(1)}, u32[]{:S(2)}, u32[]{:S(2)}) collective-permute-start(bf16[272,128]{1,0:T(8,128)(2,1)S(1)} %get-tuple-element.13), channel_id=1, source_target_pairs={{0,0},{1,1},{2,8},{3,9},{4,2},{5,3},{6,10},{7,11},{8,4},{9,5},{10,... | collective-permute-start | bytes 208904 | tf_op jit(solution)/shard_map/ppermute | solution.py:344
  11.4 0.2 collective-permute-start.4
  11.7 0.0 collective-permute-done.refs_0_
  11.7 1.3 %collective-permute-start.1 = (bf16[272,128]{1,0:T(8,128)(2,1)S(1)}, bf16[272,128]{1,0:T(8,128)(2,1)S(1)}, u32[]{:S(2)}, u32[]{:S(2)}) collective-permute-start(bf16[272,128]{1,0:T(8,128)(2,1)S(1)} %collective-permute-done.refs_0_), channel_id=1, source_target_pairs={{0,4},{1,5},{2,6},{3,7},{4,0},{5,1},{6,2},{7,3},{8,12},{9,13},{10,... | collective-permute-start | bytes 208904 | tf_op jit(solution)/shard_map/ppermute | solution.py:348
  13.0 3.5 %collective-permute-done.2.refs_2_ = bf16[272,128]{1,0:T(8,128)(2,1)S(1)} collective-permute-done((bf16[272,128]{1,0:T(8,128)(2,1)S(1)}, bf16[272,128]{1,0:T(8,128)(2,1)S(1)}, u32[]{:S(2)}, u32[]{:S(2)}) %collective-permute-start.2) | collective-permute-done | bytes 69664 | tf_op jit(solution)/shard_map/ppermute | solution.py:344
  16.5 0.0 collective-permute-start.3
  16.5 0.0 collective-permute-done.4.refs_4_
  16.5 0.2 collective-permute-done.1.refs_1_
  16.7 2.9 %collective-permute-done.3.refs_3_ = bf16[272,128]{1,0:T(8,128)(2,1)S(1)} collective-permute-done((bf16[272,128]{1,0:T(8,128)(2,1)S(1)}, bf16[272,128]{1,0:T(8,128)(2,1)S(1)}, u32[]{:S(2)}, u32[]{:S(2)}) %collective-permute-start.3) | collective-permute-done | bytes 69664 | tf_op jit(solution)/shard_map/ppermute | solution.py:345
  19.6 1.0 %other_pair_sums.1 = bf16[288,128]{1,0:T(8,128)(2,1)S(1)} custom-call(bf16[272,128]{1,0:T(8,128)(2,1)S(1)} %collective-permute-done.refs_0_, bf16[272,128]{1,0:T(8,128)(2,1)S(1)} %collective-permute-done.1.refs_1_, bf16[272,128]{1,0:T(8,128)(2,1)S(1)} %collective-permute-done.2.refs_2_, bf16[272,128]{1,0:T(8,128)(2,1)S(1)} %collective-permute-done.3.refs_3_, ...), custom_call_target="tpu_custom_call" | custom-call | flops 268435456 | bytes 1048576 | tf_op jit(solution)/shard_map/other_pair_sums/pallas_call | solution.py:351
  20.6 4.0 %collective-permute-start.5 = (bf16[288,128]{1,0:T(8,128)(2,1)S(1)}, bf16[288,128]{1,0:T(8,128)(2,1)S(1)}, u32[]{:S(2)}, u32[]{:S(2)}) collective-permute-start(bf16[288,128]{1,0:T(8,128)(2,1)S(1)} %other_pair_sums.1), channel_id=1, source_target_pairs={{0,1},{1,0},{2,3},{3,2},{4,5},{5,4},{6,7},{7,6},{8,9},{9,8},{10,11... | collective-permute-start | bytes 221192 | tf_op jit(solution)/shard_map/ppermute | solution.py:369
  24.6 1.0 %own_pair_sums.1.mine_ref = f32[288,128]{1,0:T(8,128)S(1)} custom-call(bf16[272,128]{1,0:T(8,128)(2,1)S(1)} %collective-permute-done.refs_0_, bf16[272,128]{1,0:T(8,128)(2,1)S(1)} %collective-permute-done.1.refs_1_, bf16[272,128]{1,0:T(8,128)(2,1)S(1)} %collective-permute-done.2.refs_2_, bf16[272,128]{1,0:T(8,128)(2,1)S(1)} %collective-permute-done.3.refs_3_, ...), custom_call_target="tpu_custom_call" | custom-call | flops 268435456 | bytes 1048576 | tf_op jit(solution)/shard_map/own_pair_sums/pallas_call | solution.py:351
  25.6 0.0 collective-permute-done.5.other_ref
  25.6 1.0 %divide.1 = bf16[16,16,128]{2,1,0:T(8,128)(2,1)} custom-call(f32[288,128]{1,0:T(8,128)S(1)} %own_pair_sums.1.mine_ref, bf16[288,128]{1,0:T(8,128)(2,1)S(1)} %collective-permute-done.5.other_ref), custom_call_target="tpu_custom_call" | custom-call | tf_op jit(solution)/shard_map/divide/pallas_call | solution.py:371
Async XLA Ops:
  3.5 8.2 %collective-permute-start = (bf16[272,128]{1,0:T(8,128)(2,1)}, bf16[272,128]{1,0:T(8,128)(2,1)S(1)}, u32[]{:S(2)}, u32[]{:S(2)}) collective-permute-start(bf16[272,128]{1,0:T(8,128)(2,1)} %get-tuple-element.11.right_ref), channel_id=1, source_target_pairs={{0,8},{1,9},{2,10},{3,11},{4,12},{5,13},{6,14},{7,15},{8,0},{9,1},... | collective-permute-start | bytes 208904 | tf_op jit(solution)/shard_map/ppermute | solution.py:346
  5.9 0.9 %copy-start = (bf16[1024,128]{1,0:T(8,128)(2,1)S(1)}, bf16[1024,128]{1,0:T(8,128)(2,1)}, u32[]{:S(2)}) copy-start(bf16[1024,128]{1,0:T(8,128)(2,1)} %w_ref.1) | copy-start | bytes 786436
  6.8 0.9 %copy-start.1 = (bf16[272,128]{1,0:T(8,128)(2,1)S(1)}, bf16[272,128]{1,0:T(8,128)(2,1)}, u32[]{:S(2)}) copy-start(bf16[272,128]{1,0:T(8,128)(2,1)} %get-tuple-element.11.right_ref) | copy-start | bytes 208900
  7.7 0.9 %copy-start.2 = (bf16[272,128]{1,0:T(8,128)(2,1)S(1)}, bf16[272,128]{1,0:T(8,128)(2,1)}, u32[]{:S(2)}) copy-start(bf16[272,128]{1,0:T(8,128)(2,1)} %get-tuple-element.12.left_ref) | copy-start | bytes 208900
  8.6 0.7 %copy-start.3 = (f32[128]{0:T(128)S(1)}, f32[128]{0:T(128)}, u32[]{:S(2)}) copy-start(f32[128]{0:T(128)} %param.21) | copy-start | bytes 1540
  9.5 7.0 %collective-permute-start.2 = (bf16[272,128]{1,0:T(8,128)(2,1)S(1)}, bf16[272,128]{1,0:T(8,128)(2,1)S(1)}, u32[]{:S(2)}, u32[]{:S(2)}) collective-permute-start(bf16[272,128]{1,0:T(8,128)(2,1)S(1)} %get-tuple-element.13), channel_id=1, source_target_pairs={{0,0},{1,1},{2,8},{3,9},{4,2},{5,3},{6,10},{7,11},{8,4},{9,5},{10,... | collective-permute-start | bytes 208904 | tf_op jit(solution)/shard_map/ppermute | solution.py:344
  11.4 5.0 %collective-permute-start.4 = (bf16[272,128]{1,0:T(8,128)(2,1)S(1)}, bf16[272,128]{1,0:T(8,128)(2,1)S(1)}, u32[]{:S(2)}, u32[]{:S(2)}) collective-permute-start(bf16[272,128]{1,0:T(8,128)(2,1)S(1)} %copy-done.1), channel_id=1, source_target_pairs={{0,4},{1,5},{2,6},{3,7},{4,0},{5,1},{6,2},{7,3},{8,12},{9,13},{10,... | collective-permute-start | bytes 208904 | tf_op jit(solution)/shard_map/ppermute | solution.py:347
  11.7 5.0 %collective-permute-start.1 = (bf16[272,128]{1,0:T(8,128)(2,1)S(1)}, bf16[272,128]{1,0:T(8,128)(2,1)S(1)}, u32[]{:S(2)}, u32[]{:S(2)}) collective-permute-start(bf16[272,128]{1,0:T(8,128)(2,1)S(1)} %collective-permute-done.refs_0_), channel_id=1, source_target_pairs={{0,4},{1,5},{2,6},{3,7},{4,0},{5,1},{6,2},{7,3},{8,12},{9,13},{10,... | collective-permute-start | bytes 208904 | tf_op jit(solution)/shard_map/ppermute | solution.py:348
  16.5 3.2 %collective-permute-start.3 = (bf16[272,128]{1,0:T(8,128)(2,1)S(1)}, bf16[272,128]{1,0:T(8,128)(2,1)S(1)}, u32[]{:S(2)}, u32[]{:S(2)}) collective-permute-start(bf16[272,128]{1,0:T(8,128)(2,1)S(1)} %collective-permute-done.2.refs_2_), channel_id=1, source_target_pairs={{0,2},{1,3},{2,0},{3,1},{4,6},{5,7},{6,4},{7,5},{8,10},{9,11},{10,... | collective-permute-start | bytes 208904 | tf_op jit(solution)/shard_map/ppermute | solution.py:345
  20.6 5.0 %collective-permute-start.5 = (bf16[288,128]{1,0:T(8,128)(2,1)S(1)}, bf16[288,128]{1,0:T(8,128)(2,1)S(1)}, u32[]{:S(2)}, u32[]{:S(2)}) collective-permute-start(bf16[288,128]{1,0:T(8,128)(2,1)S(1)} %other_pair_sums.1), channel_id=1, source_target_pairs={{0,1},{1,0},{2,3},{3,2},{4,5},{5,4},{6,7},{7,6},{8,9},{9,8},{10,11... | collective-permute-start | bytes 221192 | tf_op jit(solution)/shard_map/ppermute | solution.py:369

commit v7 on v6

--- a/solution.py
+++ b/solution.py
@@ -109,7 +109,7 @@
 
 def project_kernel(
     pept_hbm, x_hbm, occ_hbm, gain_hbm, shift_hbm, wl_hbm, bl_hbm, wr_hbm, br_hbm,
-    right_ref, left_ref,
+    left_ref, right_ref,
     pept_ref, x_ref, occ_ref, gain_ref, shift_ref, wl_ref, bl_ref, wr_ref, br_ref,
     y_ref, l_ref, x_sems, sems,
 ):
@@ -170,10 +170,13 @@
             store(first, part * (lane == a).astype(jnp.bfloat16))
 
 
-def keep_kernel(right_ref, left_ref, w_ref, b_ref, right_out, left_out, w_out, b_out):
+def join_kernel(right_ref, far_ref, out_ref):
+    out_ref[0] = right_ref[...]
+    out_ref[1] = far_ref[...]
+
+
+def keep_kernel(w_ref, b_ref, w_out, b_out):
     hidden = 32
-    right_out[...] = right_ref[...]
-    left_out[...] = left_ref[...]
     b_out[...] = b_ref[...]
     width = b_ref.shape[1]
     zero = jnp.zeros((hidden, width), jnp.bfloat16)
@@ -187,7 +190,7 @@
 
 
 def pair_kernel(
-    own, r2, r3, l0, l1, r1, r0, w_ref, b_ref, out_ref, ls_ref, rs_ref, big_ref
+    own, l0, l1, held, passed, w_ref, b_ref, out_ref, ls_ref, rs_ref, big_ref
 ):
     body = l0.shape[0] - MASK_ROWS
     hidden = 32
@@ -195,8 +198,9 @@
     row, col, seq = (lax.axis_index(name) for name in GROUP)
     for k, piece in enumerate((l0, l1)):
         ls_ref[col ^ k] = piece[...]
-    for k, piece in enumerate((r0, r1, r2, r3)):
-        rs_ref[row ^ k] = piece[...]
+    for k in range(2):
+        rs_ref[row ^ (2 * k)] = held[k]
+        rs_ref[row ^ (2 * k + 1)] = passed[k]
     half = 2 * (seq if own else 1 - seq)
 
     def rows(ref, at, first, last):
@@ -293,7 +297,7 @@
     payload = jax.ShapeDtypeStruct((rows, sequences), jnp.bfloat16)
     vmem = pl.BlockSpec(memory_space=pltpu.VMEM)
     in_hbm = pl.BlockSpec(memory_space=pltpu.HBM)
-    right, left = pl.pallas_call(
+    left, right = pl.pallas_call(
         project_kernel,
         out_shape=(payload, payload),
         in_specs=[in_hbm] * 9,
@@ -326,32 +330,35 @@
         rhs_linear_map.T,
         rhs_linear_constant.reshape(1, hidden),
     )
-    kept, left, weight, bias = pl.pallas_call(
+    far = lax.ppermute(right, GROUP, route(lambda r, c, q: (r ^ 2, c, q)))
+    first = lax.ppermute(left, GROUP, route(lambda r, c, q: (2 * c + r // 2, r % 2, q)))
+    held = pl.pallas_call(
+        join_kernel,
+        out_shape=jax.ShapeDtypeStruct((2,) + payload.shape, jnp.bfloat16),
+        in_specs=[vmem] * 2,
+        out_specs=vmem,
+        name="join",
+    )(right, far)
+    passed = lax.ppermute(held, GROUP, route(lambda r, c, q: (r ^ 1, c, q)))
+    second = lax.ppermute(first, GROUP, route(lambda r, c, q: (r, 1 - c, q)))
+    weight, bias = pl.pallas_call(
         keep_kernel,
         out_shape=(
-            payload,
-            payload,
             jax.ShapeDtypeStruct((hidden * 128, WIDE * width), jnp.bfloat16),
             jax.ShapeDtypeStruct((1, width), jnp.float32),
         ),
-        in_specs=[vmem] * 4,
-        out_specs=(vmem,) * 4,
+        in_specs=[vmem] * 2,
+        out_specs=(vmem,) * 2,
         compiler_params=pltpu.CompilerParams(vmem_limit_bytes=16 * 1024 * 1024),
         cost_estimate=pl.CostEstimate(flops=0, bytes_accessed=1 << 22, transcendentals=0),
         name="keep",
-    )(right, left, closing_linear_map, closing_linear_constant.reshape(1, width))
-
-    first = lax.ppermute(left, GROUP, route(lambda r, c, q: (2 * c + r // 2, r % 2, q)))
-    second = lax.ppermute(first, GROUP, route(lambda r, c, q: (r, 1 - c, q)))
-    far = lax.ppermute(right, GROUP, route(lambda r, c, q: (r ^ 2, c, q)))
-    near = lax.ppermute(right, GROUP, route(lambda r, c, q: (r ^ 1, c, q)))
-    passed = lax.ppermute(far, GROUP, route(lambda r, c, q: (r ^ 1, c, q)))
+    )(closing_linear_map, closing_linear_constant.reshape(1, width))
 
     def pair_sums(own, kind):
         return pl.pallas_call(
             lambda *refs: pair_kernel(own, *refs),
             out_shape=jax.ShapeDtypeStruct((pairs + 2 * MASK_ROWS, width), kind),
-            in_specs=[vmem] * 8,
+            in_specs=[vmem] * 6,
             out_specs=vmem,
             scratch_shapes=[
                 pltpu.VMEM((2, rows, sequences), jnp.bfloat16),
@@ -363,7 +370,7 @@
                 flops=2 * pairs * hidden * 128 * width, bytes_accessed=1 << 20, transcendentals=0
             ),
             name="own_pair_sums" if own else "other_pair_sums",
-        )(far, passed, first, second, near, kept, weight, bias)
+        )(first, second, held, passed, weight, bias)
 
     theirs = pair_sums(False, jnp.bfloat16)
     received = lax.ppermute(theirs, GROUP, route(lambda r, c, q: (r, c, 1 - q)))

time: 26.8 us -> 24.8 us (0.925)
  the two profiles are of different devices: /device:TPU:11 before, /device:TPU:23 now
where the time goes in v7:
time: 24.8 us; the launch traced here: 24.5 us
  starting transfers between devices  10.7 us (43%)
  Pallas kernels  8.22 us (33%)
  local copies, waits for them, and re-layouts  3.14 us (13%)
  waiting for transfers between devices  2.39 us (10%)
    ppermute x1, starting transfers between devices, direct_shards(): passed = lax.ppermute(held, GROUP, route(lambda r, c, q: (r ^ 1, c, q)))  3.99 us
    pallas_call x1, Pallas kernels, direct_shards(): pl.pallas_call(project_kernel, out_shape=(payload, payload), in_specs=[in...  3.46 us
    ppermute x1, starting transfers between devices, direct_shards(): received = lax.ppermute(theirs, GROUP, route(lambda r, c, q: (r, c, 1 - q)))  3.44 us
    ppermute x1, starting transfers between devices, direct_shards(): lax.ppermute(left, GROUP, route(lambda r, c, q: (2 * c + r // 2, r % 2, q)))  3.16 us
    unnamed x10, local copies, waits for them, and re-layouts  3.14 us
    pallas_call x2, Pallas kernels, pair_sums(): pl.pallas_call(lambda *refs: pair_kernel(own, *refs), out_shape=jax.Shape...  1.96 us
    pallas_call x1, Pallas kernels, direct_shards(): pl.pallas_call(join_kernel, out_shape=jax.ShapeDtypeStruct((2,) + payload...  1.57 us
    ppermute x1, waiting for transfers between devices, direct_shards(): second = lax.ppermute(first, GROUP, route(lambda r, c, q: (r, 1 - c, q)))  1.28 us
  transfers between devices with their start and end apart: 5, of which 2 were waited for; matrix products, arithmetic and copies ran while one was open for 0% of the time, Pallas kernels for 12%

profile of v7, /device:TPU:23, one launch (start us, length us, event | category | flops | bytes accessed | tf_op | source)
XLA Modules:
  0.0 24.5 jit_solution(11223152087485325896)
XLA Ops:
  0.0 3.5 %normalize_and_project.1 = (bf16[272,128]{1,0:T(8,128)(2,1)}, bf16[272,128]{1,0:T(8,128)(2,1)}) custom-call(s32[8]{0:T(128)} %pept_hbm.1, bf16[1024,256]{1,0:T(8,128)(2,1)} %bitcast.10, s32[8,128]{1,0:T(8,128)} %bitcast.13, f32[1,256]{1,0:T(1,128)} %bitcast.14, f32[1,256]{1,0:T(1,128)} %bitcast.15, bf16[32,256]{1,0:T(8,128)(2,1)} %bitcast.11, ...), custom_call_target="tpu_custom_call" | custom-call | tf_op jit(solution)/shard_map/normalize_and_project/pallas_call | solution.py:300
  3.5 0.1 collective-permute-start.2
  3.6 3.2 %collective-permute-start = (bf16[272,128]{1,0:T(8,128)(2,1)}, bf16[272,128]{1,0:T(8,128)(2,1)S(1)}, u32[]{:S(2)}, u32[]{:S(2)}) collective-permute-start(bf16[272,128]{1,0:T(8,128)(2,1)} %get-tuple-element.9), channel_id=1, source_target_pairs={{0,0},{1,1},{2,8},{3,9},{4,2},{5,3},{6,10},{7,11},{8,4},{9,5},{10,... | collective-permute-start | bytes 208904 | tf_op jit(solution)/shard_map/ppermute | solution.py:334
  6.8 1.1 %collective-permute-done.2.far_ref = bf16[272,128]{1,0:T(8,128)(2,1)S(1)} collective-permute-done((bf16[272,128]{1,0:T(8,128)(2,1)}, bf16[272,128]{1,0:T(8,128)(2,1)S(1)}, u32[]{:S(2)}, u32[]{:S(2)}) %collective-permute-start.2) | collective-permute-done | bytes 69664 | tf_op jit(solution)/shard_map/ppermute | solution.py:333
  7.9 0.0 copy-start.4
  7.9 0.6 %copy-done.4 = bf16[272,128]{1,0:T(8,128)(2,1)} copy-done((bf16[272,128]{1,0:T(8,128)(2,1)}, bf16[272,128]{1,0:T(8,128)(2,1)S(1)}, u32[]{:S(2)}) %copy-start.4) | copy-done | bytes 69656
  8.5 1.6 %join.1.refs_2_ = bf16[2,272,128]{2,1,0:T(8,128)(2,1)} custom-call(bf16[272,128]{1,0:T(8,128)(2,1)} %get-tuple-element.10.right_ref, bf16[272,128]{1,0:T(8,128)(2,1)} %copy-done.4), custom_call_target="tpu_custom_call" | custom-call | tf_op jit(solution)/shard_map/join/pallas_call | solution.py:335
  10.1 0.0 copy-start.1
  10.1 4.0 %collective-permute-start.3 = (bf16[2,272,128]{2,1,0:T(8,128)(2,1)}, bf16[2,272,128]{2,1,0:T(8,128)(2,1)S(1)}, u32[]{:S(2)}, u32[]{:S(2)}) collective-permute-start(bf16[2,272,128]{2,1,0:T(8,128)(2,1)} %join.1.refs_2_), channel_id=1, source_target_pairs={{0,4},{1,5},{2,6},{3,7},{4,0},{5,1},{6,2},{7,3},{8,12},{9,13},{10,... | collective-permute-start | bytes 417800 | tf_op jit(solution)/shard_map/ppermute | solution.py:342
  14.1 0.0 collective-permute-done.refs_0_
  14.1 0.0 collective-permute-start.1
  14.1 0.0 copy-start.2
  14.1 0.9 %copy-done.2 = bf16[1024,128]{1,0:T(8,128)(2,1)S(1)} copy-done((bf16[1024,128]{1,0:T(8,128)(2,1)S(1)}, bf16[1024,128]{1,0:T(8,128)(2,1)}, u32[]{:S(2)}) %copy-start.2) | copy-done | bytes 262168
  15.0 0.0 copy-start.3
  15.0 0.7 %copy-done.3 = f32[128]{0:T(128)S(1)} copy-done((f32[128]{0:T(128)S(1)}, f32[128]{0:T(128)}, u32[]{:S(2)}) %copy-start.3) | copy-done | bytes 536
  15.7 0.3 %keep.1 = (bf16[4096,256]{1,0:T(8,128)(2,1)S(1)}, f32[1,128]{1,0:T(1,128)S(1)}) custom-call(bf16[1024,128]{1,0:T(8,128)(2,1)S(1)} %copy-done.2, f32[1,128]{1,0:T(1,128)S(1)} %bitcast.9), custom_call_target="tpu_custom_call" | custom-call | bytes 4194304 | tf_op jit(solution)/shard_map/keep/pallas_call | solution.py:344
  15.9 1.3 %collective-permute-done.1.refs_1_ = bf16[272,128]{1,0:T(8,128)(2,1)S(1)} collective-permute-done((bf16[272,128]{1,0:T(8,128)(2,1)S(1)}, bf16[272,128]{1,0:T(8,128)(2,1)S(1)}, u32[]{:S(2)}, u32[]{:S(2)}) %collective-permute-start.1) | collective-permute-done | bytes 69664 | tf_op jit(solution)/shard_map/ppermute | solution.py:343
  17.2 0.0 collective-permute-done.3.refs_3_
  17.2 0.0 copy-start
  17.2 0.9 %copy-done = bf16[2,272,128]{2,1,0:T(8,128)(2,1)S(1)} copy-done((bf16[2,272,128]{2,1,0:T(8,128)(2,1)S(1)}, bf16[2,272,128]{2,1,0:T(8,128)(2,1)}, u32[]{:S(2)}) %copy-start) | copy-done | bytes 139288
  18.1 1.0 %other_pair_sums.1 = bf16[288,128]{1,0:T(8,128)(2,1)S(1)} custom-call(bf16[272,128]{1,0:T(8,128)(2,1)S(1)} %collective-permute-done.refs_0_, bf16[272,128]{1,0:T(8,128)(2,1)S(1)} %collective-permute-done.1.refs_1_, bf16[2,272,128]{2,1,0:T(8,128)(2,1)S(1)} %copy-done, bf16[2,272,128]{2,1,0:T(8,128)(2,1)S(1)} %collective-permute-done.3.refs_3_, ...), custom_call_target="tpu_custom_call" | custom-call | flops 268435456 | bytes 1048576 | tf_op jit(solution)/shard_map/other_pair_sums/pallas_call | solution.py:358
  19.1 3.4 %collective-permute-start.4 = (bf16[288,128]{1,0:T(8,128)(2,1)S(1)}, bf16[288,128]{1,0:T(8,128)(2,1)S(1)}, u32[]{:S(2)}, u32[]{:S(2)}) collective-permute-start(bf16[288,128]{1,0:T(8,128)(2,1)S(1)} %other_pair_sums.1), channel_id=1, source_target_pairs={{0,1},{1,0},{2,3},{3,2},{4,5},{5,4},{6,7},{7,6},{8,9},{9,8},{10,11... | collective-permute-start | bytes 221192 | tf_op jit(solution)/shard_map/ppermute | solution.py:376
  22.6 0.0 copy-done.1
  22.6 1.0 %own_pair_sums.1.mine_ref = f32[288,128]{1,0:T(8,128)S(1)} custom-call(bf16[272,128]{1,0:T(8,128)(2,1)S(1)} %collective-permute-done.refs_0_, bf16[272,128]{1,0:T(8,128)(2,1)S(1)} %collective-permute-done.1.refs_1_, bf16[2,272,128]{2,1,0:T(8,128)(2,1)S(1)} %copy-done.1, bf16[2,272,128]{2,1,0:T(8,128)(2,1)S(1)} %collective-permute-done.3.refs_3_, ...), custom_call_target="tpu_custom_call" | custom-call | flops 268435456 | bytes 1048576 | tf_op jit(solution)/shard_map/own_pair_sums/pallas_call | solution.py:358
  23.5 0.0 collective-permute-done.4.other_ref
  23.6 1.0 %divide.1 = bf16[16,16,128]{2,1,0:T(8,128)(2,1)} custom-call(f32[288,128]{1,0:T(8,128)S(1)} %own_pair_sums.1.mine_ref, bf16[288,128]{1,0:T(8,128)(2,1)S(1)} %collective-permute-done.4.other_ref), custom_call_target="tpu_custom_call" | custom-call | tf_op jit(solution)/shard_map/divide/pallas_call | solution.py:378
Async XLA Ops:
  3.5 4.4 %collective-permute-start.2 = (bf16[272,128]{1,0:T(8,128)(2,1)}, bf16[272,128]{1,0:T(8,128)(2,1)S(1)}, u32[]{:S(2)}, u32[]{:S(2)}) collective-permute-start(bf16[272,128]{1,0:T(8,128)(2,1)} %get-tuple-element.10.right_ref), channel_id=1, source_target_pairs={{0,8},{1,9},{2,10},{3,11},{4,12},{5,13},{6,14},{7,15},{8,0},{9,1},... | collective-permute-start | bytes 208904 | tf_op jit(solution)/shard_map/ppermute | solution.py:333
  3.6 10.5 %collective-permute-start = (bf16[272,128]{1,0:T(8,128)(2,1)}, bf16[272,128]{1,0:T(8,128)(2,1)S(1)}, u32[]{:S(2)}, u32[]{:S(2)}) collective-permute-start(bf16[272,128]{1,0:T(8,128)(2,1)} %get-tuple-element.9), channel_id=1, source_target_pairs={{0,0},{1,1},{2,8},{3,9},{4,2},{5,3},{6,10},{7,11},{8,4},{9,5},{10,... | collective-permute-start | bytes 208904 | tf_op jit(solution)/shard_map/ppermute | solution.py:334
  7.9 0.6 %copy-start.4 = (bf16[272,128]{1,0:T(8,128)(2,1)}, bf16[272,128]{1,0:T(8,128)(2,1)S(1)}, u32[]{:S(2)}) copy-start(bf16[272,128]{1,0:T(8,128)(2,1)S(1)} %collective-permute-done.2.far_ref) | copy-start | bytes 208900
  10.1 12.5 %copy-start.1 = (bf16[2,272,128]{2,1,0:T(8,128)(2,1)S(1)}, bf16[2,272,128]{2,1,0:T(8,128)(2,1)}, u32[]{:S(2)}) copy-start(bf16[2,272,128]{2,1,0:T(8,128)(2,1)} %join.1.refs_2_) | copy-start | bytes 417796
  10.1 7.2 %collective-permute-start.3 = (bf16[2,272,128]{2,1,0:T(8,128)(2,1)}, bf16[2,272,128]{2,1,0:T(8,128)(2,1)S(1)}, u32[]{:S(2)}, u32[]{:S(2)}) collective-permute-start(bf16[2,272,128]{2,1,0:T(8,128)(2,1)} %join.1.refs_2_), channel_id=1, source_target_pairs={{0,4},{1,5},{2,6},{3,7},{4,0},{5,1},{6,2},{7,3},{8,12},{9,13},{10,... | collective-permute-start | bytes 417800 | tf_op jit(solution)/shard_map/ppermute | solution.py:342
  14.1 3.2 %collective-permute-start.1 = (bf16[272,128]{1,0:T(8,128)(2,1)S(1)}, bf16[272,128]{1,0:T(8,128)(2,1)S(1)}, u32[]{:S(2)}, u32[]{:S(2)}) collective-permute-start(bf16[272,128]{1,0:T(8,128)(2,1)S(1)} %collective-permute-done.refs_0_), channel_id=1, source_target_pairs={{0,2},{1,3},{2,0},{3,1},{4,6},{5,7},{6,4},{7,5},{8,10},{9,11},{10,... | collective-permute-start | bytes 208904 | tf_op jit(solution)/shard_map/ppermute | solution.py:343
  14.1 1.0 %copy-start.2 = (bf16[1024,128]{1,0:T(8,128)(2,1)S(1)}, bf16[1024,128]{1,0:T(8,128)(2,1)}, u32[]{:S(2)}) copy-start(bf16[1024,128]{1,0:T(8,128)(2,1)} %w_ref.1) | copy-start | bytes 786436
  15.0 0.7 %copy-start.3 = (f32[128]{0:T(128)S(1)}, f32[128]{0:T(128)}, u32[]{:S(2)}) copy-start(f32[128]{0:T(128)} %param.21) | copy-start | bytes 1540
  17.2 0.9 %copy-start = (bf16[2,272,128]{2,1,0:T(8,128)(2,1)S(1)}, bf16[2,272,128]{2,1,0:T(8,128)(2,1)}, u32[]{:S(2)}) copy-start(bf16[2,272,128]{2,1,0:T(8,128)(2,1)} %join.1.refs_2_) | copy-start | bytes 417796
  19.1 4.4 %collective-permute-start.4 = (bf16[288,128]{1,0:T(8,128)(2,1)S(1)}, bf16[288,128]{1,0:T(8,128)(2,1)S(1)}, u32[]{:S(2)}, u32[]{:S(2)}) collective-permute-start(bf16[288,128]{1,0:T(8,128)(2,1)S(1)} %other_pair_sums.1), channel_id=1, source_target_pairs={{0,1},{1,0},{2,3},{3,2},{4,5},{5,4},{6,7},{7,6},{8,9},{9,8},{10,11... | collective-permute-start | bytes 221192 | tf_op jit(solution)/shard_map/ppermute | solution.py:376

commit v8 on v7

--- a/solution.py
+++ b/solution.py
@@ -168,6 +168,10 @@
         for a in range(per_vector // wide):
             first = (g * (per_vector // wide) + a) * rows
             store(first, part * (lane == a).astype(jnp.bfloat16))
+
+
+def hold_kernel(right_ref, out_ref):
+    out_ref[...] = right_ref[...]
 
 
 def join_kernel(right_ref, far_ref, out_ref):
@@ -332,13 +336,24 @@
     )
     far = lax.ppermute(right, GROUP, route(lambda r, c, q: (r ^ 2, c, q)))
     first = lax.ppermute(left, GROUP, route(lambda r, c, q: (2 * c + r // 2, r % 2, q)))
+    small = pltpu.CompilerParams(vmem_limit_bytes=16 * 1024 * 1024)
+    mine = pl.pallas_call(
+        hold_kernel,
+        out_shape=payload,
+        in_specs=[vmem],
+        out_specs=vmem,
+        compiler_params=small,
+        cost_estimate=pl.CostEstimate(flops=0, bytes_accessed=1 << 22, transcendentals=0),
+        name="hold",
+    )(right)
     held = pl.pallas_call(
         join_kernel,
         out_shape=jax.ShapeDtypeStruct((2,) + payload.shape, jnp.bfloat16),
         in_specs=[vmem] * 2,
         out_specs=vmem,
+        compiler_params=small,
         name="join",
-    )(right, far)
+    )(mine, far)
     passed = lax.ppermute(held, GROUP, route(lambda r, c, q: (r ^ 1, c, q)))
     second = lax.ppermute(first, GROUP, route(lambda r, c, q: (r, 1 - c, q)))
     weight, bias = pl.pallas_call(

time: 24.8 us -> 23.3 us (0.940)
  the two profiles are of different devices: /device:TPU:23 before, /device:TPU:15 now
where the time goes in v8:
time: 23.3 us; the launch traced here: 23 us
  starting transfers between devices  7.97 us (34%)
  Pallas kernels  6.67 us (29%)
  waiting for transfers between devices  5.8 us (25%)
  local copies, waits for them, and re-layouts  2.48 us (11%)
    ppermute x1, starting transfers between devices, direct_shards(): received = lax.ppermute(theirs, GROUP, route(lambda r, c, q: (r, c, 1 - q)))  3.61 us
    pallas_call x1, Pallas kernels, direct_shards(): pl.pallas_call(project_kernel, out_shape=(payload, payload), in_specs=[in...  3.45 us
    ppermute x1, waiting for transfers between devices, direct_shards(): lax.ppermute(left, GROUP, route(lambda r, c, q: (2 * c + r // 2, r % 2, q)))  3.17 us
    unnamed x6, local copies, waits for them, and re-layouts  2.48 us
    ppermute x1, starting transfers between devices, direct_shards(): far = lax.ppermute(right, GROUP, route(lambda r, c, q: (r ^ 2, c, q)))  2.37 us
    pallas_call x2, Pallas kernels, pair_sums(): pl.pallas_call(lambda *refs: pair_kernel(own, *refs), out_shape=jax.Shape...  1.96 us
    ppermute x1, starting transfers between devices, direct_shards(): lax.ppermute(left, GROUP, route(lambda r, c, q: (2 * c + r // 2, r % 2, q)))  1.91 us
    ppermute x1, waiting for transfers between devices, direct_shards(): second = lax.ppermute(first, GROUP, route(lambda r, c, q: (r, 1 - c, q)))  1.54 us
  transfers between devices with their start and end apart: 5, of which 3 were waited for; matrix products, arithmetic and copies ran while one was open for 0% of the time, Pallas kernels for 6%

profile of v8, /device:TPU:15, one launch (start us, length us, event | category | flops | bytes accessed | tf_op | source)
XLA Modules:
  0.0 23.0 jit_solution(16129489278780440885)
XLA Ops:
  0.0 3.5 %normalize_and_project.1 = (bf16[272,128]{1,0:T(8,128)(2,1)}, bf16[272,128]{1,0:T(8,128)(2,1)}) custom-call(s32[8]{0:T(128)} %pept_hbm.1, bf16[1024,256]{1,0:T(8,128)(2,1)} %bitcast.10, s32[8,128]{1,0:T(8,128)} %bitcast.13, f32[1,256]{1,0:T(1,128)} %bitcast.14, f32[1,256]{1,0:T(1,128)} %bitcast.15, bf16[32,256]{1,0:T(8,128)(2,1)} %bitcast.11, ...), custom_call_target="tpu_custom_call" | custom-call | tf_op jit(solution)/shard_map/normalize_and_project/pallas_call | solution.py:304
  3.5 2.4 %collective-permute-start.2 = (bf16[272,128]{1,0:T(8,128)(2,1)}, bf16[272,128]{1,0:T(8,128)(2,1)S(1)}, u32[]{:S(2)}, u32[]{:S(2)}) collective-permute-start(bf16[272,128]{1,0:T(8,128)(2,1)} %get-tuple-element.10.right_ref), channel_id=1, source_target_pairs={{0,8},{1,9},{2,10},{3,11},{4,12},{5,13},{6,14},{7,15},{8,0},{9,1},... | collective-permute-start | bytes 208904 | tf_op jit(solution)/shard_map/ppermute | solution.py:337
  5.8 1.9 %collective-permute-start = (bf16[272,128]{1,0:T(8,128)(2,1)}, bf16[272,128]{1,0:T(8,128)(2,1)S(1)}, u32[]{:S(2)}, u32[]{:S(2)}) collective-permute-start(bf16[272,128]{1,0:T(8,128)(2,1)} %get-tuple-element.9), channel_id=1, source_target_pairs={{0,0},{1,1},{2,8},{3,9},{4,2},{5,3},{6,10},{7,11},{8,4},{9,5},{10,... | collective-permute-start | bytes 208904 | tf_op jit(solution)/shard_map/ppermute | solution.py:338
  7.8 0.0 copy-start.1
  7.8 0.9 %copy-done.1 = bf16[272,128]{1,0:T(8,128)(2,1)S(1)} copy-done((bf16[272,128]{1,0:T(8,128)(2,1)S(1)}, bf16[272,128]{1,0:T(8,128)(2,1)}, u32[]{:S(2)}) %copy-start.1) | copy-done | bytes 69656
  8.6 1.1 %collective-permute-done.2.far_ref = bf16[272,128]{1,0:T(8,128)(2,1)S(1)} collective-permute-done((bf16[272,128]{1,0:T(8,128)(2,1)}, bf16[272,128]{1,0:T(8,128)(2,1)S(1)}, u32[]{:S(2)}, u32[]{:S(2)}) %collective-permute-start.2) | collective-permute-done | bytes 69664 | tf_op jit(solution)/shard_map/ppermute | solution.py:337
  9.7 0.1 collective-permute-start.3
  9.8 3.2 %collective-permute-done.refs_0_ = bf16[272,128]{1,0:T(8,128)(2,1)S(1)} collective-permute-done((bf16[272,128]{1,0:T(8,128)(2,1)}, bf16[272,128]{1,0:T(8,128)(2,1)S(1)}, u32[]{:S(2)}, u32[]{:S(2)}) %collective-permute-start) | collective-permute-done | bytes 69664 | tf_op jit(solution)/shard_map/ppermute | solution.py:338
  13.0 0.0 collective-permute-start.1
  13.0 0.0 copy-start
  13.0 0.9 %copy-done = bf16[1024,128]{1,0:T(8,128)(2,1)S(1)} copy-done((bf16[1024,128]{1,0:T(8,128)(2,1)S(1)}, bf16[1024,128]{1,0:T(8,128)(2,1)}, u32[]{:S(2)}) %copy-start) | copy-done | bytes 262168
  13.9 0.0 copy-start.2
  13.9 0.7 %copy-done.2 = f32[128]{0:T(128)S(1)} copy-done((f32[128]{0:T(128)S(1)}, f32[128]{0:T(128)}, u32[]{:S(2)}) %copy-start.2) | copy-done | bytes 536
  14.6 0.3 %keep.1 = (bf16[4096,256]{1,0:T(8,128)(2,1)S(1)}, f32[1,128]{1,0:T(1,128)S(1)}) custom-call(bf16[1024,128]{1,0:T(8,128)(2,1)S(1)} %copy-done, f32[1,128]{1,0:T(1,128)S(1)} %bitcast.9), custom_call_target="tpu_custom_call" | custom-call | bytes 4194304 | tf_op jit(solution)/shard_map/keep/pallas_call | solution.py:359
  14.9 1.5 %collective-permute-done.1.refs_1_ = bf16[272,128]{1,0:T(8,128)(2,1)S(1)} collective-permute-done((bf16[272,128]{1,0:T(8,128)(2,1)S(1)}, bf16[272,128]{1,0:T(8,128)(2,1)S(1)}, u32[]{:S(2)}, u32[]{:S(2)}) %collective-permute-start.1) | collective-permute-done | bytes 69664 | tf_op jit(solution)/shard_map/ppermute | solution.py:358
  16.4 0.0 collective-permute-done.3.refs_3_
  16.4 1.0 %other_pair_sums.1 = bf16[288,128]{1,0:T(8,128)(2,1)S(1)} custom-call(bf16[272,128]{1,0:T(8,128)(2,1)S(1)} %collective-permute-done.refs_0_, bf16[272,128]{1,0:T(8,128)(2,1)S(1)} %collective-permute-done.1.refs_1_, bf16[2,272,128]{2,1,0:T(8,128)(2,1)S(1)} %join.1.refs_2_, bf16[2,272,128]{2,1,0:T(8,128)(2,1)S(1)} %collective-permute-done.3.refs_3_, ...), custom_call_target="tpu_custom_call" | custom-call | flops 268435456 | bytes 1048576 | tf_op jit(solution)/shard_map/other_pair_sums/pallas_call | solution.py:373
  17.4 3.6 %collective-permute-start.4 = (bf16[288,128]{1,0:T(8,128)(2,1)S(1)}, bf16[288,128]{1,0:T(8,128)(2,1)S(1)}, u32[]{:S(2)}, u32[]{:S(2)}) collective-permute-start(bf16[288,128]{1,0:T(8,128)(2,1)S(1)} %other_pair_sums.1), channel_id=1, source_target_pairs={{0,1},{1,0},{2,3},{3,2},{4,5},{5,4},{6,7},{7,6},{8,9},{9,8},{10,11... | collective-permute-start | bytes 221192 | tf_op jit(solution)/shard_map/ppermute | solution.py:391
  21.0 1.0 %own_pair_sums.1.mine_ref = f32[288,128]{1,0:T(8,128)S(1)} custom-call(bf16[272,128]{1,0:T(8,128)(2,1)S(1)} %collective-permute-done.refs_0_, bf16[272,128]{1,0:T(8,128)(2,1)S(1)} %collective-permute-done.1.refs_1_, bf16[2,272,128]{2,1,0:T(8,128)(2,1)S(1)} %join.1.refs_2_, bf16[2,272,128]{2,1,0:T(8,128)(2,1)S(1)} %collective-permute-done.3.refs_3_, ...), custom_call_target="tpu_custom_call" | custom-call | flops 268435456 | bytes 1048576 | tf_op jit(solution)/shard_map/own_pair_sums/pallas_call | solution.py:373
  22.0 0.0 collective-permute-done.4.other_ref
  22.0 1.0 %divide.1 = bf16[16,16,128]{2,1,0:T(8,128)(2,1)} custom-call(f32[288,128]{1,0:T(8,128)S(1)} %own_pair_sums.1.mine_ref, bf16[288,128]{1,0:T(8,128)(2,1)S(1)} %collective-permute-done.4.other_ref), custom_call_target="tpu_custom_call" | custom-call | tf_op jit(solution)/shard_map/divide/pallas_call | solution.py:393
  (2 shorter events, 0.0 us)
Async XLA Ops:
  3.5 6.3 %collective-permute-start.2 = (bf16[272,128]{1,0:T(8,128)(2,1)}, bf16[272,128]{1,0:T(8,128)(2,1)S(1)}, u32[]{:S(2)}, u32[]{:S(2)}) collective-permute-start(bf16[272,128]{1,0:T(8,128)(2,1)} %get-tuple-element.10.right_ref), channel_id=1, source_target_pairs={{0,8},{1,9},{2,10},{3,11},{4,12},{5,13},{6,14},{7,15},{8,0},{9,1},... | collective-permute-start | bytes 208904 | tf_op jit(solution)/shard_map/ppermute | solution.py:337
  5.8 7.2 %collective-permute-start = (bf16[272,128]{1,0:T(8,128)(2,1)}, bf16[272,128]{1,0:T(8,128)(2,1)S(1)}, u32[]{:S(2)}, u32[]{:S(2)}) collective-permute-start(bf16[272,128]{1,0:T(8,128)(2,1)} %get-tuple-element.9), channel_id=1, source_target_pairs={{0,0},{1,1},{2,8},{3,9},{4,2},{5,3},{6,10},{7,11},{8,4},{9,5},{10,... | collective-permute-start | bytes 208904 | tf_op jit(solution)/shard_map/ppermute | solution.py:338
  7.8 0.9 %copy-start.1 = (bf16[272,128]{1,0:T(8,128)(2,1)S(1)}, bf16[272,128]{1,0:T(8,128)(2,1)}, u32[]{:S(2)}) copy-start(bf16[272,128]{1,0:T(8,128)(2,1)} %get-tuple-element.10.right_ref) | copy-start | bytes 208900
  9.7 6.7 %collective-permute-start.3 = (bf16[2,272,128]{2,1,0:T(8,128)(2,1)S(1)}, bf16[2,272,128]{2,1,0:T(8,128)(2,1)S(1)}, u32[]{:S(2)}, u32[]{:S(2)}) collective-permute-start(bf16[2,272,128]{2,1,0:T(8,128)(2,1)S(1)} %join.1.refs_2_), channel_id=1, source_target_pairs={{0,4},{1,5},{2,6},{3,7},{4,0},{5,1},{6,2},{7,3},{8,12},{9,13},{10,... | collective-permute-start | bytes 417800 | tf_op jit(solution)/shard_map/ppermute | solution.py:357
  13.0 3.4 %collective-permute-start.1 = (bf16[272,128]{1,0:T(8,128)(2,1)S(1)}, bf16[272,128]{1,0:T(8,128)(2,1)S(1)}, u32[]{:S(2)}, u32[]{:S(2)}) collective-permute-start(bf16[272,128]{1,0:T(8,128)(2,1)S(1)} %collective-permute-done.refs_0_), channel_id=1, source_target_pairs={{0,2},{1,3},{2,0},{3,1},{4,6},{5,7},{6,4},{7,5},{8,10},{9,11},{10,... | collective-permute-start | bytes 208904 | tf_op jit(solution)/shard_map/ppermute | solution.py:358
  13.0 1.0 %copy-start = (bf16[1024,128]{1,0:T(8,128)(2,1)S(1)}, bf16[1024,128]{1,0:T(8,128)(2,1)}, u32[]{:S(2)}) copy-start(bf16[1024,128]{1,0:T(8,128)(2,1)} %w_ref.1) | copy-start | bytes 786436
  13.9 0.7 %copy-start.2 = (f32[128]{0:T(128)S(1)}, f32[128]{0:T(128)}, u32[]{:S(2)}) copy-start(f32[128]{0:T(128)} %param.21) | copy-start | bytes 1540
  17.4 4.6 %collective-permute-start.4 = (bf16[288,128]{1,0:T(8,128)(2,1)S(1)}, bf16[288,128]{1,0:T(8,128)(2,1)S(1)}, u32[]{:S(2)}, u32[]{:S(2)}) collective-permute-start(bf16[288,128]{1,0:T(8,128)(2,1)S(1)} %other_pair_sums.1), channel_id=1, source_target_pairs={{0,1},{1,0},{2,3},{3,2},{4,5},{5,4},{6,7},{7,6},{8,9},{9,8},{10,11... | collective-permute-start | bytes 221192 | tf_op jit(solution)/shard_map/ppermute | solution.py:391

commit v9 on v8

--- a/solution.py
+++ b/solution.py
@@ -335,7 +335,7 @@
         rhs_linear_constant.reshape(1, hidden),
     )
     far = lax.ppermute(right, GROUP, route(lambda r, c, q: (r ^ 2, c, q)))
-    first = lax.ppermute(left, GROUP, route(lambda r, c, q: (2 * c + r // 2, r % 2, q)))
+    first = lax.ppermute(left, GROUP, route(lambda r, c, q: (2 * c + r // 2, 1 - r % 2, q)))
     small = pltpu.CompilerParams(vmem_limit_bytes=16 * 1024 * 1024)
     mine = pl.pallas_call(
         hold_kernel,
@@ -385,7 +385,7 @@
                 flops=2 * pairs * hidden * 128 * width, bytes_accessed=1 << 20, transcendentals=0
             ),
             name="own_pair_sums" if own else "other_pair_sums",
-        )(first, second, held, passed, weight, bias)
+        )(second, first, held, passed, weight, bias)
 
     theirs = pair_sums(False, jnp.bfloat16)
     received = lax.ppermute(theirs, GROUP, route(lambda r, c, q: (r, c, 1 - q)))

time: 23.3 us -> 22.2 us (0.953)
  the two profiles are of different devices: /device:TPU:15 before, /device:TPU:21 now
where the time goes in v9:
time: 22.2 us; the launch traced here: 22 us
  starting transfers between devices  8.55 us (39%)
  Pallas kernels  6.67 us (30%)
  waiting for transfers between devices  4.22 us (19%)
  local copies, waits for them, and re-layouts  2.49 us (11%)
    pallas_call x1, Pallas kernels, direct_shards(): pl.pallas_call(project_kernel, out_shape=(payload, payload), in_specs=[in...  3.45 us
    ppermute x1, starting transfers between devices, direct_shards(): lax.ppermute(left, GROUP, route(lambda r, c, q: (2 * c + r // 2, 1 - r %...  3.35 us
    ppermute x1, starting transfers between devices, direct_shards(): passed = lax.ppermute(held, GROUP, route(lambda r, c, q: (r ^ 1, c, q)))  3.31 us
    ppermute x1, waiting for transfers between devices, direct_shards(): lax.ppermute(left, GROUP, route(lambda r, c, q: (2 * c + r // 2, 1 - r %...  2.96 us
    unnamed x6, local copies, waits for them, and re-layouts  2.49 us
    pallas_call x2, Pallas kernels, pair_sums(): pl.pallas_call(lambda *refs: pair_kernel(own, *refs), out_shape=jax.Shape...  1.96 us
    ppermute x1, starting transfers between devices, direct_shards(): received = lax.ppermute(theirs, GROUP, route(lambda r, c, q: (r, c, 1 - q)))  1.71 us
    ppermute x1, waiting for transfers between devices, direct_shards(): second = lax.ppermute(first, GROUP, route(lambda r, c, q: (r, 1 - c, q)))  1.22 us
  transfers between devices with their start and end apart: 5, of which 2 were waited for; matrix products, arithmetic and copies ran while one was open for 0% of the time, Pallas kernels for 6%

profile of v9, /device:TPU:21, one launch (start us, length us, event | category | flops | bytes accessed | tf_op | source)
XLA Modules:
  0.0 22.0 jit_solution(3736351049781474811)
XLA Ops:
  0.0 3.5 %normalize_and_project.1 = (bf16[272,128]{1,0:T(8,128)(2,1)}, bf16[272,128]{1,0:T(8,128)(2,1)}) custom-call(s32[8]{0:T(128)} %pept_hbm.1, bf16[1024,256]{1,0:T(8,128)(2,1)} %bitcast.10, s32[8,128]{1,0:T(8,128)} %bitcast.13, f32[1,256]{1,0:T(1,128)} %bitcast.14, f32[1,256]{1,0:T(1,128)} %bitcast.15, bf16[32,256]{1,0:T(8,128)(2,1)} %bitcast.11, ...), custom_call_target="tpu_custom_call" | custom-call | tf_op jit(solution)/shard_map/normalize_and_project/pallas_call | solution.py:304
  3.5 0.1 collective-permute-start.2
  3.6 3.4 %collective-permute-start = (bf16[272,128]{1,0:T(8,128)(2,1)}, bf16[272,128]{1,0:T(8,128)(2,1)S(1)}, u32[]{:S(2)}, u32[]{:S(2)}) collective-permute-start(bf16[272,128]{1,0:T(8,128)(2,1)} %get-tuple-element.9), channel_id=1, source_target_pairs={{0,2},{1,3},{2,10},{3,11},{4,0},{5,1},{6,8},{7,9},{8,6},{9,7},{10,... | collective-permute-start | bytes 208904 | tf_op jit(solution)/shard_map/ppermute | solution.py:338
  6.9 0.0 copy-start.1
  6.9 0.9 %copy-done.1 = bf16[272,128]{1,0:T(8,128)(2,1)S(1)} copy-done((bf16[272,128]{1,0:T(8,128)(2,1)S(1)}, bf16[272,128]{1,0:T(8,128)(2,1)}, u32[]{:S(2)}) %copy-start.1) | copy-done | bytes 69656
  7.8 0.0 collective-permute-done.2.far_ref
  7.9 3.3 %collective-permute-start.3 = (bf16[2,272,128]{2,1,0:T(8,128)(2,1)S(1)}, bf16[2,272,128]{2,1,0:T(8,128)(2,1)S(1)}, u32[]{:S(2)}, u32[]{:S(2)}) collective-permute-start(bf16[2,272,128]{2,1,0:T(8,128)(2,1)S(1)} %join.1.refs_2_), channel_id=1, source_target_pairs={{0,4},{1,5},{2,6},{3,7},{4,0},{5,1},{6,2},{7,3},{8,12},{9,13},{10,... | collective-permute-start | bytes 417800 | tf_op jit(solution)/shard_map/ppermute | solution.py:357
  11.2 3.0 %collective-permute-done.refs_1_ = bf16[272,128]{1,0:T(8,128)(2,1)S(1)} collective-permute-done((bf16[272,128]{1,0:T(8,128)(2,1)}, bf16[272,128]{1,0:T(8,128)(2,1)S(1)}, u32[]{:S(2)}, u32[]{:S(2)}) %collective-permute-start) | collective-permute-done | bytes 69664 | tf_op jit(solution)/shard_map/ppermute | solution.py:338
  14.1 0.1 collective-permute-start.1
  14.2 0.0 copy-start
  14.2 0.9 %copy-done = bf16[1024,128]{1,0:T(8,128)(2,1)S(1)} copy-done((bf16[1024,128]{1,0:T(8,128)(2,1)S(1)}, bf16[1024,128]{1,0:T(8,128)(2,1)}, u32[]{:S(2)}) %copy-start) | copy-done | bytes 262168
  15.2 0.0 copy-start.2
  15.2 0.7 %copy-done.2 = f32[128]{0:T(128)S(1)} copy-done((f32[128]{0:T(128)S(1)}, f32[128]{0:T(128)}, u32[]{:S(2)}) %copy-start.2) | copy-done | bytes 536
  15.8 0.3 %keep.1 = (bf16[4096,256]{1,0:T(8,128)(2,1)S(1)}, f32[1,128]{1,0:T(1,128)S(1)}) custom-call(bf16[1024,128]{1,0:T(8,128)(2,1)S(1)} %copy-done, f32[1,128]{1,0:T(1,128)S(1)} %bitcast.9), custom_call_target="tpu_custom_call" | custom-call | bytes 4194304 | tf_op jit(solution)/shard_map/keep/pallas_call | solution.py:359
  16.1 1.2 %collective-permute-done.1.refs_0_ = bf16[272,128]{1,0:T(8,128)(2,1)S(1)} collective-permute-done((bf16[272,128]{1,0:T(8,128)(2,1)S(1)}, bf16[272,128]{1,0:T(8,128)(2,1)S(1)}, u32[]{:S(2)}, u32[]{:S(2)}) %collective-permute-start.1) | collective-permute-done | bytes 69664 | tf_op jit(solution)/shard_map/ppermute | solution.py:358
  17.3 0.0 collective-permute-done.3.refs_3_
  17.3 1.0 %other_pair_sums.1 = bf16[288,128]{1,0:T(8,128)(2,1)S(1)} custom-call(bf16[272,128]{1,0:T(8,128)(2,1)S(1)} %collective-permute-done.1.refs_0_, bf16[272,128]{1,0:T(8,128)(2,1)S(1)} %collective-permute-done.refs_1_, bf16[2,272,128]{2,1,0:T(8,128)(2,1)S(1)} %join.1.refs_2_, bf16[2,272,128]{2,1,0:T(8,128)(2,1)S(1)} %collective-permute-done.3.refs_3_, ...), custom_call_target="tpu_custom_call" | custom-call | flops 268435456 | bytes 1048576 | tf_op jit(solution)/shard_map/other_pair_sums/pallas_call | solution.py:373
  18.3 1.7 %collective-permute-start.4 = (bf16[288,128]{1,0:T(8,128)(2,1)S(1)}, bf16[288,128]{1,0:T(8,128)(2,1)S(1)}, u32[]{:S(2)}, u32[]{:S(2)}) collective-permute-start(bf16[288,128]{1,0:T(8,128)(2,1)S(1)} %other_pair_sums.1), channel_id=1, source_target_pairs={{0,1},{1,0},{2,3},{3,2},{4,5},{5,4},{6,7},{7,6},{8,9},{9,8},{10,11... | collective-permute-start | bytes 221192 | tf_op jit(solution)/shard_map/ppermute | solution.py:391
  20.0 1.0 %own_pair_sums.1.mine_ref = f32[288,128]{1,0:T(8,128)S(1)} custom-call(bf16[272,128]{1,0:T(8,128)(2,1)S(1)} %collective-permute-done.1.refs_0_, bf16[272,128]{1,0:T(8,128)(2,1)S(1)} %collective-permute-done.refs_1_, bf16[2,272,128]{2,1,0:T(8,128)(2,1)S(1)} %join.1.refs_2_, bf16[2,272,128]{2,1,0:T(8,128)(2,1)S(1)} %collective-permute-done.3.refs_3_, ...), custom_call_target="tpu_custom_call" | custom-call | flops 268435456 | bytes 1048576 | tf_op jit(solution)/shard_map/own_pair_sums/pallas_call | solution.py:373
  21.0 0.0 collective-permute-done.4.other_ref
  21.0 1.0 %divide.1 = bf16[16,16,128]{2,1,0:T(8,128)(2,1)} custom-call(f32[288,128]{1,0:T(8,128)S(1)} %own_pair_sums.1.mine_ref, bf16[288,128]{1,0:T(8,128)(2,1)S(1)} %collective-permute-done.4.other_ref), custom_call_target="tpu_custom_call" | custom-call | tf_op jit(solution)/shard_map/divide/pallas_call | solution.py:393
  (2 shorter events, 0.0 us)
Async XLA Ops:
  3.5 4.4 %collective-permute-start.2 = (bf16[272,128]{1,0:T(8,128)(2,1)}, bf16[272,128]{1,0:T(8,128)(2,1)S(1)}, u32[]{:S(2)}, u32[]{:S(2)}) collective-permute-start(bf16[272,128]{1,0:T(8,128)(2,1)} %get-tuple-element.10.right_ref), channel_id=1, source_target_pairs={{0,8},{1,9},{2,10},{3,11},{4,12},{5,13},{6,14},{7,15},{8,0},{9,1},... | collective-permute-start | bytes 208904 | tf_op jit(solution)/shard_map/ppermute | solution.py:337
  3.6 10.6 %collective-permute-start = (bf16[272,128]{1,0:T(8,128)(2,1)}, bf16[272,128]{1,0:T(8,128)(2,1)S(1)}, u32[]{:S(2)}, u32[]{:S(2)}) collective-permute-start(bf16[272,128]{1,0:T(8,128)(2,1)} %get-tuple-element.9), channel_id=1, source_target_pairs={{0,2},{1,3},{2,10},{3,11},{4,0},{5,1},{6,8},{7,9},{8,6},{9,7},{10,... | collective-permute-start | bytes 208904 | tf_op jit(solution)/shard_map/ppermute | solution.py:338
  6.9 0.9 %copy-start.1 = (bf16[272,128]{1,0:T(8,128)(2,1)S(1)}, bf16[272,128]{1,0:T(8,128)(2,1)}, u32[]{:S(2)}) copy-start(bf16[272,128]{1,0:T(8,128)(2,1)} %get-tuple-element.10.right_ref) | copy-start | bytes 208900
  7.9 9.4 %collective-permute-start.3 = (bf16[2,272,128]{2,1,0:T(8,128)(2,1)S(1)}, bf16[2,272,128]{2,1,0:T(8,128)(2,1)S(1)}, u32[]{:S(2)}, u32[]{:S(2)}) collective-permute-start(bf16[2,272,128]{2,1,0:T(8,128)(2,1)S(1)} %join.1.refs_2_), channel_id=1, source_target_pairs={{0,4},{1,5},{2,6},{3,7},{4,0},{5,1},{6,2},{7,3},{8,12},{9,13},{10,... | collective-permute-start | bytes 417800 | tf_op jit(solution)/shard_map/ppermute | solution.py:357
  14.1 3.2 %collective-permute-start.1 = (bf16[272,128]{1,0:T(8,128)(2,1)S(1)}, bf16[272,128]{1,0:T(8,128)(2,1)S(1)}, u32[]{:S(2)}, u32[]{:S(2)}) collective-permute-start(bf16[272,128]{1,0:T(8,128)(2,1)S(1)} %collective-permute-done.refs_1_), channel_id=1, source_target_pairs={{0,2},{1,3},{2,0},{3,1},{4,6},{5,7},{6,4},{7,5},{8,10},{9,11},{10,... | collective-permute-start | bytes 208904 | tf_op jit(solution)/shard_map/ppermute | solution.py:358
  14.2 0.9 %copy-start = (bf16[1024,128]{1,0:T(8,128)(2,1)S(1)}, bf16[1024,128]{1,0:T(8,128)(2,1)}, u32[]{:S(2)}) copy-start(bf16[1024,128]{1,0:T(8,128)(2,1)} %w_ref.1) | copy-start | bytes 786436
  15.2 0.7 %copy-start.2 = (f32[128]{0:T(128)S(1)}, f32[128]{0:T(128)}, u32[]{:S(2)}) copy-start(f32[128]{0:T(128)} %param.21) | copy-start | bytes 1540
  18.3 2.7 %collective-permute-start.4 = (bf16[288,128]{1,0:T(8,128)(2,1)S(1)}, bf16[288,128]{1,0:T(8,128)(2,1)S(1)}, u32[]{:S(2)}, u32[]{:S(2)}) collective-permute-start(bf16[288,128]{1,0:T(8,128)(2,1)S(1)} %other_pair_sums.1), channel_id=1, source_target_pairs={{0,1},{1,0},{2,3},{3,2},{4,5},{5,4},{6,7},{7,6},{8,9},{9,8},{10,11... | collective-permute-start | bytes 221192 | tf_op jit(solution)/shard_map/ppermute | solution.py:391

commit v10 on v9

--- a/solution.py
+++ b/solution.py
@@ -10,7 +10,7 @@
 GROUP = ("row", "col", "seq")
 NT = (((1,), (1,)), ((), ()))
 MASK_ROWS = 16
-WIDE = 2
+WIDE = 4
 
 
 def from_root(x, axis, root):
@@ -318,7 +318,7 @@
             pltpu.VMEM((1, hidden), jnp.float32),
             pltpu.VMEM((sequences * residues, 128), jnp.float32),
             pltpu.VMEM((rows, sequences), jnp.float32),
-            pltpu.SemaphoreType.DMA((4,)),
+            pltpu.SemaphoreType.DMA((8,)),
             pltpu.SemaphoreType.DMA((8,)),
         ],
         compiler_params=pltpu.CompilerParams(vmem_limit_bytes=60 * 1024 * 1024),

time: 22.2 us -> 23.6 us (1.063)
  the two profiles are of different devices: /device:TPU:21 before, /device:TPU:17 now
where the time goes in v10:
time: 23.6 us; the launch traced here: 23.4 us
  starting transfers between devices  8.53 us (36%)
  Pallas kernels  8.38 us (36%)
  waiting for transfers between devices  3.95 us (17%)
  local copies, waits for them, and re-layouts  2.49 us (11%)
    pallas_call x1, Pallas kernels, direct_shards(): pl.pallas_call(project_kernel, out_shape=(payload, payload), in_specs=[in...  4.53 us
    ppermute x1, starting transfers between devices, direct_shards(): lax.ppermute(left, GROUP, route(lambda r, c, q: (2 * c + r // 2, 1 - r %...  3.39 us
    ppermute x1, starting transfers between devices, direct_shards(): passed = lax.ppermute(held, GROUP, route(lambda r, c, q: (r ^ 1, c, q)))  3.31 us
    ppermute x1, waiting for transfers between devices, direct_shards(): lax.ppermute(left, GROUP, route(lambda r, c, q: (2 * c + r // 2, 1 - r %...  2.95 us
    unnamed x6, local copies, waits for them, and re-layouts  2.49 us
    pallas_call x2, Pallas kernels, pair_sums(): pl.pallas_call(lambda *refs: pair_kernel(own, *refs), out_shape=jax.Shape...  2.33 us
    ppermute x1, starting transfers between devices, direct_shards(): received = lax.ppermute(theirs, GROUP, route(lambda r, c, q: (r, c, 1 - q)))  1.7 us
    pallas_call x1, Pallas kernels, direct_shards(): pl.pallas_call(finish_kernel, out_shape=jax.ShapeDtypeStruct((2 * residue...  0.97 us
  transfers between devices with their start and end apart: 5, of which 2 were waited for; matrix products, arithmetic and copies ran while one was open for 0% of the time, Pallas kernels for 7%

profile of v10, /device:TPU:17, one launch (start us, length us, event | category | flops | bytes accessed | tf_op | source)
XLA Modules:
  0.0 23.4 jit_solution(4912866991471440376)
XLA Ops:
  0.0 4.5 %normalize_and_project.1 = (bf16[272,128]{1,0:T(8,128)(2,1)}, bf16[272,128]{1,0:T(8,128)(2,1)}) custom-call(s32[8]{0:T(128)} %pept_hbm.1, bf16[1024,256]{1,0:T(8,128)(2,1)} %bitcast.10, s32[8,128]{1,0:T(8,128)} %bitcast.13, f32[1,256]{1,0:T(1,128)} %bitcast.14, f32[1,256]{1,0:T(1,128)} %bitcast.15, bf16[32,256]{1,0:T(8,128)(2,1)} %bitcast.11, ...), custom_call_target="tpu_custom_call" | custom-call | tf_op jit(solution)/shard_map/normalize_and_project/pallas_call | solution.py:304
  4.5 0.1 collective-permute-start.2
  4.6 3.4 %collective-permute-start = (bf16[272,128]{1,0:T(8,128)(2,1)}, bf16[272,128]{1,0:T(8,128)(2,1)S(1)}, u32[]{:S(2)}, u32[]{:S(2)}) collective-permute-start(bf16[272,128]{1,0:T(8,128)(2,1)} %get-tuple-element.9), channel_id=1, source_target_pairs={{0,2},{1,3},{2,10},{3,11},{4,0},{5,1},{6,8},{7,9},{8,6},{9,7},{10,... | collective-permute-start | bytes 208904 | tf_op jit(solution)/shard_map/ppermute | solution.py:338
  8.0 0.0 copy-start.1
  8.0 0.9 %copy-done.1 = bf16[272,128]{1,0:T(8,128)(2,1)S(1)} copy-done((bf16[272,128]{1,0:T(8,128)(2,1)S(1)}, bf16[272,128]{1,0:T(8,128)(2,1)}, u32[]{:S(2)}) %copy-start.1) | copy-done | bytes 69656
  8.9 0.0 collective-permute-done.2.far_ref
  9.0 3.3 %collective-permute-start.3 = (bf16[2,272,128]{2,1,0:T(8,128)(2,1)S(1)}, bf16[2,272,128]{2,1,0:T(8,128)(2,1)S(1)}, u32[]{:S(2)}, u32[]{:S(2)}) collective-permute-start(bf16[2,272,128]{2,1,0:T(8,128)(2,1)S(1)} %join.1.refs_2_), channel_id=1, source_target_pairs={{0,4},{1,5},{2,6},{3,7},{4,0},{5,1},{6,2},{7,3},{8,12},{9,13},{10,... | collective-permute-start | bytes 417800 | tf_op jit(solution)/shard_map/ppermute | solution.py:357
  12.3 3.0 %collective-permute-done.refs_1_ = bf16[272,128]{1,0:T(8,128)(2,1)S(1)} collective-permute-done((bf16[272,128]{1,0:T(8,128)(2,1)}, bf16[272,128]{1,0:T(8,128)(2,1)S(1)}, u32[]{:S(2)}, u32[]{:S(2)}) %collective-permute-start) | collective-permute-done | bytes 69664 | tf_op jit(solution)/shard_map/ppermute | solution.py:338
  15.2 0.1 collective-permute-start.1
  15.3 0.0 copy-start
  15.3 0.9 %copy-done = bf16[1024,128]{1,0:T(8,128)(2,1)S(1)} copy-done((bf16[1024,128]{1,0:T(8,128)(2,1)S(1)}, bf16[1024,128]{1,0:T(8,128)(2,1)}, u32[]{:S(2)}) %copy-start) | copy-done | bytes 262168
  16.2 0.0 copy-start.2
  16.2 0.7 %copy-done.2 = f32[128]{0:T(128)S(1)} copy-done((f32[128]{0:T(128)S(1)}, f32[128]{0:T(128)}, u32[]{:S(2)}) %copy-start.2) | copy-done | bytes 536
  16.9 0.5 %keep.1 = (bf16[4096,512]{1,0:T(8,128)(2,1)S(1)}, f32[1,128]{1,0:T(1,128)S(1)}) custom-call(bf16[1024,128]{1,0:T(8,128)(2,1)S(1)} %copy-done, f32[1,128]{1,0:T(1,128)S(1)} %bitcast.9), custom_call_target="tpu_custom_call" | custom-call | bytes 4194304 | tf_op jit(solution)/shard_map/keep/pallas_call | solution.py:359
  17.4 1.0 %collective-permute-done.1.refs_0_ = bf16[272,128]{1,0:T(8,128)(2,1)S(1)} collective-permute-done((bf16[272,128]{1,0:T(8,128)(2,1)S(1)}, bf16[272,128]{1,0:T(8,128)(2,1)S(1)}, u32[]{:S(2)}, u32[]{:S(2)}) %collective-permute-start.1) | collective-permute-done | bytes 69664 | tf_op jit(solution)/shard_map/ppermute | solution.py:358
  18.4 0.0 collective-permute-done.3.refs_3_
  18.4 1.2 %other_pair_sums.1 = bf16[288,128]{1,0:T(8,128)(2,1)S(1)} custom-call(bf16[272,128]{1,0:T(8,128)(2,1)S(1)} %collective-permute-done.1.refs_0_, bf16[272,128]{1,0:T(8,128)(2,1)S(1)} %collective-permute-done.refs_1_, bf16[2,272,128]{2,1,0:T(8,128)(2,1)S(1)} %join.1.refs_2_, bf16[2,272,128]{2,1,0:T(8,128)(2,1)S(1)} %collective-permute-done.3.refs_3_, ...), custom_call_target="tpu_custom_call" | custom-call | flops 268435456 | bytes 1048576 | tf_op jit(solution)/shard_map/other_pair_sums/pallas_call | solution.py:373
  19.6 1.7 %collective-permute-start.4 = (bf16[288,128]{1,0:T(8,128)(2,1)S(1)}, bf16[288,128]{1,0:T(8,128)(2,1)S(1)}, u32[]{:S(2)}, u32[]{:S(2)}) collective-permute-start(bf16[288,128]{1,0:T(8,128)(2,1)S(1)} %other_pair_sums.1), channel_id=1, source_target_pairs={{0,1},{1,0},{2,3},{3,2},{4,5},{5,4},{6,7},{7,6},{8,9},{9,8},{10,11... | collective-permute-start | bytes 221192 | tf_op jit(solution)/shard_map/ppermute | solution.py:391
  21.3 1.2 %own_pair_sums.1.mine_ref = f32[288,128]{1,0:T(8,128)S(1)} custom-call(bf16[272,128]{1,0:T(8,128)(2,1)S(1)} %collective-permute-done.1.refs_0_, bf16[272,128]{1,0:T(8,128)(2,1)S(1)} %collective-permute-done.refs_1_, bf16[2,272,128]{2,1,0:T(8,128)(2,1)S(1)} %join.1.refs_2_, bf16[2,272,128]{2,1,0:T(8,128)(2,1)S(1)} %collective-permute-done.3.refs_3_, ...), custom_call_target="tpu_custom_call" | custom-call | flops 268435456 | bytes 1048576 | tf_op jit(solution)/shard_map/own_pair_sums/pallas_call | solution.py:373
  22.4 0.0 collective-permute-done.4.other_ref
  22.4 1.0 %divide.1 = bf16[16,16,128]{2,1,0:T(8,128)(2,1)} custom-call(f32[288,128]{1,0:T(8,128)S(1)} %own_pair_sums.1.mine_ref, bf16[288,128]{1,0:T(8,128)(2,1)S(1)} %collective-permute-done.4.other_ref), custom_call_target="tpu_custom_call" | custom-call | tf_op jit(solution)/shard_map/divide/pallas_call | solution.py:393
  (2 shorter events, 0.0 us)
Async XLA Ops:
  4.5 4.4 %collective-permute-start.2 = (bf16[272,128]{1,0:T(8,128)(2,1)}, bf16[272,128]{1,0:T(8,128)(2,1)S(1)}, u32[]{:S(2)}, u32[]{:S(2)}) collective-permute-start(bf16[272,128]{1,0:T(8,128)(2,1)} %get-tuple-element.10.right_ref), channel_id=1, source_target_pairs={{0,8},{1,9},{2,10},{3,11},{4,12},{5,13},{6,14},{7,15},{8,0},{9,1},... | collective-permute-start | bytes 208904 | tf_op jit(solution)/shard_map/ppermute | solution.py:337
  4.6 10.6 %collective-permute-start = (bf16[272,128]{1,0:T(8,128)(2,1)}, bf16[272,128]{1,0:T(8,128)(2,1)S(1)}, u32[]{:S(2)}, u32[]{:S(2)}) collective-permute-start(bf16[272,128]{1,0:T(8,128)(2,1)} %get-tuple-element.9), channel_id=1, source_target_pairs={{0,2},{1,3},{2,10},{3,11},{4,0},{5,1},{6,8},{7,9},{8,6},{9,7},{10,... | collective-permute-start | bytes 208904 | tf_op jit(solution)/shard_map/ppermute | solution.py:338
  8.0 0.9 %copy-start.1 = (bf16[272,128]{1,0:T(8,128)(2,1)S(1)}, bf16[272,128]{1,0:T(8,128)(2,1)}, u32[]{:S(2)}) copy-start(bf16[272,128]{1,0:T(8,128)(2,1)} %get-tuple-element.10.right_ref) | copy-start | bytes 208900
  9.0 9.4 %collective-permute-start.3 = (bf16[2,272,128]{2,1,0:T(8,128)(2,1)S(1)}, bf16[2,272,128]{2,1,0:T(8,128)(2,1)S(1)}, u32[]{:S(2)}, u32[]{:S(2)}) collective-permute-start(bf16[2,272,128]{2,1,0:T(8,128)(2,1)S(1)} %join.1.refs_2_), channel_id=1, source_target_pairs={{0,4},{1,5},{2,6},{3,7},{4,0},{5,1},{6,2},{7,3},{8,12},{9,13},{10,... | collective-permute-start | bytes 417800 | tf_op jit(solution)/shard_map/ppermute | solution.py:357
  15.2 3.2 %collective-permute-start.1 = (bf16[272,128]{1,0:T(8,128)(2,1)S(1)}, bf16[272,128]{1,0:T(8,128)(2,1)S(1)}, u32[]{:S(2)}, u32[]{:S(2)}) collective-permute-start(bf16[272,128]{1,0:T(8,128)(2,1)S(1)} %collective-permute-done.refs_1_), channel_id=1, source_target_pairs={{0,2},{1,3},{2,0},{3,1},{4,6},{5,7},{6,4},{7,5},{8,10},{9,11},{10,... | collective-permute-start | bytes 208904 | tf_op jit(solution)/shard_map/ppermute | solution.py:358
  15.3 0.9 %copy-start = (bf16[1024,128]{1,0:T(8,128)(2,1)S(1)}, bf16[1024,128]{1,0:T(8,128)(2,1)}, u32[]{:S(2)}) copy-start(bf16[1024,128]{1,0:T(8,128)(2,1)} %w_ref.1) | copy-start | bytes 786436
  16.2 0.7 %copy-start.2 = (f32[128]{0:T(128)S(1)}, f32[128]{0:T(128)}, u32[]{:S(2)}) copy-start(f32[128]{0:T(128)} %param.21) | copy-start | bytes 1540
  19.6 2.9 %collective-permute-start.4 = (bf16[288,128]{1,0:T(8,128)(2,1)S(1)}, bf16[288,128]{1,0:T(8,128)(2,1)S(1)}, u32[]{:S(2)}, u32[]{:S(2)}) collective-permute-start(bf16[288,128]{1,0:T(8,128)(2,1)S(1)} %other_pair_sums.1), channel_id=1, source_target_pairs={{0,1},{1,0},{2,3},{3,2},{4,5},{5,4},{6,7},{7,6},{8,9},{9,8},{10,11... | collective-permute-start | bytes 221192 | tf_op jit(solution)/shard_map/ppermute | solution.py:391

commit v11 on v9

--- a/solution.py
+++ b/solution.py
@@ -128,26 +128,23 @@
         (bl_hbm, bl_ref), (br_hbm, br_ref), (occ_hbm, occ_ref), (pept_hbm, pept_ref),
     )
     copies = [pltpu.make_async_copy(a, b, sems.at[n]) for n, (a, b) in enumerate(pairs)]
-    x_copies[0].start()
-    for copy in copies:
-        copy.start()
-    for copy in x_copies[1:]:
+    for copy in x_copies + copies:
         copy.start()
     for copy in copies:
         copy.wait()
     weight = jnp.concatenate([wl_ref[...], wr_ref[...]], axis=0)
     bias = jnp.concatenate([bl_ref[...], br_ref[...]], axis=1)
-    for n, copy in enumerate(x_copies):
+    for copy in x_copies:
         copy.wait()
-        x = x_ref[n * size : (n + 1) * size, :].astype(jnp.float32)
-        average = jnp.mean(x, axis=-1, keepdims=True)
-        centred = x - average
-        spread = jnp.mean(jnp.square(centred), axis=-1, keepdims=True)
-        normed = (centred * lax.rsqrt(spread + 1e-05) * gain_ref[...] + shift_ref[...]).astype(
-            jnp.bfloat16
-        )
-        y = lax.dot_general(normed, weight, NT, preferred_element_type=jnp.float32) + bias
-        y_ref[n * size : (n + 1) * size, : 2 * hidden] = y
+    x = x_ref[...].astype(jnp.float32)
+    average = jnp.mean(x, axis=-1, keepdims=True)
+    centred = x - average
+    spread = jnp.mean(jnp.square(centred), axis=-1, keepdims=True)
+    normed = (centred * lax.rsqrt(spread + 1e-05) * gain_ref[...] + shift_ref[...]).astype(
+        jnp.bfloat16
+    )
+    y = lax.dot_general(normed, weight, NT, preferred_element_type=jnp.float32) + bias
+    y_ref[:, : 2 * hidden] = y
     for i in range(residues):
         live = (occ_ref[i : i + 1, :] * pept_ref[i]).astype(jnp.float32)
         part = y_ref[pl.ds(i, sequences, stride=residues), :].T[: 2 * hidden] * live

time: 22.2 us -> 21.5 us (0.968)
  the two profiles are of different devices: /device:TPU:21 before, /device:TPU:17 now
where the time goes in v11:
time: 21.5 us; the launch traced here: 21.2 us
  starting transfers between devices  8.54 us (40%)
  Pallas kernels  5.91 us (27%)
  waiting for transfers between devices  4.22 us (20%)
  local copies, waits for them, and re-layouts  2.49 us (12%)
    ppermute x1, starting transfers between devices, direct_shards(): lax.ppermute(left, GROUP, route(lambda r, c, q: (2 * c + r // 2, 1 - r %...  3.39 us
    ppermute x1, starting transfers between devices, direct_shards(): passed = lax.ppermute(held, GROUP, route(lambda r, c, q: (r ^ 1, c, q)))  3.31 us
    ppermute x1, waiting for transfers between devices, direct_shards(): lax.ppermute(left, GROUP, route(lambda r, c, q: (2 * c + r // 2, 1 - r %...  2.96 us
    pallas_call x1, Pallas kernels, direct_shards(): pl.pallas_call(project_kernel, out_shape=(payload, payload), in_specs=[in...  2.69 us
    unnamed x6, local copies, waits for them, and re-layouts  2.49 us
    pallas_call x2, Pallas kernels, pair_sums(): pl.pallas_call(lambda *refs: pair_kernel(own, *refs), out_shape=jax.Shape...  1.96 us
    ppermute x1, starting transfers between devices, direct_shards(): received = lax.ppermute(theirs, GROUP, route(lambda r, c, q: (r, c, 1 - q)))  1.71 us
    ppermute x1, waiting for transfers between devices, direct_shards(): second = lax.ppermute(first, GROUP, route(lambda r, c, q: (r, 1 - c, q)))  1.22 us
  transfers between devices with their start and end apart: 5, of which 2 were waited for; matrix products, arithmetic and copies ran while one was open for 0% of the time, Pallas kernels for 6%

profile of v11, /device:TPU:17, one launch (start us, length us, event | category | flops | bytes accessed | tf_op | source)
XLA Modules:
  0.0 21.2 jit_solution(16705864267554887762)
XLA Ops:
  0.0 2.7 %normalize_and_project.1 = (bf16[272,128]{1,0:T(8,128)(2,1)}, bf16[272,128]{1,0:T(8,128)(2,1)}) custom-call(s32[8]{0:T(128)} %pept_hbm.1, bf16[1024,256]{1,0:T(8,128)(2,1)} %bitcast.10, s32[8,128]{1,0:T(8,128)} %bitcast.13, f32[1,256]{1,0:T(1,128)} %bitcast.14, f32[1,256]{1,0:T(1,128)} %bitcast.15, bf16[32,256]{1,0:T(8,128)(2,1)} %bitcast.11, ...), custom_call_target="tpu_custom_call" | custom-call | tf_op jit(solution)/shard_map/normalize_and_project/pallas_call | solution.py:301
  2.7 0.1 collective-permute-start.2
  2.8 3.4 %collective-permute-start = (bf16[272,128]{1,0:T(8,128)(2,1)}, bf16[272,128]{1,0:T(8,128)(2,1)S(1)}, u32[]{:S(2)}, u32[]{:S(2)}) collective-permute-start(bf16[272,128]{1,0:T(8,128)(2,1)} %get-tuple-element.9), channel_id=1, source_target_pairs={{0,2},{1,3},{2,10},{3,11},{4,0},{5,1},{6,8},{7,9},{8,6},{9,7},{10,... | collective-permute-start | bytes 208904 | tf_op jit(solution)/shard_map/ppermute | solution.py:335
  6.2 0.0 copy-start.1
  6.2 0.9 %copy-done.1 = bf16[272,128]{1,0:T(8,128)(2,1)S(1)} copy-done((bf16[272,128]{1,0:T(8,128)(2,1)S(1)}, bf16[272,128]{1,0:T(8,128)(2,1)}, u32[]{:S(2)}) %copy-start.1) | copy-done | bytes 69656
  7.1 0.0 collective-permute-done.2.far_ref
  7.1 3.3 %collective-permute-start.3 = (bf16[2,272,128]{2,1,0:T(8,128)(2,1)S(1)}, bf16[2,272,128]{2,1,0:T(8,128)(2,1)S(1)}, u32[]{:S(2)}, u32[]{:S(2)}) collective-permute-start(bf16[2,272,128]{2,1,0:T(8,128)(2,1)S(1)} %join.1.refs_2_), channel_id=1, source_target_pairs={{0,4},{1,5},{2,6},{3,7},{4,0},{5,1},{6,2},{7,3},{8,12},{9,13},{10,... | collective-permute-start | bytes 417800 | tf_op jit(solution)/shard_map/ppermute | solution.py:354
  10.4 3.0 %collective-permute-done.refs_1_ = bf16[272,128]{1,0:T(8,128)(2,1)S(1)} collective-permute-done((bf16[272,128]{1,0:T(8,128)(2,1)}, bf16[272,128]{1,0:T(8,128)(2,1)S(1)}, u32[]{:S(2)}, u32[]{:S(2)}) %collective-permute-start) | collective-permute-done | bytes 69664 | tf_op jit(solution)/shard_map/ppermute | solution.py:335
  13.4 0.1 collective-permute-start.1
  13.4 0.0 copy-start
  13.4 0.9 %copy-done = bf16[1024,128]{1,0:T(8,128)(2,1)S(1)} copy-done((bf16[1024,128]{1,0:T(8,128)(2,1)S(1)}, bf16[1024,128]{1,0:T(8,128)(2,1)}, u32[]{:S(2)}) %copy-start) | copy-done | bytes 262168
  14.4 0.0 copy-start.2
  14.4 0.7 %copy-done.2 = f32[128]{0:T(128)S(1)} copy-done((f32[128]{0:T(128)S(1)}, f32[128]{0:T(128)}, u32[]{:S(2)}) %copy-start.2) | copy-done | bytes 536
  15.0 0.3 %keep.1 = (bf16[4096,256]{1,0:T(8,128)(2,1)S(1)}, f32[1,128]{1,0:T(1,128)S(1)}) custom-call(bf16[1024,128]{1,0:T(8,128)(2,1)S(1)} %copy-done, f32[1,128]{1,0:T(1,128)S(1)} %bitcast.9), custom_call_target="tpu_custom_call" | custom-call | bytes 4194304 | tf_op jit(solution)/shard_map/keep/pallas_call | solution.py:356
  15.3 1.2 %collective-permute-done.1.refs_0_ = bf16[272,128]{1,0:T(8,128)(2,1)S(1)} collective-permute-done((bf16[272,128]{1,0:T(8,128)(2,1)S(1)}, bf16[272,128]{1,0:T(8,128)(2,1)S(1)}, u32[]{:S(2)}, u32[]{:S(2)}) %collective-permute-start.1) | collective-permute-done | bytes 69664 | tf_op jit(solution)/shard_map/ppermute | solution.py:355
  16.5 0.0 collective-permute-done.3.refs_3_
  16.5 1.0 %other_pair_sums.1 = bf16[288,128]{1,0:T(8,128)(2,1)S(1)} custom-call(bf16[272,128]{1,0:T(8,128)(2,1)S(1)} %collective-permute-done.1.refs_0_, bf16[272,128]{1,0:T(8,128)(2,1)S(1)} %collective-permute-done.refs_1_, bf16[2,272,128]{2,1,0:T(8,128)(2,1)S(1)} %join.1.refs_2_, bf16[2,272,128]{2,1,0:T(8,128)(2,1)S(1)} %collective-permute-done.3.refs_3_, ...), custom_call_target="tpu_custom_call" | custom-call | flops 268435456 | bytes 1048576 | tf_op jit(solution)/shard_map/other_pair_sums/pallas_call | solution.py:370
  17.5 1.7 %collective-permute-start.4 = (bf16[288,128]{1,0:T(8,128)(2,1)S(1)}, bf16[288,128]{1,0:T(8,128)(2,1)S(1)}, u32[]{:S(2)}, u32[]{:S(2)}) collective-permute-start(bf16[288,128]{1,0:T(8,128)(2,1)S(1)} %other_pair_sums.1), channel_id=1, source_target_pairs={{0,1},{1,0},{2,3},{3,2},{4,5},{5,4},{6,7},{7,6},{8,9},{9,8},{10,11... | collective-permute-start | bytes 221192 | tf_op jit(solution)/shard_map/ppermute | solution.py:388
  19.2 1.0 %own_pair_sums.1.mine_ref = f32[288,128]{1,0:T(8,128)S(1)} custom-call(bf16[272,128]{1,0:T(8,128)(2,1)S(1)} %collective-permute-done.1.refs_0_, bf16[272,128]{1,0:T(8,128)(2,1)S(1)} %collective-permute-done.refs_1_, bf16[2,272,128]{2,1,0:T(8,128)(2,1)S(1)} %join.1.refs_2_, bf16[2,272,128]{2,1,0:T(8,128)(2,1)S(1)} %collective-permute-done.3.refs_3_, ...), custom_call_target="tpu_custom_call" | custom-call | flops 268435456 | bytes 1048576 | tf_op jit(solution)/shard_map/own_pair_sums/pallas_call | solution.py:370
  20.2 0.0 collective-permute-done.4.other_ref
  20.2 1.0 %divide.1 = bf16[16,16,128]{2,1,0:T(8,128)(2,1)} custom-call(f32[288,128]{1,0:T(8,128)S(1)} %own_pair_sums.1.mine_ref, bf16[288,128]{1,0:T(8,128)(2,1)S(1)} %collective-permute-done.4.other_ref), custom_call_target="tpu_custom_call" | custom-call | tf_op jit(solution)/shard_map/divide/pallas_call | solution.py:390
  (2 shorter events, 0.0 us)
Async XLA Ops:
  2.7 4.4 %collective-permute-start.2 = (bf16[272,128]{1,0:T(8,128)(2,1)}, bf16[272,128]{1,0:T(8,128)(2,1)S(1)}, u32[]{:S(2)}, u32[]{:S(2)}) collective-permute-start(bf16[272,128]{1,0:T(8,128)(2,1)} %get-tuple-element.10.right_ref), channel_id=1, source_target_pairs={{0,8},{1,9},{2,10},{3,11},{4,12},{5,13},{6,14},{7,15},{8,0},{9,1},... | collective-permute-start | bytes 208904 | tf_op jit(solution)/shard_map/ppermute | solution.py:334
  2.8 10.6 %collective-permute-start = (bf16[272,128]{1,0:T(8,128)(2,1)}, bf16[272,128]{1,0:T(8,128)(2,1)S(1)}, u32[]{:S(2)}, u32[]{:S(2)}) collective-permute-start(bf16[272,128]{1,0:T(8,128)(2,1)} %get-tuple-element.9), channel_id=1, source_target_pairs={{0,2},{1,3},{2,10},{3,11},{4,0},{5,1},{6,8},{7,9},{8,6},{9,7},{10,... | collective-permute-start | bytes 208904 | tf_op jit(solution)/shard_map/ppermute | solution.py:335
  6.2 0.9 %copy-start.1 = (bf16[272,128]{1,0:T(8,128)(2,1)S(1)}, bf16[272,128]{1,0:T(8,128)(2,1)}, u32[]{:S(2)}) copy-start(bf16[272,128]{1,0:T(8,128)(2,1)} %get-tuple-element.10.right_ref) | copy-start | bytes 208900
  7.1 9.4 %collective-permute-start.3 = (bf16[2,272,128]{2,1,0:T(8,128)(2,1)S(1)}, bf16[2,272,128]{2,1,0:T(8,128)(2,1)S(1)}, u32[]{:S(2)}, u32[]{:S(2)}) collective-permute-start(bf16[2,272,128]{2,1,0:T(8,128)(2,1)S(1)} %join.1.refs_2_), channel_id=1, source_target_pairs={{0,4},{1,5},{2,6},{3,7},{4,0},{5,1},{6,2},{7,3},{8,12},{9,13},{10,... | collective-permute-start | bytes 417800 | tf_op jit(solution)/shard_map/ppermute | solution.py:354
  13.4 3.2 %collective-permute-start.1 = (bf16[272,128]{1,0:T(8,128)(2,1)S(1)}, bf16[272,128]{1,0:T(8,128)(2,1)S(1)}, u32[]{:S(2)}, u32[]{:S(2)}) collective-permute-start(bf16[272,128]{1,0:T(8,128)(2,1)S(1)} %collective-permute-done.refs_1_), channel_id=1, source_target_pairs={{0,2},{1,3},{2,0},{3,1},{4,6},{5,7},{6,4},{7,5},{8,10},{9,11},{10,... | collective-permute-start | bytes 208904 | tf_op jit(solution)/shard_map/ppermute | solution.py:355
  13.4 0.9 %copy-start = (bf16[1024,128]{1,0:T(8,128)(2,1)S(1)}, bf16[1024,128]{1,0:T(8,128)(2,1)}, u32[]{:S(2)}) copy-start(bf16[1024,128]{1,0:T(8,128)(2,1)} %w_ref.1) | copy-start | bytes 786436
  14.4 0.7 %copy-start.2 = (f32[128]{0:T(128)S(1)}, f32[128]{0:T(128)}, u32[]{:S(2)}) copy-start(f32[128]{0:T(128)} %param.21) | copy-start | bytes 1540
  17.5 2.7 %collective-permute-start.4 = (bf16[288,128]{1,0:T(8,128)(2,1)S(1)}, bf16[288,128]{1,0:T(8,128)(2,1)S(1)}, u32[]{:S(2)}, u32[]{:S(2)}) collective-permute-start(bf16[288,128]{1,0:T(8,128)(2,1)S(1)} %other_pair_sums.1), channel_id=1, source_target_pairs={{0,1},{1,0},{2,3},{3,2},{4,5},{5,4},{6,7},{7,6},{8,9},{9,8},{10,11... | collective-permute-start | bytes 221192 | tf_op jit(solution)/shard_map/ppermute | solution.py:388
